TPU v7x, 512 devices: a whole 4x8x8 slice. The times are simulated.
512 devices in a mesh: az: 16 (over y, core), ax: 32 (over x, z).
Axes of the slice: x: 4, y: 8, z: 8, core: 2. Of those that a mesh axis runs over, the one named last changes fastest.
Arguments:
- velocity: float32 [3, 512, 256, 256], P(None, 'az', 'ax'), may hold values from -6 to 6
- bubble_slip: float32 [3, 1048576], P(None, ('az', 'ax')), may hold values from -6 to 6
- bubble_size: float32 [1048576], P(('az', 'ax')), may hold values from 0.3 to 3
- bubble_growth: float32 [1048576], P(('az', 'ax')), may hold values from -6 to 6
- bubble_tile: int32 [1048576], P(('az', 'ax')), may hold values from 0 to 511
- bubble_lane: int32 [1048576], P(('az', 'ax')), may hold values from 0 to 127
- send_counts: int32 [512, 32], P(('az', 'ax')), may hold values from 0 to 128, as said below
- bubble_order: int32 [512, 2048], P(('az', 'ax')), may hold values from 0 to 2047, each once within a row
- radial_inverse: bfloat16 [256, 256, 256], P('az'), may hold values from -0.375 to 0.375
Outputs:
- predicted: float32 [3, 512, 256, 256], P(None, 'az', 'ax')
- pressure_modes: float32 [512, 256, 256], P('az', 'ax')
Inputs may be any that keep to these rules, and one draw needn't show every extreme that they name: `send_counts`: each row sums to 2048. In each azimuthal group one owner index, the same for all holders of the group and drawn from the seed, gets 128 from every holder; each row's other counts are one zero and pairs that sum to 128. `bubble_order`: row h is a permutation of 0 to 2047 listing holder h's bubbles by owner: the first send_counts[h, 0] go to ax index 0, the next send_counts[h, 1] to ax index 1, and so on.
All inputs are finite; a program needn't handle non-finite values.
Results may differ from a plain program's by a relative error of at most 0.009.
Values may be sent and summed in bfloat16 or wider, within the bound.
No kernel may reach another device: no remote copies, remote signals or barrier semaphores. Data moves between devices by JAX's collectives and lax.ppermute only.
A program may use at most 64 MiB of HBM per device.

v0:
```python
import math

import jax
import jax.numpy as jnp
from jax import lax
from jax.sharding import PartitionSpec as P

NTH = 512


DIFFUSE = 0.12


def extended(block, sides, width):
    for axis, dim in sides:
        count = lax.axis_size(axis)
        forward = [(i, i + 1) for i in range(count - 1)]
        forward.append((count - 1, 0))
        backward = [(target, source) for source, target in forward]
        low = lax.ppermute(
            lax.slice_in_dim(block, block.shape[dim] - width, None, axis=dim), axis, forward
        )
        high = lax.ppermute(lax.slice_in_dim(block, 0, width, axis=dim), axis, backward)
        block = jnp.concatenate([low, block, high], axis=dim)
    return block


def radial_parts(values):
    zero_rim = jnp.zeros_like(values[..., :1])
    outer = jnp.concatenate([values[..., 1:], zero_rim], axis=-1)
    inner = jnp.concatenate([zero_rim, values[..., :-1]], axis=-1)
    return (outer, inner)


def spectral_table(row_index, column_index, length):
    frequency = jnp.where(row_index == 1, length // 2, row_index // 2)
    phase = frequency[:, None] * column_index[None, :] % length
    angle = phase.astype(jnp.float32) * (2.0 * math.pi / length)
    use_cosine = (row_index % 2 == 0) | (row_index == 1)
    return jnp.where(use_cosine[:, None], jnp.cos(angle), jnp.sin(angle)) * math.sqrt(2.0 / length)


def solve_modes(coefficients, inverse):
    pair_count = inverse.shape[0]
    grouped = coefficients.reshape(pair_count, -1, coefficients.shape[2])
    solved = jnp.einsum("jsr,jnr->jns", inverse, grouped, preferred_element_type=jnp.float32)
    return solved.reshape(coefficients.shape)


def fill_slots(payload, order_row, count_row, peer_count, capacity):
    bub_local = payload.shape[1]
    block_rows = math.gcd(bub_local, 512)
    slot_ends = jnp.cumsum(count_row)
    slot_starts = slot_ends - count_row
    bubble_axis = jnp.arange(bub_local, dtype=jnp.int32)
    slot_axis = jnp.arange(peer_count * capacity, dtype=jnp.int32)

    def fill_one_block(block_step, running):
        row_start = block_step * block_rows
        place = row_start + jnp.arange(block_rows, dtype=jnp.int32)
        order_block = lax.dynamic_slice_in_dim(order_row, row_start, block_rows)
        listed = (bubble_axis[:, None] == order_block[None, :]).astype(jnp.float32)
        in_order = jnp.dot(
            payload, listed, precision=lax.Precision.HIGHEST, preferred_element_type=jnp.float32
        )
        owner = jnp.sum((place[:, None] >= slot_ends[None, :]).astype(jnp.int32), axis=1)
        owner_hot = (owner[:, None] == jnp.arange(peer_count, dtype=jnp.int32)[None, :]).astype(
            jnp.int32
        )
        start_of = jnp.sum(owner_hot * slot_starts[None, :], axis=1)
        slot_of = owner * capacity + place - start_of
        placing = (slot_of[:, None] == slot_axis[None, :]).astype(jnp.float32)
        return running + jnp.dot(
            in_order, placing, precision=lax.Precision.HIGHEST, preferred_element_type=jnp.float32
        )

    initial = jnp.zeros((payload.shape[0], peer_count * capacity), jnp.float32)
    return lax.fori_loop(0, bub_local // block_rows, fill_one_block, initial)


def deposit(values, cells, tile_total):
    row_total = values.shape[1]
    block_rows = math.gcd(row_total, 1024)
    tile_ids = cells // 128
    lane_ids = cells % 128
    tile_axis = jnp.arange(tile_total, dtype=jnp.int32)
    lane_axis = jnp.arange(128, dtype=jnp.int32)

    def deposit_one_block(block_step, running):
        row_start = block_step * block_rows
        tile_block = lax.dynamic_slice_in_dim(tile_ids, row_start, block_rows)
        lane_block = lax.dynamic_slice_in_dim(lane_ids, row_start, block_rows)
        value_block = lax.dynamic_slice_in_dim(values, row_start, block_rows, axis=1)
        tile_onehot = (tile_axis[:, None] == tile_block[None, :]).astype(jnp.float32)
        lane_onehot = (lane_block[:, None] == lane_axis[None, :]).astype(jnp.float32)
        parts = [
            jnp.dot(
                tile_onehot,
                lane_onehot * value_block[k][:, None],
                precision=lax.Precision.HIGHEST,
                preferred_element_type=jnp.float32,
            )
            for k in range(4)
        ]
        return running + jnp.stack(parts, axis=0)

    return lax.fori_loop(
        0, row_total // block_rows, deposit_one_block, jnp.zeros((4, tile_total, 128), jnp.float32)
    )


def on_device(
    velocity,
    bubble_slip,
    bubble_size,
    bubble_growth,
    bubble_tile,
    bubble_lane,
    send_counts,
    bubble_order,
    radial_inverse,
):
    th_local = velocity.shape[1]
    ax_local = velocity.shape[2]
    radial_cells = velocity.shape[3]
    peer_count = lax.axis_size("ax")
    bub_local = bubble_order.shape[1]
    capacity = 2 * bub_local // peer_count
    strength = jnp.sqrt(
        1.0
        + bubble_slip[0] * bubble_slip[0]
        + bubble_slip[1] * bubble_slip[1]
        + bubble_slip[2] * bubble_slip[2]
    )
    bubble_loads = jnp.concatenate(
        [bubble_size * strength * bubble_slip, (bubble_size * bubble_growth)[None]], axis=0
    )
    local_cells = (bubble_tile * 128 + bubble_lane).astype(jnp.float32)
    payload = jnp.concatenate([bubble_loads, local_cells[None]], axis=0)
    slotted = fill_slots(payload, bubble_order[0], send_counts[0], peer_count, capacity)
    outgoing = slotted[:4].reshape(4, peer_count, capacity)
    outgoing_cells = slotted[4:].astype(jnp.int32).reshape(1, peer_count, capacity)
    arrived, arrived_cells = (
        lax.all_to_all(
            outgoing.astype(jnp.bfloat16), "ax", split_axis=1, concat_axis=1, tiled=True
        ).astype(outgoing.dtype),
        lax.all_to_all(outgoing_cells, "ax", split_axis=1, concat_axis=1, tiled=True),
    )
    tile_total = th_local * ax_local * radial_cells // 128
    density = deposit(arrived.reshape(4, -1), arrived_cells.reshape(-1), tile_total)
    density = density.reshape(4, th_local, ax_local, radial_cells)
    padded = extended(velocity.astype(jnp.bfloat16), (("az", 1), ("ax", 2)), 1).astype(
        velocity.dtype
    )
    outer, inner = radial_parts(velocity)
    radius = jnp.arange(radial_cells, dtype=jnp.float32)
    axial_term = padded[:, 1:-1, 2:] + padded[:, 1:-1, :-2] - 2.0 * velocity
    azimuth_term = padded[:, 2:, 1:-1] + padded[:, :-2, 1:-1] - 2.0 * velocity
    radial_term = ((radius + 1.0) * (outer - velocity) - radius * (velocity - inner)) / (
        radius + 0.5
    )
    predicted = velocity + DIFFUSE * (axial_term + azimuth_term + radial_term) + density[:3]
    divergence = 0.5 * (padded[0, 1:-1, 2:] - padded[0, 1:-1, :-2])
    divergence = divergence + 0.5 * (padded[1, 2:, 1:-1] - padded[1, :-2, 1:-1])
    divergence = divergence + ((radius + 1.0) * outer[2] - radius * inner[2]) / (2.0 * radius + 1.0)
    source = divergence + density[3]
    column_index = lax.axis_index("az") * th_local + jnp.arange(th_local, dtype=jnp.int32)
    flat_source = source.reshape(th_local, -1)
    row_index = jnp.arange(lax.axis_size("az") * th_local, dtype=jnp.int32)
    table_part = spectral_table(row_index, column_index, NTH)
    product = jnp.dot(
        table_part, flat_source, precision=lax.Precision.HIGHEST, preferred_element_type=jnp.float32
    )
    own_coefficients = lax.psum_scatter(
        product.reshape(lax.axis_size("az") * th_local, ax_local, radial_cells),
        "az",
        scatter_dimension=0,
        tiled=True,
    )
    pressure_modes = solve_modes(own_coefficients.astype(jnp.bfloat16), radial_inverse)
    return (predicted, pressure_modes)


def solution(mesh):
    placed = (
        P(None, "az", "ax", None),
        P(None, ("az", "ax")),
        P(("az", "ax")),
        P(("az", "ax")),
        P(("az", "ax")),
        P(("az", "ax")),
        P(("az", "ax"), None),
        P(("az", "ax"), None),
        P("az", None, None),
    )
    return jax.shard_map(
        on_device,
        mesh=mesh,
        in_specs=placed,
        out_specs=(P(None, "az", "ax", None), P("az", "ax", None)),
        check_vma=False,
    )
```

profile of v0, /device:TPU:1, one launch (start us, length us, event | category | flops | bytes accessed | tf_op | source)
XLA Modules:
  0.0 201.9 jit_solution(15253968628579308439)
XLA Ops:
  12.0 20.4 %while.28 = (s32[]{:T(128)}, f32[5,4096]{1,0:T(8,128)S(1)}, s32[2048]{0:T(1024)}, f32[5,2048]{1,0:T(8,128)S(1)}, s32[32]{0:T(128)S(1)}, /*index=5*/s32[32]{0:T(128)S(1)}, s32[]{:T(128)}, s32[]{:T(128)}, s32[]{:T(128)}, s32[]{:T(128)}) while((s32[]{:T(128)}, f32[5,4096]{1,0:T(8,128)S(1)}, s32[2048]{0:T(1024)}, ...), condition=%wide.region_4.5_spmd.clone, body=%wide.region_1.4_spmd.clone.sunk | while | flops 192030208 | bytes 250289 | solution.py:78
  14.4 2.8 %fusion.120 = f32[5,4096]{1,0:T(8,128)S(1)} fusion(f32[512,5]{0,1:T(8,128)S(1)} %fusion.119, s32[512]{0:T(512)S(1)} %add_subtract_fusion.2, f32[5,4096]{1,0:T(8,128)S(1)} %get-tuple-element.441, pred[]{:T(512)S(6)} %compare.17), kind=kOutput, calls=%fused_computation.6.clone.1 | convolution fusion | flops 127967232 | bytes 176129 | tf_op jit(solution)/shard_map/while/body/eval_jaxpr/dot_general | solution.py:73
  19.4 2.8 %fusion.120 = f32[5,4096]{1,0:T(8,128)S(1)} fusion(f32[512,5]{0,1:T(8,128)S(1)} %fusion.119, s32[512]{0:T(512)S(1)} %add_subtract_fusion.2, f32[5,4096]{1,0:T(8,128)S(1)} %get-tuple-element.441, pred[]{:T(512)S(6)} %compare.17), kind=kOutput, calls=%fused_computation.6.clone.1 | convolution fusion | flops 127967232 | bytes 176129 | tf_op jit(solution)/shard_map/while/body/eval_jaxpr/dot_general | solution.py:73
  24.5 2.8 %fusion.120 = f32[5,4096]{1,0:T(8,128)S(1)} fusion(f32[512,5]{0,1:T(8,128)S(1)} %fusion.119, s32[512]{0:T(512)S(1)} %add_subtract_fusion.2, f32[5,4096]{1,0:T(8,128)S(1)} %get-tuple-element.441, pred[]{:T(512)S(6)} %compare.17), kind=kOutput, calls=%fused_computation.6.clone.1 | convolution fusion | flops 127967232 | bytes 176129 | tf_op jit(solution)/shard_map/while/body/eval_jaxpr/dot_general | solution.py:73
  29.6 2.8 %fusion.120 = f32[5,4096]{1,0:T(8,128)S(1)} fusion(f32[512,5]{0,1:T(8,128)S(1)} %fusion.119, s32[512]{0:T(512)S(1)} %add_subtract_fusion.2, f32[5,4096]{1,0:T(8,128)S(1)} %get-tuple-element.441, pred[]{:T(512)S(6)} %compare.17), kind=kOutput, calls=%fused_computation.6.clone.1 | convolution fusion | flops 127967232 | bytes 176129 | tf_op jit(solution)/shard_map/while/body/eval_jaxpr/dot_general | solution.py:73
  33.0 13.7 %all-to-all-start = ((s32[1,32,128]{2,0,1:T(1,128)}), s32[1,32,128]{2,0,1:T(1,128)S(1)}, u32[]{:S(2)}, u32[]{:S(2)}) async-start(s32[1,32,128]{2,0,1:T(1,128)} %convert_bitcast_fusion), calls=%async_computation | async-start | bytes 32768 | tf_op jit(solution)/shard_map/all_to_all | solution.py:147
  47.4 2.1 %collective-permute-start = (bf16[3,1,8,256]{3,2,1,0:T(8,128)(2,1)}, bf16[3,1,8,256]{3,2,1,0:T(8,128)(2,1)}, u32[]{:S(2)}, u32[]{:S(2)}) collective-permute-start(bf16[3,1,8,256]{3,2,1,0:T(8,128)(2,1)} %get-tuple-element.344), channel_id=1, source_target_pairs={{0,32},{32,64},{64,96},{96,128},{128,160},{160,192},{192,224},{224... | collective-permute-start | bytes 36872 | tf_op jit(solution)/shard_map/ppermute | solution.py:20
  52.4 1.4 fusion.97
  55.0 1.9 pad_slice_fusion
  61.3 1.7 copy.26
  63.1 1.7 copy.24
  64.8 1.6 pad_maximum_fusion.2
  66.4 3.4 %collective-permute-start.2 = (bf16[3,34,1,256]{3,2,1,0:T(2,128)(2,1)}, bf16[3,34,1,256]{3,2,1,0:T(2,128)(2,1)}, u32[]{:S(2)}, u32[]{:S(2)}) collective-permute-start(bf16[3,34,1,256]{3,2,1,0:T(2,128)(2,1)} %get-tuple-element.342), channel_id=1, source_target_pairs={{0,1},{1,2},{2,3},{3,4},{4,5},{5,6},{6,7},{7,8},{8,9},{9,10},{10,1... | collective-permute-start | bytes 156680 | tf_op jit(solution)/shard_map/ppermute | solution.py:20
  69.8 5.3 %collective-permute-start.3 = (bf16[3,34,1,256]{3,2,1,0:T(2,128)(2,1)}, bf16[3,34,1,256]{3,2,1,0:T(2,128)(2,1)}, u32[]{:S(2)}, u32[]{:S(2)}) collective-permute-start(bf16[3,34,1,256]{3,2,1,0:T(2,128)(2,1)} %get-tuple-element.343), channel_id=1, source_target_pairs={{1,0},{2,1},{3,2},{4,3},{5,4},{6,5},{7,6},{8,7},{9,8},{10,9},{11,1... | collective-permute-start | bytes 156680 | tf_op jit(solution)/shard_map/ppermute | solution.py:23
  75.2 7.4 %all-to-all-start.1 = ((bf16[4,32,128]{2,0,1:T(4,128)(2,1)}), bf16[4,32,128]{2,0,1:T(4,128)(2,1)}, u32[]{:S(2)}, u32[]{:S(2)}) async-start(bf16[4,32,128]{2,0,1:T(4,128)(2,1)} %fusion.73), calls=%async_computation.1 | async-start | bytes 65536 | tf_op jit(solution)/shard_map/all_to_all | solution.py:144
  84.2 7.2 %all-to-all-done.1 = bf16[4,32,128]{2,0,1:T(4,128)(2,1)} async-done(((bf16[4,32,128]{2,0,1:T(4,128)(2,1)}), bf16[4,32,128]{2,0,1:T(4,128)(2,1)}, u32[]{:S(2)}, u32[]{:S(2)}) %all-to-all-start.1) | async-done | bytes 32800 | tf_op jit(solution)/shard_map/all_to_all | solution.py:144
  91.3 1.4 bitcast_convert_fusion
  92.7 27.5 %while.29 = (s32[]{:T(128)}, f32[4,512,128]{2,1,0:T(8,128)S(1)}, s32[4096]{0:T(1024)}, s32[4096]{0:T(1024)S(1)}, f32[4,4096]{1,0:T(4,128)}, /*index=5*/s32[]{:T(...) while((s32[]{:T(128)}, f32[4,512,128]{2,1,0:T(8,128)S(1)}, s32[4096]{0:T(1024)}, ...), condition=%wide.region_6.7_spmd.clone, body=%wide.region_5.6_spmd.clone.sunk | while | flops 3225681920 | bytes 4292849 | solution.py:107
  121.0 1.7 squeeze.41
  122.8 1.5 maximum_convert_fusion
  126.1 5.6 %fusion.56 = f32[512,8,256]{2,0,1:T(8,128)} fusion(f32[4,8,8,256]{3,2,1,0:T(8,128)S(1)} %bitcast.80, s32[32]{0:T(128)S(1)} %copy-done.16, s32[512]{0:T(512)S(1)} %copy-done.13, pred[512]{0:T(512)(128)(4,1)S(1)} %copy-done.15), kind=kOutput, calls=%fused_computation.64 | convolution fusion | flops 402915328 | bytes 4459136 | tf_op jit(solution)/shard_map/dot_general | solution.py:171
  132.7 2.4 %slice.121 = f32[3,32,8,256]{3,2,1,0:T(8,128)} reshape(f32[3,512,128]{2,1,0:T(8,128)} %slice.120) | data formatting | bytes 1572864 | tf_op jit(solution)/shard_map/slice | solution.py:162
  135.0 5.1 %fusion.54 = f32[3,32,8,256]{3,2,1,0:T(8,128)} fusion(f32[3,32,8,256]{3,2,1,0:T(8,128)} %slice.121, f32[3,32,8,256]{3,2,1,0:T(8,128)S(1)} %copy-done.3, f32[3,34,10,256]{3,2,1,0:T(8,128)} %copy-done.1, f32[3,32,8,255]{3,2,1,0:T(8,128)} %get-tuple-element.341, f32[3,32,8,255]{3,2,1,0:T(8,128)} %get-tuple-element.340, f32[256]{0:T(256)S(1)} %copy-done.14, ...), kind=kLoop, calls=%fused_computation.59 | loop fusion | flops 3145728 | bytes 7073792 | tf_op jit(solution)/shard_map/add | solution.py:162
  140.1 52.5 %reduce-scatter.2.cloned.1.call-done = f32[32,8,256]{2,0,1:T(8,128)} async-done(((f32[512,8,256]{2,0,1:T(8,128)}), f32[32,8,256]{2,0,1:T(8,128)}) %reduce-scatter.2.cloned.1.call-update) | async-done | bytes 262160 | tf_op jit(solution)/shard_map/reduce_scatter | solution.py:174
  (133 shorter events, 58.6 us)
Async XLA Ops:
  7.2 186.5 %copy-start = (bf16[16,256,256]{2,1,0:T(8,128)(2,1)S(1)}, bf16[16,256,256]{2,1,0:T(8,128)(2,1)}, u32[]{:S(2)}) copy-start(bf16[16,256,256]{2,1,0:T(8,128)(2,1)} %param.21) | copy-start | bytes 6291460
  12.0 34.7 %copy-start.2 = (f32[3,32,8,256]{3,2,1,0:T(8,128)S(1)}, f32[3,32,8,256]{3,2,1,0:T(8,128)}, u32[]{:S(2)}) copy-start(f32[3,32,8,256]{3,2,1,0:T(8,128)} %param.13) | copy-start | bytes 2359300
  33.0 42.2 %all-to-all-start = ((s32[1,32,128]{2,0,1:T(1,128)}), s32[1,32,128]{2,0,1:T(1,128)S(1)}, u32[]{:S(2)}, u32[]{:S(2)}) async-start(s32[1,32,128]{2,0,1:T(1,128)} %convert_bitcast_fusion), calls=%async_computation | async-start | bytes 32768 | tf_op jit(solution)/shard_map/all_to_all | solution.py:147
  47.4 17.4 %collective-permute-start = (bf16[3,1,8,256]{3,2,1,0:T(8,128)(2,1)}, bf16[3,1,8,256]{3,2,1,0:T(8,128)(2,1)}, u32[]{:S(2)}, u32[]{:S(2)}) collective-permute-start(bf16[3,1,8,256]{3,2,1,0:T(8,128)(2,1)} %get-tuple-element.344), channel_id=1, source_target_pairs={{0,32},{32,64},{64,96},{96,128},{128,160},{160,192},{192,224},{224... | collective-permute-start | bytes 36872 | tf_op jit(solution)/shard_map/ppermute | solution.py:20
  49.5 15.3 %collective-permute-start.1 = (bf16[3,1,8,256]{3,2,1,0:T(8,128)(2,1)}, bf16[3,1,8,256]{3,2,1,0:T(8,128)(2,1)}, u32[]{:S(2)}, u32[]{:S(2)}) collective-permute-start(bf16[3,1,8,256]{3,2,1,0:T(8,128)(2,1)} %get-tuple-element.345), channel_id=1, source_target_pairs={{32,0},{64,32},{96,64},{128,96},{160,128},{192,160},{224,192},{256... | collective-permute-start | bytes 36872 | tf_op jit(solution)/shard_map/ppermute | solution.py:23
  51.2 5.7 %copy-start.11 = (f32[256]{0:T(256)}, f32[256]{0:T(256)S(1)}, u32[]{:S(2)}) copy-start(f32[256]{0:T(256)S(1)} %get-tuple-element.353) | copy-start | bytes 3076
  66.4 56.3 %collective-permute-start.2 = (bf16[3,34,1,256]{3,2,1,0:T(2,128)(2,1)}, bf16[3,34,1,256]{3,2,1,0:T(2,128)(2,1)}, u32[]{:S(2)}, u32[]{:S(2)}) collective-permute-start(bf16[3,34,1,256]{3,2,1,0:T(2,128)(2,1)} %get-tuple-element.342), channel_id=1, source_target_pairs={{0,1},{1,2},{2,3},{3,4},{4,5},{5,6},{6,7},{7,8},{8,9},{9,10},{10,1... | collective-permute-start | bytes 156680 | tf_op jit(solution)/shard_map/ppermute | solution.py:20
  69.8 52.9 %collective-permute-start.3 = (bf16[3,34,1,256]{3,2,1,0:T(2,128)(2,1)}, bf16[3,34,1,256]{3,2,1,0:T(2,128)(2,1)}, u32[]{:S(2)}, u32[]{:S(2)}) collective-permute-start(bf16[3,34,1,256]{3,2,1,0:T(2,128)(2,1)} %get-tuple-element.343), channel_id=1, source_target_pairs={{1,0},{2,1},{3,2},{4,3},{5,4},{6,5},{7,6},{8,7},{9,8},{10,9},{11,1... | collective-permute-start | bytes 156680 | tf_op jit(solution)/shard_map/ppermute | solution.py:23
  75.2 7.6 %copy-start.7 = (s32[1,32,128]{2,0,1:T(1,128)}, s32[1,32,128]{2,0,1:T(1,128)S(1)}, u32[]{:S(2)}) copy-start(s32[1,32,128]{2,0,1:T(1,128)S(1)} %all-to-all-done) | copy-start | bytes 49156
  75.2 16.1 %all-to-all-start.1 = ((bf16[4,32,128]{2,0,1:T(4,128)(2,1)}), bf16[4,32,128]{2,0,1:T(4,128)(2,1)}, u32[]{:S(2)}, u32[]{:S(2)}) async-start(bf16[4,32,128]{2,0,1:T(4,128)(2,1)} %fusion.73), calls=%async_computation.1 | async-start | bytes 65536 | tf_op jit(solution)/shard_map/all_to_all | solution.py:144
  82.6 110.0 %reduce-scatter.2.cloned.1.call-start = ((), (), s32[]{:S(2)}) async-start(), calls=%async_computation.3 | async-start | bytes 4456448 | tf_op jit(solution)/shard_map/reduce_scatter | solution.py:174
  122.7 2.9 %copy-start.4 = (f32[4,8,8,256]{3,1,2,0:T(8,128)S(1)}, f32[4,8,8,256]{3,1,2,0:T(8,128)}, u32[]{:S(2)}) copy-start(f32[4,8,8,256]{3,1,2,0:T(8,128)} %copy.26) | copy-start | bytes 786436
  122.7 2.9 %copy-start.5 = (f32[4,8,8,256]{3,1,2,0:T(8,128)S(1)}, f32[4,8,8,256]{3,1,2,0:T(8,128)}, u32[]{:S(2)}) copy-start(f32[4,8,8,256]{3,1,2,0:T(8,128)} %copy.24) | copy-start | bytes 786436
  122.7 2.9 %copy-start.6 = (f32[32,2048]{1,0:T(8,128)S(1)}, f32[32,2048]{1,0:T(8,128)}, u32[]{:S(2)}) copy-start(f32[32,2048]{1,0:T(8,128)} %squeeze.41) | copy-start | bytes 786436
  122.7 2.9 %copy-start.8 = (f32[1,2,8,128]{3,1,2,0:T(2,128)S(1)}, f32[1,2,8,128]{3,1,2,0:T(2,128)}, u32[]{:S(2)}) copy-start(f32[1,2,8,128]{3,1,2,0:T(2,128)} %copy.27) | copy-start | bytes 24580
  122.7 2.9 %copy-start.9 = (f32[1,2,8,128]{3,1,2,0:T(2,128)S(1)}, f32[1,2,8,128]{3,1,2,0:T(2,128)}, u32[]{:S(2)}) copy-start(f32[1,2,8,128]{3,1,2,0:T(2,128)} %copy.23) | copy-start | bytes 24580
  122.7 2.9 %copy-start.10 = (f32[1,2,8,128]{3,1,2,0:T(2,128)S(1)}, f32[1,2,8,128]{3,1,2,0:T(2,128)}, u32[]{:S(2)}) copy-start(f32[1,2,8,128]{3,1,2,0:T(2,128)} %copy.25) | copy-start | bytes 24580
  124.2 1.2 copy-start.1
  125.4 0.7 copy-start.13
  125.4 0.7 copy-start.15
  125.4 0.7 copy-start.16
  131.7 3.3 %copy-start.12 = (f32[256]{0:T(256)S(1)}, f32[256]{0:T(256)}, u32[]{:S(2)}) copy-start(f32[256]{0:T(256)} %copy-done.11) | copy-start | bytes 3076
  131.7 3.3 %copy-start.14 = (f32[256]{0:T(256)S(1)}, f32[256]{0:T(256)}, u32[]{:S(2)}) copy-start(f32[256]{0:T(256)} %get-tuple-element.352) | copy-start | bytes 3076
  132.7 2.4 %copy-start.3 = (f32[3,32,8,256]{3,2,1,0:T(8,128)S(1)}, f32[3,32,8,256]{3,2,1,0:T(8,128)}, u32[]{:S(2)}) copy-start(f32[3,32,8,256]{3,2,1,0:T(8,128)} %param.13) | copy-start | bytes 2359300
Sparse Core Ops, SparseCore 0:
  131.8 60.7 reduce-scatter.1
where the time goes:
time: 205 us; the launch traced here: 202 us
  waiting for transfers between devices  59.7 us (29%)
  matrix products  43.1 us (21%)
  starting transfers between devices  32.2 us (16%)
  local copies, waits for them, and re-layouts  31.6 us (15%)
  other arithmetic  20.7 us (10%)
  between operations  14.3 us (7%)
    reduce_scatter x1, waiting for transfers between devices, on_device(): lax.psum_scatter(product.reshape(lax.axis_size('az') * th_local, ax_local...  52.5 us
    dot_general x16, matrix products, deposit_one_block(): jnp.dot(tile_onehot, lane_onehot * value_block[k][:, None], precision=lax...  19.8 us
    all_to_all x1, starting transfers between devices, on_device(): lax.all_to_all(outgoing_cells, 'ax', split_axis=1, concat_axis=1, tiled=T...  13.7 us
    dot_general x4, matrix products, fill_one_block(): jnp.dot(in_order, placing, precision=lax.Precision.HIGHEST, preferred_ele...  11.1 us
    unnamed x43, local copies, waits for them, and re-layouts  10.8 us
    all_to_all x1, starting transfers between devices, on_device(): lax.all_to_all(outgoing.astype(jnp.bfloat16), 'ax', split_axis=1, concat_...  7.39 us
    all_to_all x1, waiting for transfers between devices, on_device(): lax.all_to_all(outgoing.astype(jnp.bfloat16), 'ax', split_axis=1, concat_...  7.16 us
    dot_general x1, matrix products, on_device(): jnp.dot(table_part, flat_source, precision=lax.Precision.HIGHEST, preferr...  5.59 us
  transfers between devices with their start and end apart: 7, of which 2 were waited for; matrix products, arithmetic and copies ran while one was open for 29% of the time, Pallas kernels for 0%

commit v1 on v0

v1 whole, which is shorter than its diff:
```python
import functools
import math

import jax
import jax.numpy as jnp
import numpy as np
from jax import lax
from jax.experimental import pallas as pl
from jax.experimental.pallas import tpu as pltpu
from jax.sharding import PartitionSpec as P

DIFFUSE = 0.12
LANES = 128
ROWS = 8

VMEM = pl.BlockSpec(memory_space=pltpu.VMEM)
ANY = pl.BlockSpec(memory_space=pl.ANY)


def call(body, name, out_shape, operands, scratch=(), specs=None, flops=0, limit=24):
    moved = sum(x.size * x.dtype.itemsize for x in operands)
    return pl.pallas_call(
        body,
        name=name,
        out_shape=out_shape,
        in_specs=[VMEM] * len(operands) if specs is None else specs,
        out_specs=jax.tree.map(lambda _: VMEM, out_shape),
        scratch_shapes=list(scratch),
        compiler_params=pltpu.CompilerParams(vmem_limit_bytes=limit * 1024 * 1024),
        cost_estimate=pl.CostEstimate(flops=flops, bytes_accessed=moved, transcendentals=0),
    )(*operands)


def take_rows(table, row, lane, shape):
    found = jnp.zeros(shape, table.dtype)
    for r in range(table.shape[0]):
        line = jnp.broadcast_to(table[r : r + 1, :], shape)
        picked = jnp.take_along_axis(line, lane, axis=1, mode="promise_in_bounds")
        found = jnp.where(row == r, picked, found)
    return found


def pack_body(
    slip, size, growth, tile, lane, counts, order, out, listed, slips, payload, staged
):
    lines = listed.shape[0]
    peers = counts.shape[1]
    for j in range(lines):
        span = slice(j * LANES, (j + 1) * LANES)
        listed[j : j + 1, :] = order[0:1, span]
        for k in range(3):
            slips[k, j : j + 1, :] = slip[k : k + 1, span]
    s0, s1, s2 = slips[0], slips[1], slips[2]
    scale = size[...] * jnp.sqrt(1.0 + s0 * s0 + s1 * s1 + s2 * s2)
    payload[0] = scale * s0
    payload[1] = scale * s1
    payload[2] = scale * s2
    payload[3] = size[...] * growth[...]
    payload[4] = (tile[...] * LANES + lane[...]).astype(jnp.float32)
    count_rows = jnp.broadcast_to(counts[...], (peers, peers))
    below = lax.broadcasted_iota(jnp.int32, (peers, peers), 1) < lax.broadcasted_iota(
        jnp.int32, (peers, peers), 0
    )
    own = lax.broadcasted_iota(jnp.int32, (peers, peers), 1) == lax.broadcasted_iota(
        jnp.int32, (peers, peers), 0
    )
    start = jnp.sum(jnp.where(below, count_rows, 0), axis=1, keepdims=True)
    count = jnp.sum(jnp.where(own, count_rows, 0), axis=1, keepdims=True)
    shape = (peers, LANES)
    slot = lax.broadcasted_iota(jnp.int32, shape, 1)
    used = slot < count
    place = jnp.minimum(start + slot, lines * LANES - 1)
    bubble = take_rows(listed, place >> 7, place & 127, shape)
    row, column = bubble >> 7, bubble & 127
    for k in range(4):
        value = take_rows(payload.at[k], row, column, shape)
        staged[:, k, :] = jnp.where(used, value, 0.0)
    cell = take_rows(payload.at[4], row, column, shape).astype(jnp.int32)
    cell = jnp.where(used, cell, 0)
    staged[:, 4, :] = (cell >> 8).astype(jnp.float32)
    staged[:, 5, :] = (cell & 255).astype(jnp.float32)
    staged[:, 6, :] = jnp.zeros(shape, jnp.float32)
    staged[:, 7, :] = jnp.zeros(shape, jnp.float32)
    out[...] = staged[...].astype(jnp.bfloat16)


def edges_body(velocity, _, first_theta, last_theta, first_x, last_x):
    th = velocity.shape[1]
    first_theta[...] = velocity[:, 0].astype(jnp.bfloat16)
    last_theta[...] = velocity[:, th - 1].astype(jnp.bfloat16)
    first_x[...] = velocity[:, :, 0, :].astype(jnp.bfloat16)
    last_x[...] = velocity[:, :, ROWS - 1, :].astype(jnp.bfloat16)


def radial_neighbours(v):
    column = lax.broadcasted_iota(jnp.int32, v.shape, 1)
    last = v.shape[1] - 1
    outer = jnp.where(column == last, 0.0, pltpu.roll(v, last, 1))
    inner = jnp.where(column == 0, 0.0, pltpu.roll(v, 1, 1))
    return outer, inner


def axial_neighbours(v, before, after):
    row = lax.broadcasted_iota(jnp.int32, v.shape, 0)
    ahead = jnp.where(row == ROWS - 1, after, pltpu.roll(v, ROWS - 1, 0))
    behind = jnp.where(row == 0, before, pltpu.roll(v, 1, 0))
    return ahead, behind


def divergence_body(velocity, theta_before, theta_after, x_before, x_after, out, low, high):
    th, width = velocity.shape[1], velocity.shape[3]
    low[...] = x_before[0].astype(jnp.float32)
    high[...] = x_after[0].astype(jnp.float32)
    radius = lax.broadcasted_iota(jnp.int32, (ROWS, width), 1).astype(jnp.float32)
    outward = (radius + 1.0) / (2.0 * radius + 1.0)
    inward = radius / (2.0 * radius + 1.0)
    for t in range(th):
        ahead, behind = axial_neighbours(velocity[0, t], low[t : t + 1, :], high[t : t + 1, :])
        above = velocity[1, t + 1] if t < th - 1 else theta_after[1].astype(jnp.float32)
        under = velocity[1, t - 1] if t > 0 else theta_before[1].astype(jnp.float32)
        outer, inner = radial_neighbours(velocity[2, t])
        out[t] = 0.5 * ((ahead - behind) + (above - under)) + (outward * outer - inward * inner)


def cell_hot(index_line, cells):
    row = lax.broadcasted_iota(jnp.int32, (cells, LANES), 0).astype(jnp.bfloat16)
    return row == jnp.broadcast_to(index_line, (cells, LANES))


def hot_parts(arrived, first, count, across, along):
    cells = across.shape[0]
    zero = jnp.zeros((cells, LANES), jnp.bfloat16)
    for h in range(arrived.shape[0]):
        span = slice(h * LANES, (h + 1) * LANES)
        block = arrived[h]
        across[:, span] = jnp.where(
            cell_hot(block[4:5, :], cells), jnp.ones_like(zero), zero
        )
        here = cell_hot(block[5:6, :], cells)
        for k in range(count):
            value = jnp.broadcast_to(block[first + k : first + k + 1, :], zero.shape)
            along[k, :, span] = jnp.where(here, value, zero)


def deposit(across, along):
    return lax.dot_general(
        across, along, (((1,), (1,)), ((), ())), preferred_element_type=jnp.float32
    )


def source_body(arrived, divergence, out, across, along, whole):
    th = divergence.shape[0]
    hot_parts(arrived, 3, 1, across, along)
    density = deposit(across[...], along[0])
    total = density + divergence[...].reshape(density.shape)
    halves = whole.shape[0]
    for half in range(halves):
        whole[half] = total[:, half * LANES : (half + 1) * LANES]
        for x in range(ROWS):
            layer = whole[half, pl.ds(x, th, stride=ROWS), :]
            out[x * halves + half] = layer.astype(jnp.bfloat16)


def predictor_body(
    arrived, velocity, theta_before, theta_after, x_before, x_after, out, across, along, low, high,
    density,
):
    th, width = velocity.shape[1], velocity.shape[3]
    hot_parts(arrived, 0, 3, across, along)
    radius = lax.broadcasted_iota(jnp.int32, (ROWS, width), 1).astype(jnp.float32)
    outward = (radius + 1.0) / (radius + 0.5)
    inward = radius / (radius + 0.5)
    low[...] = x_before[...].astype(jnp.float32)
    high[...] = x_after[...].astype(jnp.float32)
    for c in range(3):
        density[...] = deposit(across[...], along[c])
        for t in range(th):
            v = velocity[c, t]
            ahead, behind = axial_neighbours(v, low[c, t : t + 1, :], high[c, t : t + 1, :])
            above = velocity[c, t + 1] if t < th - 1 else theta_after[c].astype(jnp.float32)
            under = velocity[c, t - 1] if t > 0 else theta_before[c].astype(jnp.float32)
            outer, inner = radial_neighbours(v)
            around = (ahead + behind) + (above + under) + (outward * outer + inward * inner)
            out[c, t] = (
                (1.0 - 6.0 * DIFFUSE) * v
                + DIFFUSE * around
                + density[t * ROWS : (t + 1) * ROWS, :]
            )


def transform_body(table, source, out):
    product = jnp.dot(table[...], source[...], preferred_element_type=jnp.float32)
    out[...] = product.astype(jnp.bfloat16)


def solve_body(spread, inverse, out, whole):
    rows = spread.shape[1]
    halves = whole.shape[0]
    for x in range(ROWS):
        for half in range(halves):
            layer = spread[x * halves + half].astype(jnp.float32)
            whole[half, pl.ds(x, rows, stride=ROWS), :] = layer
    group = 2 * ROWS
    for j in range(inverse.shape[0]):
        span = slice(j * group, (j + 1) * group)
        pair = jnp.concatenate([whole[half, span, :] for half in range(halves)], axis=1)
        out[span, :] = lax.dot_general(
            pair.astype(jnp.bfloat16),
            inverse[j],
            (((1,), (1,)), ((), ())),
            preferred_element_type=jnp.float32,
        )


def spectral_table(length):
    row = np.arange(length)[:, None]
    frequency = np.where(row == 1, length // 2, row // 2)
    angle = (frequency * np.arange(length)[None, :] % length) * (2.0 * math.pi / length)
    cosine = (row % 2 == 0) | (row == 1)
    table = np.where(cosine, np.cos(angle), np.sin(angle)) * math.sqrt(2.0 / length)
    return table.astype(jnp.bfloat16)


def ring(axis, step):
    count = lax.axis_size(axis)
    return [(i, (i + step) % count) for i in range(count)]


def on_device(
    velocity,
    bubble_slip,
    bubble_size,
    bubble_growth,
    bubble_tile,
    bubble_lane,
    send_counts,
    bubble_order,
    radial_inverse,
):
    _, th, ax, width = velocity.shape
    peers = send_counts.shape[1]
    bubbles = bubble_order.shape[1]
    lines = bubbles // LANES
    groups = lax.axis_size("az")
    f32, bf16 = jnp.float32, jnp.bfloat16
    struct = jax.ShapeDtypeStruct
    square = (lines, LANES)

    packed = call(
        pack_body,
        "pack_bubbles",
        struct((peers, ROWS, LANES), bf16),
        (
            bubble_slip,
            bubble_size.reshape(square),
            bubble_growth.reshape(square),
            bubble_tile.reshape(square),
            bubble_lane.reshape(square),
            send_counts,
            bubble_order,
        ),
        scratch=(
            pltpu.VMEM(square, jnp.int32),
            pltpu.VMEM((3,) + square, f32),
            pltpu.VMEM((5,) + square, f32),
            pltpu.VMEM((peers, ROWS, LANES), f32),
        ),
    )
    arrived = lax.all_to_all(packed, "ax", split_axis=0, concat_axis=0, tiled=True)

    first_theta, last_theta, first_x, last_x = call(
        edges_body,
        "edge_layers",
        (
            struct((3, ax, width), bf16),
            struct((3, ax, width), bf16),
            struct((3, th, width), bf16),
            struct((3, th, width), bf16),
        ),
        (velocity, packed),
        specs=[VMEM, ANY],
    )
    theta_before = lax.ppermute(last_theta, "az", ring("az", 1))
    theta_after = lax.ppermute(first_theta, "az", ring("az", -1))
    x_before = lax.ppermute(last_x, "ax", ring("ax", 1))
    x_after = lax.ppermute(first_x, "ax", ring("ax", -1))
    divergence = call(
        divergence_body,
        "divergence",
        struct((th, ax, width), f32),
        (velocity, theta_before, theta_after, x_before, x_after),
        scratch=(pltpu.VMEM((th, width), f32), pltpu.VMEM((th, width), f32)),
    )

    slots = peers * LANES
    cells = th * ax
    source = call(
        source_body,
        "source",
        struct((groups, th, LANES), bf16),
        (arrived, divergence),
        scratch=(
            pltpu.VMEM((cells, slots), bf16),
            pltpu.VMEM((1, width, slots), bf16),
            pltpu.VMEM((width // LANES, cells, LANES), f32),
        ),
        flops=2 * cells * slots * width,
    )
    gathered = lax.all_to_all(source, "az", split_axis=0, concat_axis=0, tiled=True)

    predicted = call(
        predictor_body,
        "predictor",
        struct(velocity.shape, f32),
        (arrived, velocity, theta_before, theta_after, x_before, x_after),
        scratch=(
            pltpu.VMEM((cells, slots), bf16),
            pltpu.VMEM((3, width, slots), bf16),
            pltpu.VMEM((3, th, width), f32),
            pltpu.VMEM((3, th, width), f32),
            pltpu.VMEM((cells, width), f32),
        ),
        flops=2 * 3 * cells * slots * width,
        limit=32,
    )

    length = groups * th
    table = jnp.asarray(spectral_table(length))
    coefficients = call(
        transform_body,
        "transform",
        struct((length, LANES), bf16),
        (table, gathered.reshape(length, LANES)),
        flops=2 * length * length * LANES,
    )
    spread = lax.all_to_all(
        coefficients.reshape(groups, th, LANES), "az", split_axis=0, concat_axis=0, tiled=True
    )
    modes = call(
        solve_body,
        "solve",
        struct((th * ax, width), f32),
        (spread, radial_inverse),
        scratch=(pltpu.VMEM((width // LANES, th * ax, LANES), f32),),
        flops=2 * th * ax * width * width,
    )
    return predicted, modes.reshape(th, ax, width)


def solution(mesh):
    placed = (
        P(None, "az", "ax", None),
        P(None, ("az", "ax")),
        P(("az", "ax")),
        P(("az", "ax")),
        P(("az", "ax")),
        P(("az", "ax")),
        P(("az", "ax"), None),
        P(("az", "ax"), None),
        P("az", None, None),
    )
    return jax.shard_map(
        on_device,
        mesh=mesh,
        in_specs=placed,
        out_specs=(P(None, "az", "ax", None), P("az", "ax", None)),
        check_vma=False,
    )
```

time: 205 us -> 71 us (0.35); the launches traced: 202 us -> 70.3 us
  waiting for transfers between devices: 59.7 us -> 7.8 us
  matrix products: 43.1 us -> 0 us
  local copies, waits for them, and re-layouts: 31.6 us -> 7.16 us
  other arithmetic: 20.7 us -> 0 us
  blocking collectives: 0 us -> 16.4 us
  between operations: 14.3 us -> 0.74 us
  Pallas kernels: 0 us -> 9.77 us
  starting transfers between devices: 32.2 us -> 28.4 us
    reduce_scatter x1 -> x0, waiting for transfers between devices: 52.5 us -> none  [on_device(): lax.psum_scatter(product.reshape(lax.axis_size('az') * th_local, ax_local...]
    dot_general x26 -> x0, matrix products: 43.1 us -> none  [the longest x16 19.8 us: deposit_one_block(): jnp.dot(tile_onehot, lane_onehot * value_block[k][:, None], precision=lax...]
    all_to_all x0 -> x1, blocking collectives: none -> 16.4 us  [on_device(): lax.all_to_all(source, 'az', split_axis=0, concat_axis=0, tiled=True)]
    slice x10 -> x0, local copies, waits for them, and re-layouts: 11.7 us -> none  [the longest x4 3.79 us: deposit_one_block(): value_block[k][:, None]]
    pallas_call x0 -> x7, Pallas kernels: none -> 9.77 us  [call(): pl.pallas_call(body, name=name, out_shape=out_shape, in_specs=[VMEM] * le...]
    add x14 -> x0, other arithmetic: 7.34 us -> none  [the longest x1 5.06 us: on_device(): velocity + DIFFUSE * (axial_term + azimuth_term + radial_term) + density[:3]]
    dynamic_slice x12 -> x0, local copies, waits for them, and re-layouts: 5.93 us -> none  [the longest x4 3.14 us: fill_one_block(): order_block = lax.dynamic_slice_in_dim(order_row, row_start, block_rows)]
    all_to_all x2, starting transfers between devices: 21.1 us -> 17.1 us  [the longest x1 13.7 us: on_device(): lax.all_to_all(packed, 'ax', split_axis=0, concat_axis=0, tiled=True)]
  transfers between devices with their start and end apart: 7 -> 6, of which waited for: 2 -> 3; matrix products, arithmetic and copies ran while one was open for 29% -> 0% of each run, Pallas kernels for 0% -> 6%
where the time goes in v1:
time: 71 us; the launch traced here: 70.3 us
  starting transfers between devices  28.4 us (40%)
  blocking collectives  16.4 us (23%)
  Pallas kernels  9.77 us (14%)
  waiting for transfers between devices  7.8 us (11%)
  local copies, waits for them, and re-layouts  7.16 us (10%)
  between operations  0.74 us (1%)
    all_to_all x1, blocking collectives, on_device(): lax.all_to_all(source, 'az', split_axis=0, concat_axis=0, tiled=True)  16.4 us
    all_to_all x1, starting transfers between devices, on_device(): lax.all_to_all(packed, 'ax', split_axis=0, concat_axis=0, tiled=True)  13.7 us
    pallas_call x7, Pallas kernels, call(): pl.pallas_call(body, name=name, out_shape=out_shape, in_specs=[VMEM] * le...  9.77 us
    unnamed x24, local copies, waits for them, and re-layouts  7.16 us
    ppermute x1, starting transfers between devices, on_device(): x_after = lax.ppermute(first_x, 'ax', ring('ax', -1))  5.46 us
    all_to_all x1, waiting for transfers between devices, on_device(): lax.all_to_all(coefficients.reshape(groups, th, LANES), 'az', split_axis=...  4.68 us
    all_to_all x1, starting transfers between devices, on_device(): lax.all_to_all(coefficients.reshape(groups, th, LANES), 'az', split_axis=...  3.41 us
    ppermute x1, starting transfers between devices, on_device(): x_before = lax.ppermute(last_x, 'ax', ring('ax', 1))  3.14 us
  transfers between devices with their start and end apart: 6, of which 3 were waited for; matrix products, arithmetic and copies ran while one was open for 0% of the time, Pallas kernels for 6%

profile of v1, /device:TPU:1, one launch (start us, length us, event | category | flops | bytes accessed | tf_op | source)
XLA Modules:
  0.0 70.3 jit_solution(18400808277399331688)
XLA Ops:
  0.6 0.7 %copy-done.5 = f32[3,2048]{1,0:T(4,128)S(1)} copy-done((f32[3,2048]{1,0:T(4,128)S(1)}, f32[3,2048]{1,0:T(4,128)}, u32[]{:S(2)}) %copy-start.5) | copy-done | bytes 24600
  1.4 0.7 copy-done.6
  2.1 0.7 copy-done.7
  2.8 0.7 copy-done.8
  3.5 0.7 copy-done.9
  4.2 0.7 copy-done.10
  4.9 0.7 copy-done.11
  5.5 1.9 %pack_bubbles.1._ = bf16[32,8,128]{2,1,0:T(8,128)(2,1)} custom-call(f32[3,2048]{1,0:T(4,128)S(1)} %copy-done.5, f32[16,128]{1,0:T(8,128)S(1)} %bitcast.8, f32[16,128]{1,0:T(8,128)S(1)} %bitcast.9, s32[16,128]{1,0:T(8,128)S(1)} %bitcast.10, s32[16,128]{1,0:T(8,128)S(1)} %bitcast.11, s32[1,32]{1,0:T(1,128)S(1)} %copy-done.11, s32[1,2048]{1,0:T(1,128)S(1)} %copy-done.10), custom_call_target="tpu_custom_call" | custom-call | bytes 65664 | tf_op jit(solution)/shard_map/pack_bubbles/pallas_call | solution.py:22
  7.5 13.7 %all-to-all-start = ((bf16[32,8,128]{2,1,0:T(8,128)(2,1)}), bf16[32,8,128]{2,1,0:T(8,128)(2,1)S(1)}, u32[]{:S(2)}, u32[]{:S(2)}) async-start(bf16[32,8,128]{2,1,0:T(8,128)(2,1)} %pack_bubbles.1._), calls=%async_computation | async-start | bytes 131072 | tf_op jit(solution)/shard_map/all_to_all | solution.py:269
  21.2 1.1 %copy-done = f32[3,32,8,256]{3,2,1,0:T(8,128)S(1)} copy-done((f32[3,32,8,256]{3,2,1,0:T(8,128)S(1)}, f32[3,32,8,256]{3,2,1,0:T(8,128)}, u32[]{:S(2)}) %copy-start) | copy-done | bytes 786456
  22.5 3.1 %collective-permute-start.2 = (bf16[3,32,256]{2,1,0:T(8,128)(2,1)S(1)}, bf16[3,32,256]{2,1,0:T(8,128)(2,1)S(1)}, u32[]{:S(2)}, u32[]{:S(2)}) collective-permute-start(bf16[3,32,256]{2,1,0:T(8,128)(2,1)S(1)} %get-tuple-element.8), channel_id=1, source_target_pairs={{0,1},{1,2},{2,3},{3,4},{4,5},{5,6},{6,7},{7,8},{8,9},{9,10},{10,1... | collective-permute-start | bytes 147464 | tf_op jit(solution)/shard_map/ppermute | solution.py:285
  25.7 5.5 %collective-permute-start.3 = (bf16[3,32,256]{2,1,0:T(8,128)(2,1)S(1)}, bf16[3,32,256]{2,1,0:T(8,128)(2,1)S(1)}, u32[]{:S(2)}, u32[]{:S(2)}) collective-permute-start(bf16[3,32,256]{2,1,0:T(8,128)(2,1)S(1)} %get-tuple-element.9), channel_id=1, source_target_pairs={{0,31},{1,0},{2,1},{3,2},{4,3},{5,4},{6,5},{7,6},{8,7},{9,8},{10,9... | collective-permute-start | bytes 147464 | tf_op jit(solution)/shard_map/ppermute | solution.py:286
  31.2 2.7 %collective-permute-start = (bf16[3,8,256]{2,1,0:T(8,128)(2,1)S(1)}, bf16[3,8,256]{2,1,0:T(8,128)(2,1)S(1)}, u32[]{:S(2)}, u32[]{:S(2)}) collective-permute-start(bf16[3,8,256]{2,1,0:T(8,128)(2,1)S(1)} %get-tuple-element.6), channel_id=1, source_target_pairs={{0,32},{32,64},{64,96},{96,128},{128,160},{160,192},{192,224},{224... | collective-permute-start | bytes 36872 | tf_op jit(solution)/shard_map/ppermute | solution.py:283
  33.9 0.8 %collective-permute-done.theta_before = bf16[3,8,256]{2,1,0:T(8,128)(2,1)S(1)} collective-permute-done((bf16[3,8,256]{2,1,0:T(8,128)(2,1)S(1)}, bf16[3,8,256]{2,1,0:T(8,128)(2,1)S(1)}, u32[]{:S(2)}, u32[]{:S(2)}) %collective-permute-start) | collective-permute-done | bytes 12320 | tf_op jit(solution)/shard_map/ppermute | solution.py:283
  34.7 2.3 %collective-permute-done.1.theta_after = bf16[3,8,256]{2,1,0:T(8,128)(2,1)S(1)} collective-permute-done((bf16[3,8,256]{2,1,0:T(8,128)(2,1)S(1)}, bf16[3,8,256]{2,1,0:T(8,128)(2,1)S(1)}, u32[]{:S(2)}, u32[]{:S(2)}) %collective-permute-start.1) | collective-permute-done | bytes 12320 | tf_op jit(solution)/shard_map/ppermute | solution.py:284
  37.0 1.1 %copy-done.1 = f32[3,32,8,256]{3,2,1,0:T(8,128)S(1)} copy-done((f32[3,32,8,256]{3,2,1,0:T(8,128)S(1)}, f32[3,32,8,256]{3,2,1,0:T(8,128)}, u32[]{:S(2)}) %copy-start.1) | copy-done | bytes 786456
  38.1 0.2 divergence.1
  38.4 1.3 %source.1 = bf16[16,32,128]{2,1,0:T(8,128)(2,1)S(1)} custom-call(bf16[32,8,128]{2,1,0:T(8,128)(2,1)S(1)} %all-to-all-done.arrived, f32[32,8,256]{2,1,0:T(8,128)S(1)} %divergence.1), custom_call_target="tpu_custom_call" | custom-call | flops 536870912 | bytes 327680 | tf_op jit(solution)/shard_map/source/pallas_call | solution.py:22
  39.7 16.4 %all_to_all.15 = bf16[16,32,128]{2,1,0:T(8,128)(2,1)S(1)} all-to-all(bf16[16,32,128]{2,1,0:T(8,128)(2,1)S(1)} %source.1), channel_id=1, replica_groups=mesh['az'=16,'ax'=32] {'az'}, dimensions={0} | all-to-all | bytes 262144 | tf_op jit(solution)/shard_map/all_to_all | solution.py:309
  56.1 1.0 %transform.1 = bf16[512,128]{1,0:T(8,128)(2,1)} custom-call(bf16[512,512]{1,0:T(8,128)(2,1)S(1)} %copy-done.4, bf16[512,128]{1,0:T(8,128)(2,1)S(1)} %bitcast.7), custom_call_target="tpu_custom_call" | custom-call | flops 67108864 | bytes 655360 | tf_op jit(solution)/shard_map/transform/pallas_call | solution.py:22
  57.0 3.4 %all-to-all-start.2 = ((bf16[16,32,128]{2,1,0:T(8,128)(2,1)}), bf16[16,32,128]{2,1,0:T(8,128)(2,1)S(1)}, u32[]{:S(2)}, u32[]{:S(2)}) async-start(bf16[16,32,128]{2,1,0:T(8,128)(2,1)} %bitcast.5), calls=%async_computation.2 | async-start | bytes 262144 | tf_op jit(solution)/shard_map/all_to_all | solution.py:336
  60.5 3.8 %predictor.1 = f32[3,32,8,256]{3,2,1,0:T(8,128)} custom-call(bf16[32,8,128]{2,1,0:T(8,128)(2,1)S(1)} %all-to-all-done.arrived, f32[3,32,8,256]{3,2,1,0:T(8,128)S(1)} %copy-done.2, bf16[3,8,256]{2,1,0:T(8,128)(2,1)S(1)} %collective-permute-done.theta_before, bf16[3,8,256]{2,1,0:T(8,128)(2,1)S(1)} %collective-permute-done.1.theta_after, ...), custom_call_target="tpu_custom_call" | custom-call | flops 1610612736 | bytes 974848 | tf_op jit(solution)/shard_map/predictor/pallas_call | solution.py:22
  64.3 4.7 %all-to-all-done.2.spread = bf16[16,32,128]{2,1,0:T(8,128)(2,1)S(1)} async-done(((bf16[16,32,128]{2,1,0:T(8,128)(2,1)}), bf16[16,32,128]{2,1,0:T(8,128)(2,1)S(1)}, u32[]{:S(2)}, u32[]{:S(2)}) %all-to-all-start.2) | async-done | bytes 131104 | tf_op jit(solution)/shard_map/all_to_all | solution.py:336
  68.9 1.4 %solve.1 = f32[256,256]{1,0:T(8,128)} custom-call(bf16[16,32,128]{2,1,0:T(8,128)(2,1)S(1)} %all-to-all-done.2.spread, bf16[16,256,256]{2,1,0:T(8,128)(2,1)S(1)} %copy-done.3), custom_call_target="tpu_custom_call" | custom-call | flops 33554432 | bytes 2228224 | tf_op jit(solution)/shard_map/solve/pallas_call | solution.py:22
  (20 shorter events, 0.2 us)
Async XLA Ops:
  0.6 0.8 %copy-start.5 = (f32[3,2048]{1,0:T(4,128)S(1)}, f32[3,2048]{1,0:T(4,128)}, u32[]{:S(2)}) copy-start(f32[3,2048]{1,0:T(4,128)} %slip.1) | copy-start | bytes 73732
  1.4 0.7 copy-start.6
  2.1 0.7 copy-start.7
  2.8 0.7 copy-start.8
  3.5 0.7 copy-start.9
  4.2 0.7 copy-start.10
  4.9 0.7 copy-start.11
  7.5 30.9 %all-to-all-start = ((bf16[32,8,128]{2,1,0:T(8,128)(2,1)}), bf16[32,8,128]{2,1,0:T(8,128)(2,1)S(1)}, u32[]{:S(2)}, u32[]{:S(2)}) async-start(bf16[32,8,128]{2,1,0:T(8,128)(2,1)} %pack_bubbles.1._), calls=%async_computation | async-start | bytes 131072 | tf_op jit(solution)/shard_map/all_to_all | solution.py:269
  21.2 1.1 %copy-start = (f32[3,32,8,256]{3,2,1,0:T(8,128)S(1)}, f32[3,32,8,256]{3,2,1,0:T(8,128)}, u32[]{:S(2)}) copy-start(f32[3,32,8,256]{3,2,1,0:T(8,128)} %velocity.5) | copy-start | bytes 2359300
  22.3 33.8 %copy-start.4 = (bf16[512,512]{1,0:T(8,128)(2,1)S(1)}, bf16[512,512]{1,0:T(8,128)(2,1)}, u32[]{:S(2)}) copy-start(bf16[512,512]{1,0:T(8,128)(2,1)} %constant.2.clone.table) | copy-start | bytes 1572868
  22.5 14.5 %collective-permute-start.2 = (bf16[3,32,256]{2,1,0:T(8,128)(2,1)S(1)}, bf16[3,32,256]{2,1,0:T(8,128)(2,1)S(1)}, u32[]{:S(2)}, u32[]{:S(2)}) collective-permute-start(bf16[3,32,256]{2,1,0:T(8,128)(2,1)S(1)} %get-tuple-element.8), channel_id=1, source_target_pairs={{0,1},{1,2},{2,3},{3,4},{4,5},{5,6},{6,7},{7,8},{8,9},{9,10},{10,1... | collective-permute-start | bytes 147464 | tf_op jit(solution)/shard_map/ppermute | solution.py:285
  25.7 11.3 %collective-permute-start.3 = (bf16[3,32,256]{2,1,0:T(8,128)(2,1)S(1)}, bf16[3,32,256]{2,1,0:T(8,128)(2,1)S(1)}, u32[]{:S(2)}, u32[]{:S(2)}) collective-permute-start(bf16[3,32,256]{2,1,0:T(8,128)(2,1)S(1)} %get-tuple-element.9), channel_id=1, source_target_pairs={{0,31},{1,0},{2,1},{3,2},{4,3},{5,4},{6,5},{7,6},{8,7},{9,8},{10,9... | collective-permute-start | bytes 147464 | tf_op jit(solution)/shard_map/ppermute | solution.py:286
  31.2 3.5 %collective-permute-start = (bf16[3,8,256]{2,1,0:T(8,128)(2,1)S(1)}, bf16[3,8,256]{2,1,0:T(8,128)(2,1)S(1)}, u32[]{:S(2)}, u32[]{:S(2)}) collective-permute-start(bf16[3,8,256]{2,1,0:T(8,128)(2,1)S(1)} %get-tuple-element.6), channel_id=1, source_target_pairs={{0,32},{32,64},{64,96},{96,128},{128,160},{160,192},{192,224},{224... | collective-permute-start | bytes 36872 | tf_op jit(solution)/shard_map/ppermute | solution.py:283
  33.9 3.1 %collective-permute-start.1 = (bf16[3,8,256]{2,1,0:T(8,128)(2,1)S(1)}, bf16[3,8,256]{2,1,0:T(8,128)(2,1)S(1)}, u32[]{:S(2)}, u32[]{:S(2)}) collective-permute-start(bf16[3,8,256]{2,1,0:T(8,128)(2,1)S(1)} %get-tuple-element.7), channel_id=1, source_target_pairs={{0,480},{32,0},{64,32},{96,64},{128,96},{160,128},{192,160},{224,1... | collective-permute-start | bytes 36872 | tf_op jit(solution)/shard_map/ppermute | solution.py:284
  37.0 1.1 %copy-start.1 = (f32[3,32,8,256]{3,2,1,0:T(8,128)S(1)}, f32[3,32,8,256]{3,2,1,0:T(8,128)}, u32[]{:S(2)}) copy-start(f32[3,32,8,256]{3,2,1,0:T(8,128)} %velocity.5) | copy-start | bytes 2359300
  38.1 22.3 %copy-start.2 = (f32[3,32,8,256]{3,2,1,0:T(8,128)S(1)}, f32[3,32,8,256]{3,2,1,0:T(8,128)}, u32[]{:S(2)}) copy-start(f32[3,32,8,256]{3,2,1,0:T(8,128)} %velocity.5) | copy-start | bytes 2359300
  57.0 11.9 %all-to-all-start.2 = ((bf16[16,32,128]{2,1,0:T(8,128)(2,1)}), bf16[16,32,128]{2,1,0:T(8,128)(2,1)S(1)}, u32[]{:S(2)}, u32[]{:S(2)}) async-start(bf16[16,32,128]{2,1,0:T(8,128)(2,1)} %bitcast.5), calls=%async_computation.2 | async-start | bytes 262144 | tf_op jit(solution)/shard_map/all_to_all | solution.py:336
  60.5 8.5 %copy-start.3 = (bf16[16,256,256]{2,1,0:T(8,128)(2,1)S(1)}, bf16[16,256,256]{2,1,0:T(8,128)(2,1)}, u32[]{:S(2)}) copy-start(bf16[16,256,256]{2,1,0:T(8,128)(2,1)} %inverse.1) | copy-start | bytes 6291460

commit v2 on v1

--- a/solution.py
+++ b/solution.py
@@ -40,9 +40,18 @@
     return found
 
 
-def pack_body(
-    slip, size, growth, tile, lane, counts, order, out, listed, slips, payload, staged
-):
+def pack_body(*refs):
+    hbm, (out, first_x, last_x), held = refs[:8], refs[8:11], refs[11:19]
+    listed, slips, payload, staged, sems = refs[19:]
+    copies = [
+        pltpu.make_async_copy(source, target, sems.at[i])
+        for i, (source, target) in enumerate(zip(hbm, held))
+    ]
+    for copy in copies:
+        copy.start()
+    for copy in copies[:7]:
+        copy.wait()
+    slip, size, growth, tile, lane, counts, order, block = held
     lines = listed.shape[0]
     peers = counts.shape[1]
     for j in range(lines):
@@ -82,14 +91,9 @@
     staged[:, 6, :] = jnp.zeros(shape, jnp.float32)
     staged[:, 7, :] = jnp.zeros(shape, jnp.float32)
     out[...] = staged[...].astype(jnp.bfloat16)
-
-
-def edges_body(velocity, _, first_theta, last_theta, first_x, last_x):
-    th = velocity.shape[1]
-    first_theta[...] = velocity[:, 0].astype(jnp.bfloat16)
-    last_theta[...] = velocity[:, th - 1].astype(jnp.bfloat16)
-    first_x[...] = velocity[:, :, 0, :].astype(jnp.bfloat16)
-    last_x[...] = velocity[:, :, ROWS - 1, :].astype(jnp.bfloat16)
+    copies[7].wait()
+    first_x[...] = block[:, :, 0, :].astype(jnp.bfloat16)
+    last_x[...] = block[:, :, ROWS - 1, :].astype(jnp.bfloat16)
 
 
 def radial_neighbours(v):
@@ -107,19 +111,48 @@
     return ahead, behind
 
 
-def divergence_body(velocity, theta_before, theta_after, x_before, x_after, out, low, high):
-    th, width = velocity.shape[1], velocity.shape[3]
-    low[...] = x_before[0].astype(jnp.float32)
-    high[...] = x_after[0].astype(jnp.float32)
+def interior_body(
+    velocity, _, first_theta, last_theta, divergence, held, sems
+):
+    th, width = held.shape[1], held.shape[3]
+    parts = sems.shape[1]
+    step = th // parts
+    copies = []
+    for c in range(3):
+        for p in range(parts):
+            span = (c, pl.ds(p * step, step))
+            copies.append(pltpu.make_async_copy(velocity.at[span], held.at[span], sems.at[c, p]))
+    for copy in copies:
+        copy.start()
+    for copy in copies:
+        copy.wait()
+    first_theta[...] = held[:, 0].astype(jnp.bfloat16)
+    last_theta[...] = held[:, th - 1].astype(jnp.bfloat16)
     radius = lax.broadcasted_iota(jnp.int32, (ROWS, width), 1).astype(jnp.float32)
     outward = (radius + 1.0) / (2.0 * radius + 1.0)
     inward = radius / (2.0 * radius + 1.0)
     for t in range(th):
-        ahead, behind = axial_neighbours(velocity[0, t], low[t : t + 1, :], high[t : t + 1, :])
-        above = velocity[1, t + 1] if t < th - 1 else theta_after[1].astype(jnp.float32)
-        under = velocity[1, t - 1] if t > 0 else theta_before[1].astype(jnp.float32)
-        outer, inner = radial_neighbours(velocity[2, t])
-        out[t] = 0.5 * ((ahead - behind) + (above - under)) + (outward * outer - inward * inner)
+        ahead, behind = axial_neighbours(held[0, t], 0.0, 0.0)
+        around = ahead - behind
+        if t < th - 1:
+            around = around + held[1, t + 1]
+        if t > 0:
+            around = around - held[1, t - 1]
+        outer, inner = radial_neighbours(held[2, t])
+        divergence[t] = 0.5 * around + (outward * outer - inward * inner)
+
+
+def after(arrays, event):
+    count = len(arrays)
+    return pl.pallas_call(
+        lambda *refs: None,
+        name="after",
+        out_shape=tuple(jax.ShapeDtypeStruct(x.shape, x.dtype) for x in arrays),
+        in_specs=[ANY] * (count + 1),
+        out_specs=(ANY,) * count,
+        input_output_aliases={i: i for i in range(count)},
+        compiler_params=pltpu.CompilerParams(vmem_limit_bytes=60 * 1024 * 1024),
+    )(*arrays, event)
 
 
 def cell_hot(index_line, cells):
@@ -133,9 +166,7 @@
     for h in range(arrived.shape[0]):
         span = slice(h * LANES, (h + 1) * LANES)
         block = arrived[h]
-        across[:, span] = jnp.where(
-            cell_hot(block[4:5, :], cells), jnp.ones_like(zero), zero
-        )
+        across[:, span] = jnp.where(cell_hot(block[4:5, :], cells), jnp.ones_like(zero), zero)
         here = cell_hot(block[5:6, :], cells)
         for k in range(count):
             value = jnp.broadcast_to(block[first + k : first + k + 1, :], zero.shape)
@@ -148,17 +179,29 @@
     )
 
 
-def source_body(arrived, divergence, out, across, along, whole):
+def source_body(
+    arrived, divergence, x_before, x_after, first_theta, last_theta, out, across, along, whole
+):
     th = divergence.shape[0]
     hot_parts(arrived, 3, 1, across, along)
     density = deposit(across[...], along[0])
     total = density + divergence[...].reshape(density.shape)
     halves = whole.shape[0]
+    blank = jnp.zeros((out.shape[1] - th - 2, LANES), jnp.float32)
+    first = first_theta[1].astype(jnp.float32)
+    last = last_theta[1].astype(jnp.float32)
     for half in range(halves):
-        whole[half] = total[:, half * LANES : (half + 1) * LANES]
+        span = slice(half * LANES, (half + 1) * LANES)
+        whole[half] = total[:, span]
         for x in range(ROWS):
             layer = whole[half, pl.ds(x, th, stride=ROWS), :]
-            out[x * halves + half] = layer.astype(jnp.bfloat16)
+            if x == 0:
+                layer = layer - 0.5 * x_before[0, :, span].astype(jnp.float32)
+            if x == ROWS - 1:
+                layer = layer + 0.5 * x_after[0, :, span].astype(jnp.float32)
+            edges = [first[x : x + 1, span], last[x : x + 1, span], blank]
+            column = jnp.concatenate([layer] + edges, axis=0)
+            out[x * halves + half] = column.astype(jnp.bfloat16)
 
 
 def predictor_body(
@@ -188,7 +231,7 @@
             )
 
 
-def transform_body(table, source, out):
+def transform_body(table, source, before, after, out):
     product = jnp.dot(table[...], source[...], preferred_element_type=jnp.float32)
     out[...] = product.astype(jnp.bfloat16)
 
@@ -212,13 +255,19 @@
         )
 
 
-def spectral_table(length):
+def spectral_table(length, blocks, extra):
     row = np.arange(length)[:, None]
     frequency = np.where(row == 1, length // 2, row // 2)
     angle = (frequency * np.arange(length)[None, :] % length) * (2.0 * math.pi / length)
     cosine = (row % 2 == 0) | (row == 1)
     table = np.where(cosine, np.cos(angle), np.sin(angle)) * math.sqrt(2.0 / length)
-    return table.astype(jnp.bfloat16)
+    step = length // blocks
+    wide = np.zeros((length, blocks, step + extra))
+    wide[:, :, :step] = table.reshape(length, blocks, step)
+    starts = np.arange(blocks) * step
+    wide[:, :, step] = 0.5 * table[:, (starts - 1) % length]
+    wide[:, :, step + 1] = -0.5 * table[:, (starts + step) % length]
+    return wide.reshape(length, -1).astype(jnp.bfloat16)
 
 
 def ring(axis, step):
@@ -246,59 +295,62 @@
     struct = jax.ShapeDtypeStruct
     square = (lines, LANES)
 
-    packed = call(
+    bubbles_in = (
+        bubble_slip,
+        bubble_size.reshape(square),
+        bubble_growth.reshape(square),
+        bubble_tile.reshape(square),
+        bubble_lane.reshape(square),
+        send_counts,
+        bubble_order,
+    )
+    bubbles_in = bubbles_in + (velocity,)
+    packed, first_x, last_x = call(
         pack_body,
         "pack_bubbles",
-        struct((peers, ROWS, LANES), bf16),
         (
-            bubble_slip,
-            bubble_size.reshape(square),
-            bubble_growth.reshape(square),
-            bubble_tile.reshape(square),
-            bubble_lane.reshape(square),
-            send_counts,
-            bubble_order,
+            struct((peers, ROWS, LANES), bf16),
+            struct((3, th, width), bf16),
+            struct((3, th, width), bf16),
         ),
-        scratch=(
+        bubbles_in,
+        specs=[ANY] * 8,
+        limit=60,
+        scratch=tuple(pltpu.VMEM(x.shape, x.dtype) for x in bubbles_in)
+        + (
             pltpu.VMEM(square, jnp.int32),
             pltpu.VMEM((3,) + square, f32),
             pltpu.VMEM((5,) + square, f32),
             pltpu.VMEM((peers, ROWS, LANES), f32),
+            pltpu.SemaphoreType.DMA((8,)),
         ),
     )
     arrived = lax.all_to_all(packed, "ax", split_axis=0, concat_axis=0, tiled=True)
 
-    first_theta, last_theta, first_x, last_x = call(
-        edges_body,
-        "edge_layers",
+    first_x, last_x = after((first_x, last_x), packed)
+    x_before = lax.ppermute(last_x, "ax", ring("ax", 1))
+    x_after = lax.ppermute(first_x, "ax", ring("ax", -1))
+    first_theta, last_theta, divergence = call(
+        interior_body,
+        "interior",
         (
             struct((3, ax, width), bf16),
             struct((3, ax, width), bf16),
-            struct((3, th, width), bf16),
-            struct((3, th, width), bf16),
+            struct((th, ax, width), f32),
         ),
         (velocity, packed),
-        specs=[VMEM, ANY],
-    )
-    theta_before = lax.ppermute(last_theta, "az", ring("az", 1))
-    theta_after = lax.ppermute(first_theta, "az", ring("az", -1))
-    x_before = lax.ppermute(last_x, "ax", ring("ax", 1))
-    x_after = lax.ppermute(first_x, "ax", ring("ax", -1))
-    divergence = call(
-        divergence_body,
-        "divergence",
-        struct((th, ax, width), f32),
-        (velocity, theta_before, theta_after, x_before, x_after),
-        scratch=(pltpu.VMEM((th, width), f32), pltpu.VMEM((th, width), f32)),
+        specs=[ANY, ANY],
+        scratch=(pltpu.VMEM(velocity.shape, f32), pltpu.SemaphoreType.DMA((3, 2))),
     )
 
     slots = peers * LANES
     cells = th * ax
+    extra = 8
     source = call(
         source_body,
         "source",
-        struct((groups, th, LANES), bf16),
-        (arrived, divergence),
+        struct((groups, th + extra, LANES), bf16),
+        (arrived, divergence, x_before, x_after, first_theta, last_theta),
         scratch=(
             pltpu.VMEM((cells, slots), bf16),
             pltpu.VMEM((1, width, slots), bf16),
@@ -307,6 +359,10 @@
         flops=2 * cells * slots * width,
     )
     gathered = lax.all_to_all(source, "az", split_axis=0, concat_axis=0, tiled=True)
+
+    first_layer, last_layer = after((first_theta, last_theta), source)
+    theta_before = lax.ppermute(last_layer, "az", ring("az", 1))
+    theta_after = lax.ppermute(first_layer, "az", ring("az", -1))
 
     predicted = call(
         predictor_body,
@@ -325,13 +381,14 @@
     )
 
     length = groups * th
-    table = jnp.asarray(spectral_table(length))
+    table = jnp.asarray(spectral_table(length, groups, extra))
     coefficients = call(
         transform_body,
         "transform",
         struct((length, LANES), bf16),
-        (table, gathered.reshape(length, LANES)),
-        flops=2 * length * length * LANES,
+        (table, gathered.reshape(-1, LANES), theta_before, theta_after),
+        specs=[VMEM, VMEM, ANY, ANY],
+        flops=2 * length * (length + groups * extra) * LANES,
     )
     spread = lax.all_to_all(
         coefficients.reshape(groups, th, LANES), "az", split_axis=0, concat_axis=0, tiled=True

time: 71 us -> 64.7 us (0.911)
  blocking collectives: 16.4 us -> 0 us
  starting transfers between devices: 28.4 us -> 36 us
  Pallas kernels: 9.77 us -> 12.5 us
  local copies, waits for them, and re-layouts: 7.16 us -> 5.15 us
  waiting for transfers between devices: 7.8 us -> 9.59 us
    all_to_all x1 -> x0, blocking collectives: 16.4 us -> none  [on_device(): lax.all_to_all(source, 'az', split_axis=0, concat_axis=0, tiled=True)]
    all_to_all x0 -> x1, starting transfers between devices: none -> 8.64 us  [on_device(): lax.all_to_all(source, 'az', split_axis=0, concat_axis=0, tiled=True)]
    all_to_all x0 -> x1, waiting for transfers between devices: none -> 3.5 us  [on_device(): lax.all_to_all(source, 'az', split_axis=0, concat_axis=0, tiled=True)]
    all_to_all x1, waiting for transfers between devices: 4.68 us -> 1.28 us  [on_device(): lax.all_to_all(coefficients.reshape(groups, th, LANES), 'az', split_axis=...]
    pallas_call x7 -> x6, Pallas kernels: 9.77 us -> 12.5 us  [call(): pl.pallas_call(body, name=name, out_shape=out_shape, in_specs=[VMEM] * le...]
    unnamed x24 -> x30, local copies, waits for them, and re-layouts: 7.16 us -> 5.15 us
    ppermute x2, waiting for transfers between devices: 3.12 us -> 4.8 us  [the longest x1 3.76 us: on_device(): theta_after = lax.ppermute(first_layer, 'az', ring('az', -1))]
    ppermute x2, starting transfers between devices: 2.71 us -> 1.65 us  [the longest x1 1.64 us: on_device(): theta_before = lax.ppermute(last_layer, 'az', ring('az', 1))]
  transfers between devices with their start and end apart: 6 -> 7, of which waited for: 3 -> 4; matrix products, arithmetic and copies ran while one was open for 0% -> 0% of each run, Pallas kernels for 6% -> 8%
where the time goes in v2:
time: 64.7 us; the launch traced here: 64 us
  starting transfers between devices  36 us (56%)
  Pallas kernels  12.5 us (19%)
  waiting for transfers between devices  9.59 us (15%)
  local copies, waits for them, and re-layouts  5.15 us (8%)
  between operations  0.82 us (1%)
    all_to_all x1, starting transfers between devices, on_device(): lax.all_to_all(packed, 'ax', split_axis=0, concat_axis=0, tiled=True)  13.7 us
    pallas_call x6, Pallas kernels, call(): pl.pallas_call(body, name=name, out_shape=out_shape, in_specs=[VMEM] * le...  12.5 us
    all_to_all x1, starting transfers between devices, on_device(): lax.all_to_all(source, 'az', split_axis=0, concat_axis=0, tiled=True)  8.64 us
    ppermute x1, starting transfers between devices, on_device(): x_after = lax.ppermute(first_x, 'ax', ring('ax', -1))  5.46 us
    unnamed x30, local copies, waits for them, and re-layouts  5.15 us
    ppermute x1, waiting for transfers between devices, on_device(): theta_after = lax.ppermute(first_layer, 'az', ring('az', -1))  3.76 us
    all_to_all x1, waiting for transfers between devices, on_device(): lax.all_to_all(source, 'az', split_axis=0, concat_axis=0, tiled=True)  3.5 us
    all_to_all x1, starting transfers between devices, on_device(): lax.all_to_all(coefficients.reshape(groups, th, LANES), 'az', split_axis=...  3.41 us
  transfers between devices with their start and end apart: 7, of which 4 were waited for; matrix products, arithmetic and copies ran while one was open for 0% of the time, Pallas kernels for 8%

profile of v2, /device:TPU:1, one launch (start us, length us, event | category | flops | bytes accessed | tf_op | source)
XLA Modules:
  0.0 64.0 jit_solution(17191687767553955310)
XLA Ops:
  0.6 0.0 copy-start.3
  0.6 3.1 %pack_bubbles.1 = (bf16[32,8,128]{2,1,0:T(8,128)(2,1)}, bf16[3,32,256]{2,1,0:T(8,128)(2,1)}, bf16[3,32,256]{2,1,0:T(8,128)(2,1)}) custom-call(f32[3,2048]{1,0:T(4,128)} %refs_0_.1, f32[16,128]{1,0:T(8,128)} %bitcast.9, f32[16,128]{1,0:T(8,128)} %bitcast.10, s32[16,128]{1,0:T(8,128)} %bitcast.11, s32[16,128]{1,0:T(8,128)} %bitcast.12, s32[1,32]{1,0:T(1,128)} %refs_5_.1, ...), custom_call_target="tpu_custom_call" | custom-call | bytes 852096 | tf_op jit(solution)/shard_map/pack_bubbles/pallas_call | solution.py:22
  3.7 13.7 %all-to-all-start = ((bf16[32,8,128]{2,1,0:T(8,128)(2,1)}), bf16[32,8,128]{2,1,0:T(8,128)(2,1)S(1)}, u32[]{:S(2)}, u32[]{:S(2)}) async-start(bf16[32,8,128]{2,1,0:T(8,128)(2,1)} %get-tuple-element.12._.refs_2_), calls=%async_computation | async-start | bytes 131072 | tf_op jit(solution)/shard_map/all_to_all | solution.py:328
  17.5 3.1 %collective-permute-start = (bf16[3,32,256]{2,1,0:T(8,128)(2,1)}, bf16[3,32,256]{2,1,0:T(8,128)(2,1)S(1)}, u32[]{:S(2)}, u32[]{:S(2)}) collective-permute-start(bf16[3,32,256]{2,1,0:T(8,128)(2,1)} %get-tuple-element.18), channel_id=1, source_target_pairs={{0,1},{1,2},{2,3},{3,4},{4,5},{5,6},{6,7},{7,8},{8,9},{9,10},{10,1... | collective-permute-start | bytes 147464 | tf_op jit(solution)/shard_map/ppermute | solution.py:331
  20.6 5.5 %collective-permute-start.1 = (bf16[3,32,256]{2,1,0:T(8,128)(2,1)}, bf16[3,32,256]{2,1,0:T(8,128)(2,1)S(1)}, u32[]{:S(2)}, u32[]{:S(2)}) collective-permute-start(bf16[3,32,256]{2,1,0:T(8,128)(2,1)} %get-tuple-element.19), channel_id=1, source_target_pairs={{0,31},{1,0},{2,1},{3,2},{4,3},{5,4},{6,5},{7,6},{8,7},{9,8},{10,9... | collective-permute-start | bytes 147464 | tf_op jit(solution)/shard_map/ppermute | solution.py:332
  26.1 1.1 %copy-done = f32[3,32,8,256]{3,2,1,0:T(8,128)S(1)} copy-done((f32[3,32,8,256]{3,2,1,0:T(8,128)S(1)}, f32[3,32,8,256]{3,2,1,0:T(8,128)}, u32[]{:S(2)}) %copy-start) | copy-done | bytes 786456
  27.2 0.8 %copy-done.4 = bf16[32,8,128]{2,1,0:T(8,128)(2,1)S(1)} copy-done((bf16[32,8,128]{2,1,0:T(8,128)(2,1)S(1)}, bf16[32,8,128]{2,1,0:T(8,128)(2,1)}, u32[]{:S(2)}) %copy-start.4) | copy-done | bytes 65560
  28.1 1.3 %interior.1 = (bf16[3,8,256]{2,1,0:T(8,128)(2,1)S(1)}, bf16[3,8,256]{2,1,0:T(8,128)(2,1)S(1)}, f32[32,8,256]{2,1,0:T(8,128)S(1)}) custom-call(f32[3,32,8,256]{3,2,1,0:T(8,128)S(1)} %copy-done, bf16[32,8,128]{2,1,0:T(8,128)(2,1)S(1)} %copy-done.4), custom_call_target="tpu_custom_call" | custom-call | bytes 851968 | tf_op jit(solution)/shard_map/interior/pallas_call | solution.py:22
  29.4 0.0 copy-start.5
  29.4 2.0 %source.1.refs_2_ = bf16[16,40,128]{2,1,0:T(8,128)(2,1)} custom-call(bf16[32,8,128]{2,1,0:T(8,128)(2,1)S(1)} %all-to-all-done.arrived, f32[32,8,256]{2,1,0:T(8,128)S(1)} %get-tuple-element.15.divergence, bf16[3,32,256]{2,1,0:T(8,128)(2,1)S(1)} %collective-permute-done.x_before, bf16[3,32,256]{2,1,0:T(8,128)(2,1)S(1)} %collective-permute-done.1.x_after, ...), custom_call_target="tpu_custom_call" | custom-call | flops 536870912 | bytes 450560 | tf_op jit(solution)/shard_map/source/pallas_call | solution.py:22
  31.4 8.6 %all-to-all-start.1 = ((bf16[16,40,128]{2,1,0:T(8,128)(2,1)}), bf16[16,40,128]{2,1,0:T(8,128)(2,1)S(1)}, u32[]{:S(2)}, u32[]{:S(2)}) async-start(bf16[16,40,128]{2,1,0:T(8,128)(2,1)} %source.1.refs_2_), calls=%async_computation.1 | async-start | bytes 327680 | tf_op jit(solution)/shard_map/all_to_all | solution.py:361
  40.1 1.6 %collective-permute-start.2 = (bf16[3,8,256]{2,1,0:T(8,128)(2,1)}, bf16[3,8,256]{2,1,0:T(8,128)(2,1)S(1)}, u32[]{:S(2)}, u32[]{:S(2)}) collective-permute-start(bf16[3,8,256]{2,1,0:T(8,128)(2,1)} %get-tuple-element.20), channel_id=1, source_target_pairs={{0,32},{32,64},{64,96},{96,128},{128,160},{160,192},{192,224},{224... | collective-permute-start | bytes 36872 | tf_op jit(solution)/shard_map/ppermute | solution.py:364
  41.7 1.0 %collective-permute-done.2.theta_before.before = bf16[3,8,256]{2,1,0:T(8,128)(2,1)S(1)} collective-permute-done((bf16[3,8,256]{2,1,0:T(8,128)(2,1)}, bf16[3,8,256]{2,1,0:T(8,128)(2,1)S(1)}, u32[]{:S(2)}, u32[]{:S(2)}) %collective-permute-start.2) | collective-permute-done | bytes 12320 | tf_op jit(solution)/shard_map/ppermute | solution.py:364
  42.8 3.8 %collective-permute-done.3.theta_after.after = bf16[3,8,256]{2,1,0:T(8,128)(2,1)S(1)} collective-permute-done((bf16[3,8,256]{2,1,0:T(8,128)(2,1)}, bf16[3,8,256]{2,1,0:T(8,128)(2,1)S(1)}, u32[]{:S(2)}, u32[]{:S(2)}) %collective-permute-start.3) | collective-permute-done | bytes 12320 | tf_op jit(solution)/shard_map/ppermute | solution.py:365
  46.6 3.5 %all-to-all-done.1 = bf16[16,40,128]{2,1,0:T(8,128)(2,1)S(1)} async-done(((bf16[16,40,128]{2,1,0:T(8,128)(2,1)}), bf16[16,40,128]{2,1,0:T(8,128)(2,1)S(1)}, u32[]{:S(2)}, u32[]{:S(2)}) %all-to-all-start.1) | async-done | bytes 163872 | tf_op jit(solution)/shard_map/all_to_all | solution.py:361
  50.1 1.0 %transform.1 = bf16[512,128]{1,0:T(8,128)(2,1)} custom-call(bf16[512,640]{1,0:T(8,128)(2,1)S(1)} %copy-done.3, bf16[640,128]{1,0:T(8,128)(2,1)S(1)} %bitcast.7, bf16[3,8,256]{2,1,0:T(8,128)(2,1)S(1)} %collective-permute-done.2.theta_before.before, bf16[3,8,256]{2,1,0:T(8,128)(2,1)S(1)} %collective-permute-done.3.theta_after.after), custom_call_target="tpu_custom_call" | custom-call | flops 83886080 | bytes 843776 | tf_op jit(solution)/shard_map/transform/pallas_call | solution.py:22
  51.1 3.4 %all-to-all-start.2 = ((bf16[16,32,128]{2,1,0:T(8,128)(2,1)}), bf16[16,32,128]{2,1,0:T(8,128)(2,1)S(1)}, u32[]{:S(2)}, u32[]{:S(2)}) async-start(bf16[16,32,128]{2,1,0:T(8,128)(2,1)} %bitcast.5), calls=%async_computation.2 | async-start | bytes 262144 | tf_op jit(solution)/shard_map/all_to_all | solution.py:393
  54.5 0.8 %copy-done.6 = bf16[32,8,128]{2,1,0:T(8,128)(2,1)S(1)} copy-done((bf16[32,8,128]{2,1,0:T(8,128)(2,1)S(1)}, bf16[32,8,128]{2,1,0:T(8,128)(2,1)}, u32[]{:S(2)}) %copy-start.6) | copy-done | bytes 65560
  55.3 0.7 %copy-done.8 = bf16[3,8,256]{2,1,0:T(8,128)(2,1)S(1)} copy-done((bf16[3,8,256]{2,1,0:T(8,128)(2,1)S(1)}, bf16[3,8,256]{2,1,0:T(8,128)(2,1)}, u32[]{:S(2)}) %copy-start.8) | copy-done | bytes 12312
  56.0 0.8 %copy-done.12 = bf16[3,32,256]{2,1,0:T(8,128)(2,1)S(1)} copy-done((bf16[3,32,256]{2,1,0:T(8,128)(2,1)S(1)}, bf16[3,32,256]{2,1,0:T(8,128)(2,1)}, u32[]{:S(2)}) %copy-start.12) | copy-done | bytes 49176
  56.8 0.8 %copy-done.14 = bf16[3,32,256]{2,1,0:T(8,128)(2,1)S(1)} copy-done((bf16[3,32,256]{2,1,0:T(8,128)(2,1)S(1)}, bf16[3,32,256]{2,1,0:T(8,128)(2,1)}, u32[]{:S(2)}) %copy-start.14) | copy-done | bytes 49176
  57.6 3.8 %predictor.1 = f32[3,32,8,256]{3,2,1,0:T(8,128)} custom-call(bf16[32,8,128]{2,1,0:T(8,128)(2,1)S(1)} %copy-done.6, f32[3,32,8,256]{3,2,1,0:T(8,128)S(1)} %copy-done.1, bf16[3,8,256]{2,1,0:T(8,128)(2,1)S(1)} %collective-permute-done.2.theta_before.before, bf16[3,8,256]{2,1,0:T(8,128)(2,1)S(1)} %copy-done.8, bf16[3,32,256]{2,1,0:T(8,128)(2,1)S(1)} %copy-done.12, ...), custom_call_target="tpu_custom_call" | custom-call | flops 1610612736 | bytes 974848 | tf_op jit(solution)/shard_map/predictor/pallas_call | solution.py:22
  61.4 1.3 %all-to-all-done.2.spread = bf16[16,32,128]{2,1,0:T(8,128)(2,1)S(1)} async-done(((bf16[16,32,128]{2,1,0:T(8,128)(2,1)}), bf16[16,32,128]{2,1,0:T(8,128)(2,1)S(1)}, u32[]{:S(2)}, u32[]{:S(2)}) %all-to-all-start.2) | async-done | bytes 131104 | tf_op jit(solution)/shard_map/all_to_all | solution.py:393
  62.7 1.4 %solve.1 = f32[256,256]{1,0:T(8,128)} custom-call(bf16[16,32,128]{2,1,0:T(8,128)(2,1)S(1)} %all-to-all-done.2.spread, bf16[16,256,256]{2,1,0:T(8,128)(2,1)S(1)} %copy-done.2), custom_call_target="tpu_custom_call" | custom-call | flops 33554432 | bytes 2228224 | tf_op jit(solution)/shard_map/solve/pallas_call | solution.py:22
  (28 shorter events, 0.1 us)
Async XLA Ops:
  0.6 49.4 %copy-start.3 = (bf16[512,640]{1,0:T(8,128)(2,1)S(1)}, bf16[512,640]{1,0:T(8,128)(2,1)}, u32[]{:S(2)}) copy-start(bf16[512,640]{1,0:T(8,128)(2,1)} %constant.2.clone.table) | copy-start | bytes 1966084
  3.7 25.7 %all-to-all-start = ((bf16[32,8,128]{2,1,0:T(8,128)(2,1)}), bf16[32,8,128]{2,1,0:T(8,128)(2,1)S(1)}, u32[]{:S(2)}, u32[]{:S(2)}) async-start(bf16[32,8,128]{2,1,0:T(8,128)(2,1)} %get-tuple-element.12._.refs_2_), calls=%async_computation | async-start | bytes 131072 | tf_op jit(solution)/shard_map/all_to_all | solution.py:328
  17.5 11.9 %collective-permute-start = (bf16[3,32,256]{2,1,0:T(8,128)(2,1)}, bf16[3,32,256]{2,1,0:T(8,128)(2,1)S(1)}, u32[]{:S(2)}, u32[]{:S(2)}) collective-permute-start(bf16[3,32,256]{2,1,0:T(8,128)(2,1)} %get-tuple-element.18), channel_id=1, source_target_pairs={{0,1},{1,2},{2,3},{3,4},{4,5},{5,6},{6,7},{7,8},{8,9},{9,10},{10,1... | collective-permute-start | bytes 147464 | tf_op jit(solution)/shard_map/ppermute | solution.py:331
  20.6 8.8 %collective-permute-start.1 = (bf16[3,32,256]{2,1,0:T(8,128)(2,1)}, bf16[3,32,256]{2,1,0:T(8,128)(2,1)S(1)}, u32[]{:S(2)}, u32[]{:S(2)}) collective-permute-start(bf16[3,32,256]{2,1,0:T(8,128)(2,1)} %get-tuple-element.19), channel_id=1, source_target_pairs={{0,31},{1,0},{2,1},{3,2},{4,3},{5,4},{6,5},{7,6},{8,7},{9,8},{10,9... | collective-permute-start | bytes 147464 | tf_op jit(solution)/shard_map/ppermute | solution.py:332
  26.1 1.1 %copy-start = (f32[3,32,8,256]{3,2,1,0:T(8,128)S(1)}, f32[3,32,8,256]{3,2,1,0:T(8,128)}, u32[]{:S(2)}) copy-start(f32[3,32,8,256]{3,2,1,0:T(8,128)} %velocity.3) | copy-start | bytes 2359300
  27.2 0.8 %copy-start.4 = (bf16[32,8,128]{2,1,0:T(8,128)(2,1)S(1)}, bf16[32,8,128]{2,1,0:T(8,128)(2,1)}, u32[]{:S(2)}) copy-start(bf16[32,8,128]{2,1,0:T(8,128)(2,1)} %get-tuple-element.12._.refs_2_) | copy-start | bytes 196612
  28.1 26.4 %copy-start.1 = (f32[3,32,8,256]{3,2,1,0:T(8,128)S(1)}, f32[3,32,8,256]{3,2,1,0:T(8,128)}, u32[]{:S(2)}) copy-start(f32[3,32,8,256]{3,2,1,0:T(8,128)} %velocity.3) | copy-start | bytes 2359300
  29.3 10.7 %copy-start.9 = (bf16[3,8,256]{2,1,0:T(8,128)(2,1)}, bf16[3,8,256]{2,1,0:T(8,128)(2,1)S(1)}, u32[]{:S(2)}) copy-start(bf16[3,8,256]{2,1,0:T(8,128)(2,1)S(1)} %get-tuple-element.13.first_theta.refs_0_) | copy-start | bytes 36868
  29.3 10.7 %copy-start.10 = (bf16[3,8,256]{2,1,0:T(8,128)(2,1)}, bf16[3,8,256]{2,1,0:T(8,128)(2,1)S(1)}, u32[]{:S(2)}) copy-start(bf16[3,8,256]{2,1,0:T(8,128)(2,1)S(1)} %get-tuple-element.14.last_theta.refs_1_) | copy-start | bytes 36868
  29.4 2.1 %copy-start.11 = (bf16[3,32,256]{2,1,0:T(8,128)(2,1)}, bf16[3,32,256]{2,1,0:T(8,128)(2,1)S(1)}, u32[]{:S(2)}) copy-start(bf16[3,32,256]{2,1,0:T(8,128)(2,1)S(1)} %collective-permute-done.x_before) | copy-start | bytes 147460
  29.4 2.0 %copy-start.13 = (bf16[3,32,256]{2,1,0:T(8,128)(2,1)}, bf16[3,32,256]{2,1,0:T(8,128)(2,1)S(1)}, u32[]{:S(2)}) copy-start(bf16[3,32,256]{2,1,0:T(8,128)(2,1)S(1)} %collective-permute-done.1.x_after) | copy-start | bytes 147460
  29.4 2.0 %copy-start.5 = (bf16[32,8,128]{2,1,0:T(8,128)(2,1)}, bf16[32,8,128]{2,1,0:T(8,128)(2,1)S(1)}, u32[]{:S(2)}) copy-start(bf16[32,8,128]{2,1,0:T(8,128)(2,1)S(1)} %all-to-all-done.arrived) | copy-start | bytes 196612
  31.4 18.6 %all-to-all-start.1 = ((bf16[16,40,128]{2,1,0:T(8,128)(2,1)}), bf16[16,40,128]{2,1,0:T(8,128)(2,1)S(1)}, u32[]{:S(2)}, u32[]{:S(2)}) async-start(bf16[16,40,128]{2,1,0:T(8,128)(2,1)} %source.1.refs_2_), calls=%async_computation.1 | async-start | bytes 327680 | tf_op jit(solution)/shard_map/all_to_all | solution.py:361
  40.1 2.7 %collective-permute-start.2 = (bf16[3,8,256]{2,1,0:T(8,128)(2,1)}, bf16[3,8,256]{2,1,0:T(8,128)(2,1)S(1)}, u32[]{:S(2)}, u32[]{:S(2)}) collective-permute-start(bf16[3,8,256]{2,1,0:T(8,128)(2,1)} %get-tuple-element.20), channel_id=1, source_target_pairs={{0,32},{32,64},{64,96},{96,128},{128,160},{160,192},{192,224},{224... | collective-permute-start | bytes 36872 | tf_op jit(solution)/shard_map/ppermute | solution.py:364
  41.7 4.8 %collective-permute-start.3 = (bf16[3,8,256]{2,1,0:T(8,128)(2,1)}, bf16[3,8,256]{2,1,0:T(8,128)(2,1)S(1)}, u32[]{:S(2)}, u32[]{:S(2)}) collective-permute-start(bf16[3,8,256]{2,1,0:T(8,128)(2,1)} %get-tuple-element.21), channel_id=1, source_target_pairs={{0,480},{32,0},{64,32},{96,64},{128,96},{160,128},{192,160},{224,1... | collective-permute-start | bytes 36872 | tf_op jit(solution)/shard_map/ppermute | solution.py:365
  46.5 4.5 %copy-start.7 = (bf16[3,8,256]{2,1,0:T(8,128)(2,1)}, bf16[3,8,256]{2,1,0:T(8,128)(2,1)S(1)}, u32[]{:S(2)}) copy-start(bf16[3,8,256]{2,1,0:T(8,128)(2,1)S(1)} %collective-permute-done.3.theta_after.after) | copy-start | bytes 36868
  51.1 11.6 %all-to-all-start.2 = ((bf16[16,32,128]{2,1,0:T(8,128)(2,1)}), bf16[16,32,128]{2,1,0:T(8,128)(2,1)S(1)}, u32[]{:S(2)}, u32[]{:S(2)}) async-start(bf16[16,32,128]{2,1,0:T(8,128)(2,1)} %bitcast.5), calls=%async_computation.2 | async-start | bytes 262144 | tf_op jit(solution)/shard_map/all_to_all | solution.py:393
  54.5 0.8 %copy-start.6 = (bf16[32,8,128]{2,1,0:T(8,128)(2,1)S(1)}, bf16[32,8,128]{2,1,0:T(8,128)(2,1)}, u32[]{:S(2)}) copy-start(bf16[32,8,128]{2,1,0:T(8,128)(2,1)} %copy-done.5) | copy-start | bytes 196612
  55.3 0.7 %copy-start.8 = (bf16[3,8,256]{2,1,0:T(8,128)(2,1)S(1)}, bf16[3,8,256]{2,1,0:T(8,128)(2,1)}, u32[]{:S(2)}) copy-start(bf16[3,8,256]{2,1,0:T(8,128)(2,1)} %copy-done.7) | copy-start | bytes 36868
  56.0 0.8 %copy-start.12 = (bf16[3,32,256]{2,1,0:T(8,128)(2,1)S(1)}, bf16[3,32,256]{2,1,0:T(8,128)(2,1)}, u32[]{:S(2)}) copy-start(bf16[3,32,256]{2,1,0:T(8,128)(2,1)} %copy-done.11) | copy-start | bytes 147460
  56.8 0.8 %copy-start.14 = (bf16[3,32,256]{2,1,0:T(8,128)(2,1)S(1)}, bf16[3,32,256]{2,1,0:T(8,128)(2,1)}, u32[]{:S(2)}) copy-start(bf16[3,32,256]{2,1,0:T(8,128)(2,1)} %copy-done.13) | copy-start | bytes 147460
  57.6 5.1 %copy-start.2 = (bf16[16,256,256]{2,1,0:T(8,128)(2,1)S(1)}, bf16[16,256,256]{2,1,0:T(8,128)(2,1)}, u32[]{:S(2)}) copy-start(bf16[16,256,256]{2,1,0:T(8,128)(2,1)} %inverse.1) | copy-start | bytes 6291460

commit v3 on v2

--- a/solution.py
+++ b/solution.py
@@ -17,14 +17,18 @@
 ANY = pl.BlockSpec(memory_space=pl.ANY)
 
 
-def call(body, name, out_shape, operands, scratch=(), specs=None, flops=0, limit=24):
+def call(
+    body, name, out_shape, operands, scratch=(), specs=None, flops=0, limit=24, out_specs=None,
+    aliases=None,
+):
     moved = sum(x.size * x.dtype.itemsize for x in operands)
     return pl.pallas_call(
         body,
         name=name,
         out_shape=out_shape,
         in_specs=[VMEM] * len(operands) if specs is None else specs,
-        out_specs=jax.tree.map(lambda _: VMEM, out_shape),
+        out_specs=jax.tree.map(lambda _: VMEM, out_shape) if out_specs is None else out_specs,
+        input_output_aliases=aliases or {},
         scratch_shapes=list(scratch),
         compiler_params=pltpu.CompilerParams(vmem_limit_bytes=limit * 1024 * 1024),
         cost_estimate=pl.CostEstimate(flops=flops, bytes_accessed=moved, transcendentals=0),
@@ -41,8 +45,9 @@
 
 
 def pack_body(*refs):
-    hbm, (out, first_x, last_x), held = refs[:8], refs[8:11], refs[11:19]
-    listed, slips, payload, staged, sems = refs[19:]
+    hbm, held = refs[:8], refs[13:21]
+    out, first_x, last_x, first_theta, last_theta = refs[8:13]
+    listed, slips, payload, staged, sems = refs[21:]
     copies = [
         pltpu.make_async_copy(source, target, sems.at[i])
         for i, (source, target) in enumerate(zip(hbm, held))
@@ -94,6 +99,8 @@
     copies[7].wait()
     first_x[...] = block[:, :, 0, :].astype(jnp.bfloat16)
     last_x[...] = block[:, :, ROWS - 1, :].astype(jnp.bfloat16)
+    first_theta[...] = block[:, 0].astype(jnp.bfloat16)
+    last_theta[...] = block[:, block.shape[1] - 1].astype(jnp.bfloat16)
 
 
 def radial_neighbours(v):
@@ -109,37 +116,6 @@
     ahead = jnp.where(row == ROWS - 1, after, pltpu.roll(v, ROWS - 1, 0))
     behind = jnp.where(row == 0, before, pltpu.roll(v, 1, 0))
     return ahead, behind
-
-
-def interior_body(
-    velocity, _, first_theta, last_theta, divergence, held, sems
-):
-    th, width = held.shape[1], held.shape[3]
-    parts = sems.shape[1]
-    step = th // parts
-    copies = []
-    for c in range(3):
-        for p in range(parts):
-            span = (c, pl.ds(p * step, step))
-            copies.append(pltpu.make_async_copy(velocity.at[span], held.at[span], sems.at[c, p]))
-    for copy in copies:
-        copy.start()
-    for copy in copies:
-        copy.wait()
-    first_theta[...] = held[:, 0].astype(jnp.bfloat16)
-    last_theta[...] = held[:, th - 1].astype(jnp.bfloat16)
-    radius = lax.broadcasted_iota(jnp.int32, (ROWS, width), 1).astype(jnp.float32)
-    outward = (radius + 1.0) / (2.0 * radius + 1.0)
-    inward = radius / (2.0 * radius + 1.0)
-    for t in range(th):
-        ahead, behind = axial_neighbours(held[0, t], 0.0, 0.0)
-        around = ahead - behind
-        if t < th - 1:
-            around = around + held[1, t + 1]
-        if t > 0:
-            around = around - held[1, t - 1]
-        outer, inner = radial_neighbours(held[2, t])
-        divergence[t] = 0.5 * around + (outward * outer - inward * inner)
 
 
 def after(arrays, event):
@@ -179,37 +155,83 @@
     )
 
 
-def source_body(
-    arrived, divergence, x_before, x_after, first_theta, last_theta, out, across, along, whole
+def partial_body(
+    arrived, velocity, out, edges, across, along, total, whole
 ):
-    th = divergence.shape[0]
     hot_parts(arrived, 3, 1, across, along)
     density = deposit(across[...], along[0])
-    total = density + divergence[...].reshape(density.shape)
+    th, width = velocity.shape[1], velocity.shape[3]
+    radius = lax.broadcasted_iota(jnp.int32, (ROWS, width), 1).astype(jnp.float32)
+    outward = (radius + 1.0) / (2.0 * radius + 1.0)
+    inward = radius / (2.0 * radius + 1.0)
+    for t in range(th):
+        ahead, behind = axial_neighbours(velocity[0, t], 0.0, 0.0)
+        around = ahead - behind
+        if t < th - 1:
+            around = around + velocity[1, t + 1]
+        if t > 0:
+            around = around - velocity[1, t - 1]
+        outer, inner = radial_neighbours(velocity[2, t])
+        total[t * ROWS : (t + 1) * ROWS, :] = 0.5 * around + (outward * outer - inward * inner)
     halves = whole.shape[0]
     blank = jnp.zeros((out.shape[1] - th - 2, LANES), jnp.float32)
-    first = first_theta[1].astype(jnp.float32)
-    last = last_theta[1].astype(jnp.float32)
+    first = velocity[1, 0]
+    last = velocity[1, th - 1]
     for half in range(halves):
         span = slice(half * LANES, (half + 1) * LANES)
-        whole[half] = total[:, span]
+        whole[half] = density[:, span] + total[:, span]
         for x in range(ROWS):
             layer = whole[half, pl.ds(x, th, stride=ROWS), :]
+            ends = [first[x : x + 1, span], last[x : x + 1, span], blank]
+            column = jnp.concatenate([layer] + ends, axis=0)
+            out[x * halves + half] = column.astype(jnp.bfloat16)
             if x == 0:
-                layer = layer - 0.5 * x_before[0, :, span].astype(jnp.float32)
+                edges[half] = column
             if x == ROWS - 1:
-                layer = layer + 0.5 * x_after[0, :, span].astype(jnp.float32)
-            edges = [first[x : x + 1, span], last[x : x + 1, span], blank]
-            column = jnp.concatenate([layer] + edges, axis=0)
-            out[x * halves + half] = column.astype(jnp.bfloat16)
-
-
-def predictor_body(
-    arrived, velocity, theta_before, theta_after, x_before, x_after, out, across, along, low, high,
-    density,
-):
+                edges[halves + half] = column
+
+
+def complete_body(_, edges, x_before, x_after, out, staged, sems):
+    groups, th = out.shape[0], x_before.shape[1]
+    halves = edges.shape[0] // 2
+    for half in range(halves):
+        span = slice(half * LANES, (half + 1) * LANES)
+        before = 0.5 * x_before[0, :, span].astype(jnp.float32)
+        beyond = 0.5 * x_after[0, :, span].astype(jnp.float32)
+        blank = jnp.zeros((edges.shape[1] - th, LANES), jnp.float32)
+        low = edges[half] - jnp.concatenate([before, blank], axis=0)
+        high = edges[halves + half] + jnp.concatenate([beyond, blank], axis=0)
+        staged[half] = low.astype(jnp.bfloat16)
+        staged[halves + half] = high.astype(jnp.bfloat16)
+    copies = [
+        pltpu.make_async_copy(
+            staged.at[pl.ds(i * halves, halves)],
+            out.at[pl.ds(i * (groups - halves), halves)],
+            sems.at[i],
+        )
+        for i in range(2)
+    ]
+    for copy in copies:
+        copy.start()
+    for copy in copies:
+        copy.wait()
+
+
+def predictor_body(*refs):
+    hbm, out, held = refs[:6], refs[6], refs[7:13]
+    across, along, low, high, density, sems = refs[13:]
+    arrived, velocity, theta_before, theta_after, x_before, x_after = held
+    copies = [
+        pltpu.make_async_copy(source, target, sems.at[i])
+        for i, (source, target) in enumerate(zip(hbm, held))
+    ]
+    for copy in copies:
+        copy.start()
+    copies[0].wait()
     th, width = velocity.shape[1], velocity.shape[3]
     hot_parts(arrived, 0, 3, across, along)
+    for copy in copies[1:]:
+        copy.wait()
     radius = lax.broadcasted_iota(jnp.int32, (ROWS, width), 1).astype(jnp.float32)
     outward = (radius + 1.0) / (radius + 0.5)
     inward = radius / (radius + 0.5)
@@ -305,13 +327,15 @@
         bubble_order,
     )
     bubbles_in = bubbles_in + (velocity,)
-    packed, first_x, last_x = call(
+    packed, first_x, last_x, first_theta, last_theta = call(
         pack_body,
         "pack_bubbles",
         (
             struct((peers, ROWS, LANES), bf16),
             struct((3, th, width), bf16),
             struct((3, th, width), bf16),
+            struct((3, ax, width), bf16),
+            struct((3, ax, width), bf16),
         ),
         bubbles_in,
         specs=[ANY] * 8,
@@ -327,36 +351,40 @@
     )
     arrived = lax.all_to_all(packed, "ax", split_axis=0, concat_axis=0, tiled=True)
 
-    first_x, last_x = after((first_x, last_x), packed)
     x_before = lax.ppermute(last_x, "ax", ring("ax", 1))
     x_after = lax.ppermute(first_x, "ax", ring("ax", -1))
-    first_theta, last_theta, divergence = call(
-        interior_body,
-        "interior",
-        (
-            struct((3, ax, width), bf16),
-            struct((3, ax, width), bf16),
-            struct((th, ax, width), f32),
-        ),
-        (velocity, packed),
-        specs=[ANY, ANY],
-        scratch=(pltpu.VMEM(velocity.shape, f32), pltpu.SemaphoreType.DMA((3, 2))),
-    )
-
     slots = peers * LANES
     cells = th * ax
     extra = 8
-    source = call(
-        source_body,
-        "source",
-        struct((groups, th + extra, LANES), bf16),
-        (arrived, divergence, x_before, x_after, first_theta, last_theta),
+    halves = width // LANES
+    partial, edges = call(
+        partial_body,
+        "partial_source",
+        (
+            struct((groups, th + extra, LANES), bf16),
+            struct((2 * halves, th + extra, LANES), f32),
+        ),
+        (arrived, velocity),
         scratch=(
             pltpu.VMEM((cells, slots), bf16),
             pltpu.VMEM((1, width, slots), bf16),
-            pltpu.VMEM((width // LANES, cells, LANES), f32),
+            pltpu.VMEM((cells, width), f32),
+            pltpu.VMEM((halves, cells, LANES), f32),
         ),
         flops=2 * cells * slots * width,
+    )
+    source = call(
+        complete_body,
+        "complete_source",
+        struct(partial.shape, bf16),
+        (partial, edges, x_before, x_after),
+        specs=[ANY, VMEM, VMEM, VMEM],
+        out_specs=ANY,
+        aliases={0: 0},
+        scratch=(
+            pltpu.VMEM((2 * halves, th + extra, LANES), bf16),
+            pltpu.SemaphoreType.DMA((2,)),
+        ),
     )
     gathered = lax.all_to_all(source, "az", split_axis=0, concat_axis=0, tiled=True)
 
@@ -364,20 +392,24 @@
     theta_before = lax.ppermute(last_layer, "az", ring("az", 1))
     theta_after = lax.ppermute(first_layer, "az", ring("az", -1))
 
+    beside = (arrived, velocity, theta_before, theta_after, x_before, x_after)
     predicted = call(
         predictor_body,
         "predictor",
         struct(velocity.shape, f32),
-        (arrived, velocity, theta_before, theta_after, x_before, x_after),
-        scratch=(
+        beside,
+        specs=[ANY] * 6,
+        scratch=tuple(pltpu.VMEM(x.shape, x.dtype) for x in beside)
+        + (
             pltpu.VMEM((cells, slots), bf16),
             pltpu.VMEM((3, width, slots), bf16),
             pltpu.VMEM((3, th, width), f32),
             pltpu.VMEM((3, th, width), f32),
             pltpu.VMEM((cells, width), f32),
+            pltpu.SemaphoreType.DMA((6,)),
         ),
         flops=2 * 3 * cells * slots * width,
-        limit=32,
+        limit=56,
     )
 
     length = groups * th

time: 64.7 us -> 63.9 us (0.988)
  local copies, waits for them, and re-layouts: 5.15 us -> 1.17 us
  Pallas kernels: 12.5 us -> 14.2 us
  waiting for transfers between devices: 9.59 us -> 10.8 us
    unnamed x30 -> x16, local copies, waits for them, and re-layouts: 5.15 us -> 1.17 us
    pallas_call x6, Pallas kernels: 12.5 us -> 14.2 us  [call(): pl.pallas_call(body, name=name, out_shape=out_shape, in_specs=[VMEM] * le...]
    all_to_all x1, waiting for transfers between devices: 1.28 us -> 2.13 us  [on_device(): lax.all_to_all(coefficients.reshape(groups, th, LANES), 'az', split_axis=...]
  transfers between devices with their start and end apart: 7 -> 7, of which waited for: 4 -> 5; matrix products, arithmetic and copies ran while one was open for 0% -> 0% of each run, Pallas kernels for 8% -> 13%
where the time goes in v3:
time: 63.9 us; the launch traced here: 63.5 us
  starting transfers between devices  36.5 us (57%)
  Pallas kernels  14.2 us (22%)
  waiting for transfers between devices  10.8 us (17%)
  local copies, waits for them, and re-layouts  1.17 us (2%)
  between operations  0.76 us (1%)
    pallas_call x6, Pallas kernels, call(): pl.pallas_call(body, name=name, out_shape=out_shape, in_specs=[VMEM] * le...  14.2 us
    all_to_all x1, starting transfers between devices, on_device(): lax.all_to_all(packed, 'ax', split_axis=0, concat_axis=0, tiled=True)  13.7 us
    all_to_all x1, starting transfers between devices, on_device(): lax.all_to_all(source, 'az', split_axis=0, concat_axis=0, tiled=True)  9.13 us
    ppermute x1, starting transfers between devices, on_device(): x_after = lax.ppermute(first_x, 'ax', ring('ax', -1))  5.46 us
    ppermute x1, waiting for transfers between devices, on_device(): theta_after = lax.ppermute(first_layer, 'az', ring('az', -1))  3.78 us
    all_to_all x1, waiting for transfers between devices, on_device(): lax.all_to_all(source, 'az', split_axis=0, concat_axis=0, tiled=True)  3.5 us
    all_to_all x1, starting transfers between devices, on_device(): lax.all_to_all(coefficients.reshape(groups, th, LANES), 'az', split_axis=...  3.41 us
    ppermute x1, starting transfers between devices, on_device(): x_before = lax.ppermute(last_x, 'ax', ring('ax', 1))  3.14 us
  transfers between devices with their start and end apart: 7, of which 5 were waited for; matrix products, arithmetic and copies ran while one was open for 0% of the time, Pallas kernels for 13%

profile of v3, /device:TPU:1, one launch (start us, length us, event | category | flops | bytes accessed | tf_op | source)
XLA Modules:
  0.0 63.5 jit_solution(11879005088127107622)
XLA Ops:
  0.6 0.0 copy-start.2
  0.6 3.1 %pack_bubbles.1 = (bf16[32,8,128]{2,1,0:T(8,128)(2,1)}, bf16[3,32,256]{2,1,0:T(8,128)(2,1)}, bf16[3,32,256]{2,1,0:T(8,128)(2,1)}, bf16[3,8,256]{2,1,0:T(8,128)(2,1)}, bf16[3,8,256]{2,1,0:T(8,128)(2,1)}) custom-call(f32[3,2048]{1,0:T(4,128)} %refs_0_.1, f32[16,128]{1,0:T(8,128)} %bitcast.9, f32[16,128]{1,0:T(8,128)} %bitcast.10, s32[16,128]{1,0:T(8,128)} %bitcast.11, ...), custom_call_target="tpu_custom_call" | custom-call | bytes 852096 | tf_op jit(solution)/shard_map/pack_bubbles/pallas_call | solution.py:25
  3.7 13.7 %all-to-all-start = ((bf16[32,8,128]{2,1,0:T(8,128)(2,1)}), bf16[32,8,128]{2,1,0:T(8,128)(2,1)S(1)}, u32[]{:S(2)}, u32[]{:S(2)}) async-start(bf16[32,8,128]{2,1,0:T(8,128)(2,1)} %get-tuple-element.11), calls=%async_computation | async-start | bytes 131072 | tf_op jit(solution)/shard_map/all_to_all | solution.py:352
  17.5 3.1 %collective-permute-start = (bf16[3,32,256]{2,1,0:T(8,128)(2,1)}, bf16[3,32,256]{2,1,0:T(8,128)(2,1)S(1)}, u32[]{:S(2)}, u32[]{:S(2)}) collective-permute-start(bf16[3,32,256]{2,1,0:T(8,128)(2,1)} %get-tuple-element.16), channel_id=1, source_target_pairs={{0,1},{1,2},{2,3},{3,4},{4,5},{5,6},{6,7},{7,8},{8,9},{9,10},{10,1... | collective-permute-start | bytes 147464 | tf_op jit(solution)/shard_map/ppermute | solution.py:354
  20.6 5.5 %collective-permute-start.1 = (bf16[3,32,256]{2,1,0:T(8,128)(2,1)}, bf16[3,32,256]{2,1,0:T(8,128)(2,1)S(1)}, u32[]{:S(2)}, u32[]{:S(2)}) collective-permute-start(bf16[3,32,256]{2,1,0:T(8,128)(2,1)} %get-tuple-element.17), channel_id=1, source_target_pairs={{0,31},{1,0},{2,1},{3,2},{4,3},{5,4},{6,5},{7,6},{8,7},{9,8},{10,9... | collective-permute-start | bytes 147464 | tf_op jit(solution)/shard_map/ppermute | solution.py:355
  26.1 0.3 all-to-all-done.arrived.refs_0_
  26.4 1.1 %copy-done.1 = f32[3,32,8,256]{3,2,1,0:T(8,128)S(1)} copy-done((f32[3,32,8,256]{3,2,1,0:T(8,128)S(1)}, f32[3,32,8,256]{3,2,1,0:T(8,128)}, u32[]{:S(2)}) %copy-start.1) | copy-done | bytes 786456
  27.6 2.1 %partial_source.1 = (bf16[16,40,128]{2,1,0:T(8,128)(2,1)}, f32[4,40,128]{2,1,0:T(8,128)S(1)}) custom-call(bf16[32,8,128]{2,1,0:T(8,128)(2,1)S(1)} %all-to-all-done.arrived.refs_0_, f32[3,32,8,256]{3,2,1,0:T(8,128)S(1)} %copy-done.1), custom_call_target="tpu_custom_call" | custom-call | flops 536870912 | bytes 851968 | tf_op jit(solution)/shard_map/partial_source/pallas_call | solution.py:25
  29.7 0.0 collective-permute-done.x_before.refs_4_
  29.7 0.0 collective-permute-done.1.x_after.refs_5_
  29.7 0.7 %complete_source.1.refs_2_ = bf16[16,40,128]{2,1,0:T(8,128)(2,1)} custom-call(bf16[16,40,128]{2,1,0:T(8,128)(2,1)} %get-tuple-element.14._, f32[4,40,128]{2,1,0:T(8,128)S(1)} %get-tuple-element.15.edges, bf16[3,32,256]{2,1,0:T(8,128)(2,1)S(1)} %collective-permute-done.x_before.refs_4_, ...), custom_call_target="tpu_custom_call", output_to_operand_aliasing={{}: (0, {})} | custom-call | bytes 344064 | tf_op jit(solution)/shard_map/complete_source/pallas_call | solution.py:25
  30.4 9.1 %all-to-all-start.1 = ((bf16[16,40,128]{2,1,0:T(8,128)(2,1)}), bf16[16,40,128]{2,1,0:T(8,128)(2,1)S(1)}, u32[]{:S(2)}, u32[]{:S(2)}) async-start(bf16[16,40,128]{2,1,0:T(8,128)(2,1)} %complete_source.1.refs_2_), calls=%async_computation.1 | async-start | bytes 327680 | tf_op jit(solution)/shard_map/all_to_all | solution.py:389
  39.5 1.6 %collective-permute-start.2 = (bf16[3,8,256]{2,1,0:T(8,128)(2,1)}, bf16[3,8,256]{2,1,0:T(8,128)(2,1)S(1)}, u32[]{:S(2)}, u32[]{:S(2)}) collective-permute-start(bf16[3,8,256]{2,1,0:T(8,128)(2,1)} %get-tuple-element.18), channel_id=1, source_target_pairs={{0,32},{32,64},{64,96},{96,128},{128,160},{160,192},{192,224},{224... | collective-permute-start | bytes 36872 | tf_op jit(solution)/shard_map/ppermute | solution.py:392
  41.1 0.0 collective-permute-start.3
  41.1 1.0 %collective-permute-done.2.refs_2_.before = bf16[3,8,256]{2,1,0:T(8,128)(2,1)S(1)} collective-permute-done((bf16[3,8,256]{2,1,0:T(8,128)(2,1)}, bf16[3,8,256]{2,1,0:T(8,128)(2,1)S(1)}, u32[]{:S(2)}, u32[]{:S(2)}) %collective-permute-start.2) | collective-permute-done | bytes 12320 | tf_op jit(solution)/shard_map/ppermute | solution.py:392
  42.2 3.8 %collective-permute-done.3.refs_3_.after = bf16[3,8,256]{2,1,0:T(8,128)(2,1)S(1)} collective-permute-done((bf16[3,8,256]{2,1,0:T(8,128)(2,1)}, bf16[3,8,256]{2,1,0:T(8,128)(2,1)S(1)}, u32[]{:S(2)}, u32[]{:S(2)}) %collective-permute-start.3) | collective-permute-done | bytes 12320 | tf_op jit(solution)/shard_map/ppermute | solution.py:393
  46.0 3.5 %all-to-all-done.1 = bf16[16,40,128]{2,1,0:T(8,128)(2,1)S(1)} async-done(((bf16[16,40,128]{2,1,0:T(8,128)(2,1)}), bf16[16,40,128]{2,1,0:T(8,128)(2,1)S(1)}, u32[]{:S(2)}, u32[]{:S(2)}) %all-to-all-start.1) | async-done | bytes 163872 | tf_op jit(solution)/shard_map/all_to_all | solution.py:389
  49.5 1.0 %transform.1 = bf16[512,128]{1,0:T(8,128)(2,1)} custom-call(bf16[512,640]{1,0:T(8,128)(2,1)S(1)} %copy-done.2, bf16[640,128]{1,0:T(8,128)(2,1)S(1)} %bitcast.7, bf16[3,8,256]{2,1,0:T(8,128)(2,1)S(1)} %collective-permute-done.2.refs_2_.before, bf16[3,8,256]{2,1,0:T(8,128)(2,1)S(1)} %collective-permute-done.3.refs_3_.after), custom_call_target="tpu_custom_call" | custom-call | flops 83886080 | bytes 843776 | tf_op jit(solution)/shard_map/transform/pallas_call | solution.py:25
  50.5 0.0 copy-done.3
  50.5 3.4 %all-to-all-start.2 = ((bf16[16,32,128]{2,1,0:T(8,128)(2,1)}), bf16[16,32,128]{2,1,0:T(8,128)(2,1)S(1)}, u32[]{:S(2)}, u32[]{:S(2)}) async-start(bf16[16,32,128]{2,1,0:T(8,128)(2,1)} %bitcast.5), calls=%async_computation.2 | async-start | bytes 262144 | tf_op jit(solution)/shard_map/all_to_all | solution.py:425
  53.9 0.0 copy-start
  53.9 6.0 %predictor.1 = f32[3,32,8,256]{3,2,1,0:T(8,128)} custom-call(bf16[32,8,128]{2,1,0:T(8,128)(2,1)} %copy-done.3, f32[3,32,8,256]{3,2,1,0:T(8,128)} %refs_1_.1, bf16[3,8,256]{2,1,0:T(8,128)(2,1)} %copy-done.6, bf16[3,8,256]{2,1,0:T(8,128)(2,1)} %copy-done.7, bf16[3,32,256]{2,1,0:T(8,128)(2,1)} %copy-done.4, bf16[3,32,256]{2,1,0:T(8,128)(2,1)} %copy-done.5), custom_call_target="tpu_custom_call" | custom-call | flops 1610612736 | bytes 974848 | tf_op jit(solution)/shard_map/predictor/pallas_call | solution.py:25
  60.0 2.1 %all-to-all-done.2.spread = bf16[16,32,128]{2,1,0:T(8,128)(2,1)S(1)} async-done(((bf16[16,32,128]{2,1,0:T(8,128)(2,1)}), bf16[16,32,128]{2,1,0:T(8,128)(2,1)S(1)}, u32[]{:S(2)}, u32[]{:S(2)}) %all-to-all-start.2) | async-done | bytes 131104 | tf_op jit(solution)/shard_map/all_to_all | solution.py:425
  62.1 1.4 %solve.1 = f32[256,256]{1,0:T(8,128)} custom-call(bf16[16,32,128]{2,1,0:T(8,128)(2,1)S(1)} %all-to-all-done.2.spread, bf16[16,256,256]{2,1,0:T(8,128)(2,1)S(1)} %copy-done), custom_call_target="tpu_custom_call" | custom-call | flops 33554432 | bytes 2228224 | tf_op jit(solution)/shard_map/solve/pallas_call | solution.py:25
  (13 shorter events, 0.0 us)
Async XLA Ops:
  0.6 48.8 %copy-start.2 = (bf16[512,640]{1,0:T(8,128)(2,1)S(1)}, bf16[512,640]{1,0:T(8,128)(2,1)}, u32[]{:S(2)}) copy-start(bf16[512,640]{1,0:T(8,128)(2,1)} %constant.2.clone.table) | copy-start | bytes 1966084
  3.7 22.7 %all-to-all-start = ((bf16[32,8,128]{2,1,0:T(8,128)(2,1)}), bf16[32,8,128]{2,1,0:T(8,128)(2,1)S(1)}, u32[]{:S(2)}, u32[]{:S(2)}) async-start(bf16[32,8,128]{2,1,0:T(8,128)(2,1)} %get-tuple-element.11), calls=%async_computation | async-start | bytes 131072 | tf_op jit(solution)/shard_map/all_to_all | solution.py:352
  17.5 12.2 %collective-permute-start = (bf16[3,32,256]{2,1,0:T(8,128)(2,1)}, bf16[3,32,256]{2,1,0:T(8,128)(2,1)S(1)}, u32[]{:S(2)}, u32[]{:S(2)}) collective-permute-start(bf16[3,32,256]{2,1,0:T(8,128)(2,1)} %get-tuple-element.16), channel_id=1, source_target_pairs={{0,1},{1,2},{2,3},{3,4},{4,5},{5,6},{6,7},{7,8},{8,9},{9,10},{10,1... | collective-permute-start | bytes 147464 | tf_op jit(solution)/shard_map/ppermute | solution.py:354
  20.6 9.0 %collective-permute-start.1 = (bf16[3,32,256]{2,1,0:T(8,128)(2,1)}, bf16[3,32,256]{2,1,0:T(8,128)(2,1)S(1)}, u32[]{:S(2)}, u32[]{:S(2)}) collective-permute-start(bf16[3,32,256]{2,1,0:T(8,128)(2,1)} %get-tuple-element.17), channel_id=1, source_target_pairs={{0,31},{1,0},{2,1},{3,2},{4,3},{5,4},{6,5},{7,6},{8,7},{9,8},{10,9... | collective-permute-start | bytes 147464 | tf_op jit(solution)/shard_map/ppermute | solution.py:355
  26.4 1.1 %copy-start.1 = (f32[3,32,8,256]{3,2,1,0:T(8,128)S(1)}, f32[3,32,8,256]{3,2,1,0:T(8,128)}, u32[]{:S(2)}) copy-start(f32[3,32,8,256]{3,2,1,0:T(8,128)} %refs_1_.1) | copy-start | bytes 2359300
  27.6 22.9 %copy-start.3 = (bf16[32,8,128]{2,1,0:T(8,128)(2,1)}, bf16[32,8,128]{2,1,0:T(8,128)(2,1)S(1)}, u32[]{:S(2)}) copy-start(bf16[32,8,128]{2,1,0:T(8,128)(2,1)S(1)} %all-to-all-done.arrived.refs_0_) | copy-start | bytes 196612
  29.7 24.2 %copy-start.4 = (bf16[3,32,256]{2,1,0:T(8,128)(2,1)}, bf16[3,32,256]{2,1,0:T(8,128)(2,1)S(1)}, u32[]{:S(2)}) copy-start(bf16[3,32,256]{2,1,0:T(8,128)(2,1)S(1)} %collective-permute-done.x_before.refs_4_) | copy-start | bytes 147460
  29.7 24.2 %copy-start.5 = (bf16[3,32,256]{2,1,0:T(8,128)(2,1)}, bf16[3,32,256]{2,1,0:T(8,128)(2,1)S(1)}, u32[]{:S(2)}) copy-start(bf16[3,32,256]{2,1,0:T(8,128)(2,1)S(1)} %collective-permute-done.1.x_after.refs_5_) | copy-start | bytes 147460
  30.4 19.1 %all-to-all-start.1 = ((bf16[16,40,128]{2,1,0:T(8,128)(2,1)}), bf16[16,40,128]{2,1,0:T(8,128)(2,1)S(1)}, u32[]{:S(2)}, u32[]{:S(2)}) async-start(bf16[16,40,128]{2,1,0:T(8,128)(2,1)} %complete_source.1.refs_2_), calls=%async_computation.1 | async-start | bytes 327680 | tf_op jit(solution)/shard_map/all_to_all | solution.py:389
  39.5 2.7 %collective-permute-start.2 = (bf16[3,8,256]{2,1,0:T(8,128)(2,1)}, bf16[3,8,256]{2,1,0:T(8,128)(2,1)S(1)}, u32[]{:S(2)}, u32[]{:S(2)}) collective-permute-start(bf16[3,8,256]{2,1,0:T(8,128)(2,1)} %get-tuple-element.18), channel_id=1, source_target_pairs={{0,32},{32,64},{64,96},{96,128},{128,160},{160,192},{192,224},{224... | collective-permute-start | bytes 36872 | tf_op jit(solution)/shard_map/ppermute | solution.py:392
  41.1 4.8 %collective-permute-start.3 = (bf16[3,8,256]{2,1,0:T(8,128)(2,1)}, bf16[3,8,256]{2,1,0:T(8,128)(2,1)S(1)}, u32[]{:S(2)}, u32[]{:S(2)}) collective-permute-start(bf16[3,8,256]{2,1,0:T(8,128)(2,1)} %get-tuple-element.19), channel_id=1, source_target_pairs={{0,480},{32,0},{64,32},{96,64},{128,96},{160,128},{192,160},{224,1... | collective-permute-start | bytes 36872 | tf_op jit(solution)/shard_map/ppermute | solution.py:393
  42.2 11.7 %copy-start.6 = (bf16[3,8,256]{2,1,0:T(8,128)(2,1)}, bf16[3,8,256]{2,1,0:T(8,128)(2,1)S(1)}, u32[]{:S(2)}) copy-start(bf16[3,8,256]{2,1,0:T(8,128)(2,1)S(1)} %collective-permute-done.2.refs_2_.before) | copy-start | bytes 36868
  46.0 8.0 %copy-start.7 = (bf16[3,8,256]{2,1,0:T(8,128)(2,1)}, bf16[3,8,256]{2,1,0:T(8,128)(2,1)S(1)}, u32[]{:S(2)}) copy-start(bf16[3,8,256]{2,1,0:T(8,128)(2,1)S(1)} %collective-permute-done.3.refs_3_.after) | copy-start | bytes 36868
  50.5 11.6 %all-to-all-start.2 = ((bf16[16,32,128]{2,1,0:T(8,128)(2,1)}), bf16[16,32,128]{2,1,0:T(8,128)(2,1)S(1)}, u32[]{:S(2)}, u32[]{:S(2)}) async-start(bf16[16,32,128]{2,1,0:T(8,128)(2,1)} %bitcast.5), calls=%async_computation.2 | async-start | bytes 262144 | tf_op jit(solution)/shard_map/all_to_all | solution.py:425
  53.9 8.2 %copy-start = (bf16[16,256,256]{2,1,0:T(8,128)(2,1)S(1)}, bf16[16,256,256]{2,1,0:T(8,128)(2,1)}, u32[]{:S(2)}) copy-start(bf16[16,256,256]{2,1,0:T(8,128)(2,1)} %inverse.1) | copy-start | bytes 6291460

commit v4 on v3

--- a/solution.py
+++ b/solution.py
@@ -35,13 +35,17 @@
     )(*operands)
 
 
-def take_rows(table, row, lane, shape):
-    found = jnp.zeros(shape, table.dtype)
-    for r in range(table.shape[0]):
-        line = jnp.broadcast_to(table[r : r + 1, :], shape)
-        picked = jnp.take_along_axis(line, lane, axis=1, mode="promise_in_bounds")
-        found = jnp.where(row == r, picked, found)
-    return found
+def take_rows(table, row, lane):
+    blocks = []
+    for first in range(0, row.shape[0], ROWS):
+        span = slice(first, first + ROWS)
+        found = None
+        for r in range(table.shape[0]):
+            line = jnp.broadcast_to(table[r : r + 1, :], (ROWS, LANES))
+            picked = jnp.take_along_axis(line, lane[span], axis=1, mode="promise_in_bounds")
+            found = picked if found is None else jnp.where(row[span] == r, picked, found)
+        blocks.append(found)
+    return jnp.concatenate(blocks, axis=0)
 
 
 def pack_body(*refs):
@@ -84,12 +88,12 @@
     slot = lax.broadcasted_iota(jnp.int32, shape, 1)
     used = slot < count
     place = jnp.minimum(start + slot, lines * LANES - 1)
-    bubble = take_rows(listed, place >> 7, place & 127, shape)
+    bubble = take_rows(listed, place >> 7, place & 127)
     row, column = bubble >> 7, bubble & 127
     for k in range(4):
-        value = take_rows(payload.at[k], row, column, shape)
+        value = take_rows(payload.at[k], row, column)
         staged[:, k, :] = jnp.where(used, value, 0.0)
-    cell = take_rows(payload.at[4], row, column, shape).astype(jnp.int32)
+    cell = take_rows(payload.at[4], row, column).astype(jnp.int32)
     cell = jnp.where(used, cell, 0)
     staged[:, 4, :] = (cell >> 8).astype(jnp.float32)
     staged[:, 5, :] = (cell & 255).astype(jnp.float32)
@@ -136,30 +140,43 @@
     return row == jnp.broadcast_to(index_line, (cells, LANES))
 
 
-def hot_parts(arrived, first, count, across, along):
-    cells = across.shape[0]
+def hot_rows(arrived, holders, cells):
     zero = jnp.zeros((cells, LANES), jnp.bfloat16)
-    for h in range(arrived.shape[0]):
-        span = slice(h * LANES, (h + 1) * LANES)
-        block = arrived[h]
-        across[:, span] = jnp.where(cell_hot(block[4:5, :], cells), jnp.ones_like(zero), zero)
-        here = cell_hot(block[5:6, :], cells)
-        for k in range(count):
-            value = jnp.broadcast_to(block[first + k : first + k + 1, :], zero.shape)
-            along[k, :, span] = jnp.where(here, value, zero)
-
-
-def deposit(across, along):
+    parts = [
+        jnp.where(cell_hot(arrived[h][4:5, :], cells), jnp.ones_like(zero), zero) for h in holders
+    ]
+    return jnp.concatenate(parts, axis=1)
+
+
+def hot_columns(arrived, holders, cells, component):
+    zero = jnp.zeros((cells, LANES), jnp.bfloat16)
+    parts = []
+    for h in holders:
+        value = jnp.broadcast_to(arrived[h][component : component + 1, :], zero.shape)
+        parts.append(jnp.where(cell_hot(arrived[h][5:6, :], cells), value, zero))
+    return jnp.concatenate(parts, axis=1)
+
+
+def deposit(rows, columns):
     return lax.dot_general(
-        across, along, (((1,), (1,)), ((), ())), preferred_element_type=jnp.float32
-    )
-
-
-def partial_body(
-    arrived, velocity, out, edges, across, along, total, whole
-):
-    hot_parts(arrived, 3, 1, across, along)
-    density = deposit(across[...], along[0])
+        rows, columns, (((1,), (1,)), ((), ())), preferred_element_type=jnp.float32
+    )
+
+
+def density_body(arrived, out):
+    step = 4
+    total = None
+    for first in range(0, arrived.shape[0], step):
+        holders = range(first, first + step)
+        part = deposit(
+            hot_rows(arrived, holders, out.shape[0]),
+            hot_columns(arrived, holders, out.shape[1], 3),
+        )
+        total = part if total is None else total + part
+    out[...] = total
+
+
+def source_body(density, velocity, x_before, x_after, out, total, whole):
     th, width = velocity.shape[1], velocity.shape[3]
     radius = lax.broadcasted_iota(jnp.int32, (ROWS, width), 1).astype(jnp.float32)
     outward = (radius + 1.0) / (2.0 * radius + 1.0)
@@ -172,54 +189,29 @@
         if t > 0:
             around = around - velocity[1, t - 1]
         outer, inner = radial_neighbours(velocity[2, t])
-        total[t * ROWS : (t + 1) * ROWS, :] = 0.5 * around + (outward * outer - inward * inner)
+        span = slice(t * ROWS, (t + 1) * ROWS)
+        total[span, :] = 0.5 * around + (outward * outer - inward * inner) + density[span, :]
     halves = whole.shape[0]
     blank = jnp.zeros((out.shape[1] - th - 2, LANES), jnp.float32)
     first = velocity[1, 0]
     last = velocity[1, th - 1]
     for half in range(halves):
         span = slice(half * LANES, (half + 1) * LANES)
-        whole[half] = density[:, span] + total[:, span]
+        whole[half] = total[:, span]
         for x in range(ROWS):
             layer = whole[half, pl.ds(x, th, stride=ROWS), :]
+            if x == 0:
+                layer = layer - 0.5 * x_before[0, :, span].astype(jnp.float32)
+            if x == ROWS - 1:
+                layer = layer + 0.5 * x_after[0, :, span].astype(jnp.float32)
             ends = [first[x : x + 1, span], last[x : x + 1, span], blank]
             column = jnp.concatenate([layer] + ends, axis=0)
             out[x * halves + half] = column.astype(jnp.bfloat16)
-            if x == 0:
-                edges[half] = column
-            if x == ROWS - 1:
-                edges[halves + half] = column
-
-
-def complete_body(_, edges, x_before, x_after, out, staged, sems):
-    groups, th = out.shape[0], x_before.shape[1]
-    halves = edges.shape[0] // 2
-    for half in range(halves):
-        span = slice(half * LANES, (half + 1) * LANES)
-        before = 0.5 * x_before[0, :, span].astype(jnp.float32)
-        beyond = 0.5 * x_after[0, :, span].astype(jnp.float32)
-        blank = jnp.zeros((edges.shape[1] - th, LANES), jnp.float32)
-        low = edges[half] - jnp.concatenate([before, blank], axis=0)
-        high = edges[halves + half] + jnp.concatenate([beyond, blank], axis=0)
-        staged[half] = low.astype(jnp.bfloat16)
-        staged[halves + half] = high.astype(jnp.bfloat16)
-    copies = [
-        pltpu.make_async_copy(
-            staged.at[pl.ds(i * halves, halves)],
-            out.at[pl.ds(i * (groups - halves), halves)],
-            sems.at[i],
-        )
-        for i in range(2)
-    ]
-    for copy in copies:
-        copy.start()
-    for copy in copies:
-        copy.wait()
 
 
 def predictor_body(*refs):
     hbm, out, held = refs[:6], refs[6], refs[7:13]
-    across, along, low, high, density, sems = refs[13:]
+    across, low, high, density, sems = refs[13:]
     arrived, velocity, theta_before, theta_after, x_before, x_after = held
     copies = [
         pltpu.make_async_copy(source, target, sems.at[i])
@@ -229,7 +221,12 @@
         copy.start()
     copies[0].wait()
     th, width = velocity.shape[1], velocity.shape[3]
-    hot_parts(arrived, 0, 3, across, along)
+    step = 4
+    starts = range(0, arrived.shape[0], step)
+    cells = density.shape[1]
+    for start in starts:
+        span = slice(start * LANES, (start + step) * LANES)
+        across[:, span] = hot_rows(arrived, range(start, start + step), cells)
     for copy in copies[1:]:
         copy.wait()
     radius = lax.broadcasted_iota(jnp.int32, (ROWS, width), 1).astype(jnp.float32)
@@ -238,7 +235,13 @@
     low[...] = x_before[...].astype(jnp.float32)
     high[...] = x_after[...].astype(jnp.float32)
     for c in range(3):
-        density[...] = deposit(across[...], along[c])
+        total = None
+        for start in starts:
+            span = slice(start * LANES, (start + step) * LANES)
+            columns = hot_columns(arrived, range(start, start + step), width, c)
+            part = deposit(across[:, span], columns)
+            total = part if total is None else total + part
+        density[c] = total
         for t in range(th):
             v = velocity[c, t]
             ahead, behind = axial_neighbours(v, low[c, t : t + 1, :], high[c, t : t + 1, :])
@@ -249,16 +252,33 @@
             out[c, t] = (
                 (1.0 - 6.0 * DIFFUSE) * v
                 + DIFFUSE * around
-                + density[t * ROWS : (t + 1) * ROWS, :]
+                + density[c, t * ROWS : (t + 1) * ROWS, :]
             )
 
 
-def transform_body(table, source, before, after, out):
-    product = jnp.dot(table[...], source[...], preferred_element_type=jnp.float32)
-    out[...] = product.astype(jnp.bfloat16)
-
-
-def solve_body(spread, inverse, out, whole):
+def in_parts(out, staged, sems, make):
+    parts = sems.shape[0]
+    rows = out.shape[0] // parts
+    copies = []
+    for i in range(parts):
+        span = pl.ds(i * rows, rows)
+        make(i * rows, rows)
+        copies.append(pltpu.make_async_copy(staged.at[span], out.at[span], sems.at[i]))
+        copies[-1].start()
+    for copy in copies:
+        copy.wait()
+
+
+def transform_body(table, source, before, after, out, staged, sems):
+    def make(first, rows):
+        span = slice(first, first + rows)
+        product = jnp.dot(table[span, :], source[...], preferred_element_type=jnp.float32)
+        staged[span, :] = product.astype(jnp.bfloat16)
+
+    in_parts(out, staged, sems, make)
+
+
+def solve_body(spread, inverse, out, whole, staged, sems):
     rows = spread.shape[1]
     halves = whole.shape[0]
     for x in range(ROWS):
@@ -266,15 +286,19 @@
             layer = spread[x * halves + half].astype(jnp.float32)
             whole[half, pl.ds(x, rows, stride=ROWS), :] = layer
     group = 2 * ROWS
-    for j in range(inverse.shape[0]):
-        span = slice(j * group, (j + 1) * group)
-        pair = jnp.concatenate([whole[half, span, :] for half in range(halves)], axis=1)
-        out[span, :] = lax.dot_general(
-            pair.astype(jnp.bfloat16),
-            inverse[j],
-            (((1,), (1,)), ((), ())),
-            preferred_element_type=jnp.float32,
-        )
+
+    def make(first, rows):
+        for j in range(first // group, (first + rows) // group):
+            span = slice(j * group, (j + 1) * group)
+            pair = jnp.concatenate([whole[half, span, :] for half in range(halves)], axis=1)
+            staged[span, :] = lax.dot_general(
+                pair.astype(jnp.bfloat16),
+                inverse[j],
+                (((1,), (1,)), ((), ())),
+                preferred_element_type=jnp.float32,
+            )
+
+    in_parts(out, staged, sems, make)
 
 
 def spectral_table(length, blocks, extra):
@@ -357,34 +381,20 @@
     cells = th * ax
     extra = 8
     halves = width // LANES
-    partial, edges = call(
-        partial_body,
-        "partial_source",
-        (
-            struct((groups, th + extra, LANES), bf16),
-            struct((2 * halves, th + extra, LANES), f32),
-        ),
-        (arrived, velocity),
-        scratch=(
-            pltpu.VMEM((cells, slots), bf16),
-            pltpu.VMEM((1, width, slots), bf16),
-            pltpu.VMEM((cells, width), f32),
-            pltpu.VMEM((halves, cells, LANES), f32),
-        ),
+    density = call(
+        density_body,
+        "density",
+        struct((cells, width), f32),
+        (arrived,),
         flops=2 * cells * slots * width,
     )
     source = call(
-        complete_body,
-        "complete_source",
-        struct(partial.shape, bf16),
-        (partial, edges, x_before, x_after),
-        specs=[ANY, VMEM, VMEM, VMEM],
-        out_specs=ANY,
-        aliases={0: 0},
-        scratch=(
-            pltpu.VMEM((2 * halves, th + extra, LANES), bf16),
-            pltpu.SemaphoreType.DMA((2,)),
-        ),
+        source_body,
+        "source",
+        struct((groups, th + extra, LANES), bf16),
+        (density, velocity, x_before, x_after),
+        scratch=(pltpu.VMEM((cells, width), f32), pltpu.VMEM((halves, cells, LANES), f32)),
+        flops=30 * cells * width,
     )
     gathered = lax.all_to_all(source, "az", split_axis=0, concat_axis=0, tiled=True)
 
@@ -402,10 +412,9 @@
         scratch=tuple(pltpu.VMEM(x.shape, x.dtype) for x in beside)
         + (
             pltpu.VMEM((cells, slots), bf16),
-            pltpu.VMEM((3, width, slots), bf16),
             pltpu.VMEM((3, th, width), f32),
             pltpu.VMEM((3, th, width), f32),
-            pltpu.VMEM((cells, width), f32),
+            pltpu.VMEM((3, cells, width), f32),
             pltpu.SemaphoreType.DMA((6,)),
         ),
         flops=2 * 3 * cells * slots * width,
@@ -420,6 +429,8 @@
         struct((length, LANES), bf16),
         (table, gathered.reshape(-1, LANES), theta_before, theta_after),
         specs=[VMEM, VMEM, ANY, ANY],
+        out_specs=ANY,
+        scratch=(pltpu.VMEM((length, LANES), bf16), pltpu.SemaphoreType.DMA((2,))),
         flops=2 * length * (length + groups * extra) * LANES,
     )
     spread = lax.all_to_all(
@@ -430,7 +441,12 @@
         "solve",
         struct((th * ax, width), f32),
         (spread, radial_inverse),
-        scratch=(pltpu.VMEM((width // LANES, th * ax, LANES), f32),),
+        out_specs=ANY,
+        scratch=(
+            pltpu.VMEM((halves, cells, LANES), f32),
+            pltpu.VMEM((cells, width), f32),
+            pltpu.SemaphoreType.DMA((4,)),
+        ),
         flops=2 * th * ax * width * width,
     )
     return predicted, modes.reshape(th, ax, width)

time: 63.9 us -> 61.6 us (0.964)
  Pallas kernels: 14.2 us -> 10.6 us
  waiting for transfers between devices: 10.8 us -> 13 us
  local copies, waits for them, and re-layouts: 1.17 us -> 0.04 us
    pallas_call x6, Pallas kernels: 14.2 us -> 10.6 us  [call(): pl.pallas_call(body, name=name, out_shape=out_shape, in_specs=[VMEM] * le...]
    all_to_all x1, waiting for transfers between devices: 2.13 us -> 3.97 us  [on_device(): lax.all_to_all(coefficients.reshape(groups, th, LANES), 'az', split_axis=...]
    unnamed x16, local copies, waits for them, and re-layouts: 1.17 us -> 0.04 us
  transfers between devices with their start and end apart: 7 -> 7, of which waited for: 5 -> 6; matrix products, arithmetic and copies ran while one was open for 0% -> 0% of each run, Pallas kernels for 13% -> 8%
where the time goes in v4:
time: 61.6 us; the launch traced here: 61.1 us
  starting transfers between devices  36.7 us (60%)
  waiting for transfers between devices  13 us (21%)
  Pallas kernels  10.6 us (17%)
  between operations  0.79 us (1%)
    all_to_all x1, starting transfers between devices, on_device(): lax.all_to_all(packed, 'ax', split_axis=0, concat_axis=0, tiled=True)  13.9 us
    pallas_call x6, Pallas kernels, call(): pl.pallas_call(body, name=name, out_shape=out_shape, in_specs=[VMEM] * le...  10.6 us
    all_to_all x1, starting transfers between devices, on_device(): lax.all_to_all(source, 'az', split_axis=0, concat_axis=0, tiled=True)  9.2 us
    ppermute x1, starting transfers between devices, on_device(): x_after = lax.ppermute(first_x, 'ax', ring('ax', -1))  5.46 us
    all_to_all x1, waiting for transfers between devices, on_device(): lax.all_to_all(coefficients.reshape(groups, th, LANES), 'az', split_axis=...  3.97 us
    ppermute x1, waiting for transfers between devices, on_device(): theta_after = lax.ppermute(first_layer, 'az', ring('az', -1))  3.78 us
    all_to_all x1, waiting for transfers between devices, on_device(): lax.all_to_all(source, 'az', split_axis=0, concat_axis=0, tiled=True)  3.5 us
    all_to_all x1, starting transfers between devices, on_device(): lax.all_to_all(coefficients.reshape(groups, th, LANES), 'az', split_axis=...  3.42 us
  transfers between devices with their start and end apart: 7, of which 6 were waited for; matrix products, arithmetic and copies ran while one was open for 0% of the time, Pallas kernels for 8%

profile of v4, /device:TPU:1, one launch (start us, length us, event | category | flops | bytes accessed | tf_op | source)
XLA Modules:
  0.0 61.1 jit_solution(16386452655230445821)
XLA Ops:
  0.6 0.0 copy-start
  0.6 2.5 %pack_bubbles.1 = (bf16[32,8,128]{2,1,0:T(8,128)(2,1)}, bf16[3,32,256]{2,1,0:T(8,128)(2,1)}, bf16[3,32,256]{2,1,0:T(8,128)(2,1)}, bf16[3,8,256]{2,1,0:T(8,128)(2,1)}, bf16[3,8,256]{2,1,0:T(8,128)(2,1)}) custom-call(f32[3,2048]{1,0:T(4,128)} %refs_0_.1, f32[16,128]{1,0:T(8,128)} %bitcast.9, f32[16,128]{1,0:T(8,128)} %bitcast.10, s32[16,128]{1,0:T(8,128)} %bitcast.11, ...), custom_call_target="tpu_custom_call" | custom-call | bytes 852096 | tf_op jit(solution)/shard_map/pack_bubbles/pallas_call | solution.py:25
  3.1 0.0 copy-start.2
  3.1 13.9 %all-to-all-start = ((bf16[32,8,128]{2,1,0:T(8,128)(2,1)}), bf16[32,8,128]{2,1,0:T(8,128)(2,1)S(1)}, u32[]{:S(2)}, u32[]{:S(2)}) async-start(bf16[32,8,128]{2,1,0:T(8,128)(2,1)} %get-tuple-element.9), calls=%async_computation | async-start | bytes 131072 | tf_op jit(solution)/shard_map/all_to_all | solution.py:376
  17.0 3.1 %collective-permute-start = (bf16[3,32,256]{2,1,0:T(8,128)(2,1)}, bf16[3,32,256]{2,1,0:T(8,128)(2,1)S(1)}, u32[]{:S(2)}, u32[]{:S(2)}) collective-permute-start(bf16[3,32,256]{2,1,0:T(8,128)(2,1)} %get-tuple-element.12), channel_id=1, source_target_pairs={{0,1},{1,2},{2,3},{3,4},{4,5},{5,6},{6,7},{7,8},{8,9},{9,10},{10,1... | collective-permute-start | bytes 147464 | tf_op jit(solution)/shard_map/ppermute | solution.py:378
  20.1 5.5 %collective-permute-start.1 = (bf16[3,32,256]{2,1,0:T(8,128)(2,1)}, bf16[3,32,256]{2,1,0:T(8,128)(2,1)S(1)}, u32[]{:S(2)}, u32[]{:S(2)}) collective-permute-start(bf16[3,32,256]{2,1,0:T(8,128)(2,1)} %get-tuple-element.13), channel_id=1, source_target_pairs={{0,31},{1,0},{2,1},{3,2},{4,3},{5,4},{6,5},{7,6},{8,7},{9,8},{10,9... | collective-permute-start | bytes 147464 | tf_op jit(solution)/shard_map/ppermute | solution.py:379
  25.6 0.3 all-to-all-done.arrived.refs_0_
  26.0 0.7 %density.1 = f32[256,256]{1,0:T(8,128)S(1)} custom-call(bf16[32,8,128]{2,1,0:T(8,128)(2,1)S(1)} %all-to-all-done.arrived.refs_0_), custom_call_target="tpu_custom_call" | custom-call | flops 536870912 | bytes 65536 | tf_op jit(solution)/shard_map/density/pallas_call | solution.py:25
  26.7 0.0 collective-permute-done.x_before.refs_4_
  26.7 0.0 copy-start.4
  26.7 0.4 collective-permute-done.1.x_after.refs_5_
  27.1 0.9 %source.1.refs_2_ = bf16[16,40,128]{2,1,0:T(8,128)(2,1)} custom-call(f32[256,256]{1,0:T(8,128)S(1)} %density.1, f32[3,32,8,256]{3,2,1,0:T(8,128)S(1)} %copy-done, bf16[3,32,256]{2,1,0:T(8,128)(2,1)S(1)} %collective-permute-done.x_before.refs_4_, bf16[3,32,256]{2,1,0:T(8,128)(2,1)S(1)} %collective-permute-done.1.x_after.refs_5_), custom_call_target="tpu_custom_call" | custom-call | flops 1966080 | bytes 1146880 | tf_op jit(solution)/shard_map/source/pallas_call | solution.py:25
  28.0 9.2 %all-to-all-start.1 = ((bf16[16,40,128]{2,1,0:T(8,128)(2,1)}), bf16[16,40,128]{2,1,0:T(8,128)(2,1)S(1)}, u32[]{:S(2)}, u32[]{:S(2)}) async-start(bf16[16,40,128]{2,1,0:T(8,128)(2,1)} %source.1.refs_2_), calls=%async_computation.1 | async-start | bytes 327680 | tf_op jit(solution)/shard_map/all_to_all | solution.py:399
  37.2 1.6 %collective-permute-start.2 = (bf16[3,8,256]{2,1,0:T(8,128)(2,1)}, bf16[3,8,256]{2,1,0:T(8,128)(2,1)S(1)}, u32[]{:S(2)}, u32[]{:S(2)}) collective-permute-start(bf16[3,8,256]{2,1,0:T(8,128)(2,1)} %get-tuple-element.14), channel_id=1, source_target_pairs={{0,32},{32,64},{64,96},{96,128},{128,160},{160,192},{192,224},{224... | collective-permute-start | bytes 36872 | tf_op jit(solution)/shard_map/ppermute | solution.py:402
  38.8 0.0 collective-permute-start.3
  38.8 1.0 %collective-permute-done.2.refs_2_.before = bf16[3,8,256]{2,1,0:T(8,128)(2,1)S(1)} collective-permute-done((bf16[3,8,256]{2,1,0:T(8,128)(2,1)}, bf16[3,8,256]{2,1,0:T(8,128)(2,1)S(1)}, u32[]{:S(2)}, u32[]{:S(2)}) %collective-permute-start.2) | collective-permute-done | bytes 12320 | tf_op jit(solution)/shard_map/ppermute | solution.py:402
  39.9 3.8 %collective-permute-done.3.refs_3_.after = bf16[3,8,256]{2,1,0:T(8,128)(2,1)S(1)} collective-permute-done((bf16[3,8,256]{2,1,0:T(8,128)(2,1)}, bf16[3,8,256]{2,1,0:T(8,128)(2,1)S(1)}, u32[]{:S(2)}, u32[]{:S(2)}) %collective-permute-start.3) | collective-permute-done | bytes 12320 | tf_op jit(solution)/shard_map/ppermute | solution.py:403
  43.7 3.5 %all-to-all-done.1 = bf16[16,40,128]{2,1,0:T(8,128)(2,1)S(1)} async-done(((bf16[16,40,128]{2,1,0:T(8,128)(2,1)}), bf16[16,40,128]{2,1,0:T(8,128)(2,1)S(1)}, u32[]{:S(2)}, u32[]{:S(2)}) %all-to-all-start.1) | async-done | bytes 163872 | tf_op jit(solution)/shard_map/all_to_all | solution.py:399
  47.2 1.0 %transform.1 = bf16[512,128]{1,0:T(8,128)(2,1)} custom-call(bf16[512,640]{1,0:T(8,128)(2,1)S(1)} %copy-done.2, bf16[640,128]{1,0:T(8,128)(2,1)S(1)} %bitcast.7, bf16[3,8,256]{2,1,0:T(8,128)(2,1)S(1)} %collective-permute-done.2.refs_2_.before, bf16[3,8,256]{2,1,0:T(8,128)(2,1)S(1)} %collective-permute-done.3.refs_3_.after), custom_call_target="tpu_custom_call" | custom-call | flops 83886080 | bytes 843776 | tf_op jit(solution)/shard_map/transform/pallas_call | solution.py:25
  48.2 3.4 %all-to-all-start.2 = ((bf16[16,32,128]{2,1,0:T(8,128)(2,1)}), bf16[16,32,128]{2,1,0:T(8,128)(2,1)S(1)}, u32[]{:S(2)}, u32[]{:S(2)}) async-start(bf16[16,32,128]{2,1,0:T(8,128)(2,1)} %bitcast.5), calls=%async_computation.2 | async-start | bytes 262144 | tf_op jit(solution)/shard_map/all_to_all | solution.py:436
  51.6 0.0 copy-start.1
  51.6 4.2 %predictor.1 = f32[3,32,8,256]{3,2,1,0:T(8,128)} custom-call(bf16[32,8,128]{2,1,0:T(8,128)(2,1)} %copy-done.3, f32[3,32,8,256]{3,2,1,0:T(8,128)} %refs_1_.1, bf16[3,8,256]{2,1,0:T(8,128)(2,1)} %copy-done.6, bf16[3,8,256]{2,1,0:T(8,128)(2,1)} %copy-done.7, bf16[3,32,256]{2,1,0:T(8,128)(2,1)} %copy-done.4, bf16[3,32,256]{2,1,0:T(8,128)(2,1)} %copy-done.5), custom_call_target="tpu_custom_call" | custom-call | flops 1610612736 | bytes 974848 | tf_op jit(solution)/shard_map/predictor/pallas_call | solution.py:25
  55.8 4.0 %all-to-all-done.2.spread = bf16[16,32,128]{2,1,0:T(8,128)(2,1)S(1)} async-done(((bf16[16,32,128]{2,1,0:T(8,128)(2,1)}), bf16[16,32,128]{2,1,0:T(8,128)(2,1)S(1)}, u32[]{:S(2)}, u32[]{:S(2)}) %all-to-all-start.2) | async-done | bytes 131104 | tf_op jit(solution)/shard_map/all_to_all | solution.py:436
  59.8 1.3 %solve.1 = f32[256,256]{1,0:T(8,128)} custom-call(bf16[16,32,128]{2,1,0:T(8,128)(2,1)S(1)} %all-to-all-done.2.spread, bf16[16,256,256]{2,1,0:T(8,128)(2,1)S(1)} %copy-done.1), custom_call_target="tpu_custom_call" | custom-call | flops 33554432 | bytes 2228224 | tf_op jit(solution)/shard_map/solve/pallas_call | solution.py:25
  (13 shorter events, 0.0 us)
Async XLA Ops:
  0.6 26.5 %copy-start = (f32[3,32,8,256]{3,2,1,0:T(8,128)S(1)}, f32[3,32,8,256]{3,2,1,0:T(8,128)}, u32[]{:S(2)}) copy-start(f32[3,32,8,256]{3,2,1,0:T(8,128)} %refs_1_.1) | copy-start | bytes 2359300
  3.1 44.1 %copy-start.2 = (bf16[512,640]{1,0:T(8,128)(2,1)S(1)}, bf16[512,640]{1,0:T(8,128)(2,1)}, u32[]{:S(2)}) copy-start(bf16[512,640]{1,0:T(8,128)(2,1)} %constant.2.clone.table) | copy-start | bytes 1966084
  3.1 22.8 %all-to-all-start = ((bf16[32,8,128]{2,1,0:T(8,128)(2,1)}), bf16[32,8,128]{2,1,0:T(8,128)(2,1)S(1)}, u32[]{:S(2)}, u32[]{:S(2)}) async-start(bf16[32,8,128]{2,1,0:T(8,128)(2,1)} %get-tuple-element.9), calls=%async_computation | async-start | bytes 131072 | tf_op jit(solution)/shard_map/all_to_all | solution.py:376
  17.0 9.7 %collective-permute-start = (bf16[3,32,256]{2,1,0:T(8,128)(2,1)}, bf16[3,32,256]{2,1,0:T(8,128)(2,1)S(1)}, u32[]{:S(2)}, u32[]{:S(2)}) collective-permute-start(bf16[3,32,256]{2,1,0:T(8,128)(2,1)} %get-tuple-element.12), channel_id=1, source_target_pairs={{0,1},{1,2},{2,3},{3,4},{4,5},{5,6},{6,7},{7,8},{8,9},{9,10},{10,1... | collective-permute-start | bytes 147464 | tf_op jit(solution)/shard_map/ppermute | solution.py:378
  20.1 6.9 %collective-permute-start.1 = (bf16[3,32,256]{2,1,0:T(8,128)(2,1)}, bf16[3,32,256]{2,1,0:T(8,128)(2,1)S(1)}, u32[]{:S(2)}, u32[]{:S(2)}) collective-permute-start(bf16[3,32,256]{2,1,0:T(8,128)(2,1)} %get-tuple-element.13), channel_id=1, source_target_pairs={{0,31},{1,0},{2,1},{3,2},{4,3},{5,4},{6,5},{7,6},{8,7},{9,8},{10,9... | collective-permute-start | bytes 147464 | tf_op jit(solution)/shard_map/ppermute | solution.py:379
  26.0 22.2 %copy-start.3 = (bf16[32,8,128]{2,1,0:T(8,128)(2,1)}, bf16[32,8,128]{2,1,0:T(8,128)(2,1)S(1)}, u32[]{:S(2)}) copy-start(bf16[32,8,128]{2,1,0:T(8,128)(2,1)S(1)} %all-to-all-done.arrived.refs_0_) | copy-start | bytes 196612
  26.7 24.9 %copy-start.4 = (bf16[3,32,256]{2,1,0:T(8,128)(2,1)}, bf16[3,32,256]{2,1,0:T(8,128)(2,1)S(1)}, u32[]{:S(2)}) copy-start(bf16[3,32,256]{2,1,0:T(8,128)(2,1)S(1)} %collective-permute-done.x_before.refs_4_) | copy-start | bytes 147460
  27.1 24.5 %copy-start.5 = (bf16[3,32,256]{2,1,0:T(8,128)(2,1)}, bf16[3,32,256]{2,1,0:T(8,128)(2,1)S(1)}, u32[]{:S(2)}) copy-start(bf16[3,32,256]{2,1,0:T(8,128)(2,1)S(1)} %collective-permute-done.1.x_after.refs_5_) | copy-start | bytes 147460
  28.0 19.2 %all-to-all-start.1 = ((bf16[16,40,128]{2,1,0:T(8,128)(2,1)}), bf16[16,40,128]{2,1,0:T(8,128)(2,1)S(1)}, u32[]{:S(2)}, u32[]{:S(2)}) async-start(bf16[16,40,128]{2,1,0:T(8,128)(2,1)} %source.1.refs_2_), calls=%async_computation.1 | async-start | bytes 327680 | tf_op jit(solution)/shard_map/all_to_all | solution.py:399
  37.2 2.7 %collective-permute-start.2 = (bf16[3,8,256]{2,1,0:T(8,128)(2,1)}, bf16[3,8,256]{2,1,0:T(8,128)(2,1)S(1)}, u32[]{:S(2)}, u32[]{:S(2)}) collective-permute-start(bf16[3,8,256]{2,1,0:T(8,128)(2,1)} %get-tuple-element.14), channel_id=1, source_target_pairs={{0,32},{32,64},{64,96},{96,128},{128,160},{160,192},{192,224},{224... | collective-permute-start | bytes 36872 | tf_op jit(solution)/shard_map/ppermute | solution.py:402
  38.8 4.8 %collective-permute-start.3 = (bf16[3,8,256]{2,1,0:T(8,128)(2,1)}, bf16[3,8,256]{2,1,0:T(8,128)(2,1)S(1)}, u32[]{:S(2)}, u32[]{:S(2)}) collective-permute-start(bf16[3,8,256]{2,1,0:T(8,128)(2,1)} %get-tuple-element.15), channel_id=1, source_target_pairs={{0,480},{32,0},{64,32},{96,64},{128,96},{160,128},{192,160},{224,1... | collective-permute-start | bytes 36872 | tf_op jit(solution)/shard_map/ppermute | solution.py:403
  39.9 11.7 %copy-start.6 = (bf16[3,8,256]{2,1,0:T(8,128)(2,1)}, bf16[3,8,256]{2,1,0:T(8,128)(2,1)S(1)}, u32[]{:S(2)}) copy-start(bf16[3,8,256]{2,1,0:T(8,128)(2,1)S(1)} %collective-permute-done.2.refs_2_.before) | copy-start | bytes 36868
  43.7 8.0 %copy-start.7 = (bf16[3,8,256]{2,1,0:T(8,128)(2,1)}, bf16[3,8,256]{2,1,0:T(8,128)(2,1)S(1)}, u32[]{:S(2)}) copy-start(bf16[3,8,256]{2,1,0:T(8,128)(2,1)S(1)} %collective-permute-done.3.refs_3_.after) | copy-start | bytes 36868
  48.2 11.6 %all-to-all-start.2 = ((bf16[16,32,128]{2,1,0:T(8,128)(2,1)}), bf16[16,32,128]{2,1,0:T(8,128)(2,1)S(1)}, u32[]{:S(2)}, u32[]{:S(2)}) async-start(bf16[16,32,128]{2,1,0:T(8,128)(2,1)} %bitcast.5), calls=%async_computation.2 | async-start | bytes 262144 | tf_op jit(solution)/shard_map/all_to_all | solution.py:436
  51.6 8.2 %copy-start.1 = (bf16[16,256,256]{2,1,0:T(8,128)(2,1)S(1)}, bf16[16,256,256]{2,1,0:T(8,128)(2,1)}, u32[]{:S(2)}) copy-start(bf16[16,256,256]{2,1,0:T(8,128)(2,1)} %inverse.1) | copy-start | bytes 6291460

commit v5 on v4

--- a/solution.py
+++ b/solution.py
@@ -176,7 +176,7 @@
     out[...] = total
 
 
-def source_body(density, velocity, x_before, x_after, out, total, whole):
+def source_body(density, velocity, x_before, x_after, out, total, whole, staged, sems):
     th, width = velocity.shape[1], velocity.shape[3]
     radius = lax.broadcasted_iota(jnp.int32, (ROWS, width), 1).astype(jnp.float32)
     outward = (radius + 1.0) / (2.0 * radius + 1.0)
@@ -193,6 +193,7 @@
         total[span, :] = 0.5 * around + (outward * outer - inward * inner) + density[span, :]
     halves = whole.shape[0]
     blank = jnp.zeros((out.shape[1] - th - 2, LANES), jnp.float32)
+    copies = []
     first = velocity[1, 0]
     last = velocity[1, th - 1]
     for half in range(halves):
@@ -206,7 +207,14 @@
                 layer = layer + 0.5 * x_after[0, :, span].astype(jnp.float32)
             ends = [first[x : x + 1, span], last[x : x + 1, span], blank]
             column = jnp.concatenate([layer] + ends, axis=0)
-            out[x * halves + half] = column.astype(jnp.bfloat16)
+            staged[half * ROWS + x] = column.astype(jnp.bfloat16)
+            if x % 4 == 3:
+                four = pl.ds(half * ROWS + x - 3, 4)
+                sem = sems.at[len(copies)]
+                copies.append(pltpu.make_async_copy(staged.at[four], out.at[four], sem))
+                copies[-1].start()
+    for copy in copies:
+        copy.wait()
 
 
 def predictor_body(*refs):
@@ -283,7 +291,7 @@
     halves = whole.shape[0]
     for x in range(ROWS):
         for half in range(halves):
-            layer = spread[x * halves + half].astype(jnp.float32)
+            layer = spread[half * ROWS + x].astype(jnp.float32)
             whole[half, pl.ds(x, rows, stride=ROWS), :] = layer
     group = 2 * ROWS
 
@@ -393,7 +401,13 @@
         "source",
         struct((groups, th + extra, LANES), bf16),
         (density, velocity, x_before, x_after),
-        scratch=(pltpu.VMEM((cells, width), f32), pltpu.VMEM((halves, cells, LANES), f32)),
+        out_specs=ANY,
+        scratch=(
+            pltpu.VMEM((cells, width), f32),
+            pltpu.VMEM((halves, cells, LANES), f32),
+            pltpu.VMEM((groups, th + extra, LANES), bf16),
+            pltpu.SemaphoreType.DMA((groups // 4,)),
+        ),
         flops=30 * cells * width,
     )
     gathered = lax.all_to_all(source, "az", split_axis=0, concat_axis=0, tiled=True)

time: 61.6 us -> 61.6 us (level)
  no operation moved by 1% of the time
where the time goes in v5:
time: 61.6 us; the launch traced here: 61.2 us
  starting transfers between devices  36.7 us (60%)
  waiting for transfers between devices  13 us (21%)
  Pallas kernels  10.6 us (17%)
  between operations  0.79 us (1%)
    all_to_all x1, starting transfers between devices, on_device(): lax.all_to_all(packed, 'ax', split_axis=0, concat_axis=0, tiled=True)  13.9 us
    pallas_call x6, Pallas kernels, call(): pl.pallas_call(body, name=name, out_shape=out_shape, in_specs=[VMEM] * le...  10.6 us
    all_to_all x1, starting transfers between devices, on_device(): lax.all_to_all(source, 'az', split_axis=0, concat_axis=0, tiled=True)  9.21 us
    ppermute x1, starting transfers between devices, on_device(): x_after = lax.ppermute(first_x, 'ax', ring('ax', -1))  5.46 us
    all_to_all x1, waiting for transfers between devices, on_device(): lax.all_to_all(coefficients.reshape(groups, th, LANES), 'az', split_axis=...  3.98 us
    ppermute x1, waiting for transfers between devices, on_device(): theta_after = lax.ppermute(first_layer, 'az', ring('az', -1))  3.78 us
    all_to_all x1, waiting for transfers between devices, on_device(): lax.all_to_all(source, 'az', split_axis=0, concat_axis=0, tiled=True)  3.5 us
    all_to_all x1, starting transfers between devices, on_device(): lax.all_to_all(coefficients.reshape(groups, th, LANES), 'az', split_axis=...  3.42 us
  transfers between devices with their start and end apart: 7, of which 6 were waited for; matrix products, arithmetic and copies ran while one was open for 0% of the time, Pallas kernels for 8%

profile of v5, /device:TPU:1, one launch (start us, length us, event | category | flops | bytes accessed | tf_op | source)
XLA Modules:
  0.0 61.2 jit_solution(6965983908805520103)
XLA Ops:
  0.6 0.0 copy-start
  0.6 2.5 %pack_bubbles.1 = (bf16[32,8,128]{2,1,0:T(8,128)(2,1)}, bf16[3,32,256]{2,1,0:T(8,128)(2,1)}, bf16[3,32,256]{2,1,0:T(8,128)(2,1)}, bf16[3,8,256]{2,1,0:T(8,128)(2,1)}, bf16[3,8,256]{2,1,0:T(8,128)(2,1)}) custom-call(f32[3,2048]{1,0:T(4,128)} %refs_0_.1, f32[16,128]{1,0:T(8,128)} %bitcast.9, f32[16,128]{1,0:T(8,128)} %bitcast.10, s32[16,128]{1,0:T(8,128)} %bitcast.11, ...), custom_call_target="tpu_custom_call" | custom-call | bytes 852096 | tf_op jit(solution)/shard_map/pack_bubbles/pallas_call | solution.py:25
  3.1 0.0 copy-start.2
  3.1 13.9 %all-to-all-start = ((bf16[32,8,128]{2,1,0:T(8,128)(2,1)}), bf16[32,8,128]{2,1,0:T(8,128)(2,1)S(1)}, u32[]{:S(2)}, u32[]{:S(2)}) async-start(bf16[32,8,128]{2,1,0:T(8,128)(2,1)} %get-tuple-element.9), calls=%async_computation | async-start | bytes 131072 | tf_op jit(solution)/shard_map/all_to_all | solution.py:384
  17.0 3.1 %collective-permute-start = (bf16[3,32,256]{2,1,0:T(8,128)(2,1)}, bf16[3,32,256]{2,1,0:T(8,128)(2,1)S(1)}, u32[]{:S(2)}, u32[]{:S(2)}) collective-permute-start(bf16[3,32,256]{2,1,0:T(8,128)(2,1)} %get-tuple-element.12), channel_id=1, source_target_pairs={{0,1},{1,2},{2,3},{3,4},{4,5},{5,6},{6,7},{7,8},{8,9},{9,10},{10,1... | collective-permute-start | bytes 147464 | tf_op jit(solution)/shard_map/ppermute | solution.py:386
  20.1 5.5 %collective-permute-start.1 = (bf16[3,32,256]{2,1,0:T(8,128)(2,1)}, bf16[3,32,256]{2,1,0:T(8,128)(2,1)S(1)}, u32[]{:S(2)}, u32[]{:S(2)}) collective-permute-start(bf16[3,32,256]{2,1,0:T(8,128)(2,1)} %get-tuple-element.13), channel_id=1, source_target_pairs={{0,31},{1,0},{2,1},{3,2},{4,3},{5,4},{6,5},{7,6},{8,7},{9,8},{10,9... | collective-permute-start | bytes 147464 | tf_op jit(solution)/shard_map/ppermute | solution.py:387
  25.6 0.3 all-to-all-done.arrived.refs_0_
  26.0 0.7 %density.1 = f32[256,256]{1,0:T(8,128)S(1)} custom-call(bf16[32,8,128]{2,1,0:T(8,128)(2,1)S(1)} %all-to-all-done.arrived.refs_0_), custom_call_target="tpu_custom_call" | custom-call | flops 536870912 | bytes 65536 | tf_op jit(solution)/shard_map/density/pallas_call | solution.py:25
  26.7 0.0 collective-permute-done.x_before.refs_4_
  26.7 0.0 copy-start.4
  26.7 0.4 collective-permute-done.1.x_after.refs_5_
  27.1 0.9 %source.1.refs_2_ = bf16[16,40,128]{2,1,0:T(8,128)(2,1)} custom-call(f32[256,256]{1,0:T(8,128)S(1)} %density.1, f32[3,32,8,256]{3,2,1,0:T(8,128)S(1)} %copy-done, bf16[3,32,256]{2,1,0:T(8,128)(2,1)S(1)} %collective-permute-done.x_before.refs_4_, bf16[3,32,256]{2,1,0:T(8,128)(2,1)S(1)} %collective-permute-done.1.x_after.refs_5_), custom_call_target="tpu_custom_call" | custom-call | flops 1966080 | bytes 1146880 | tf_op jit(solution)/shard_map/source/pallas_call | solution.py:25
  28.0 9.2 %all-to-all-start.1 = ((bf16[16,40,128]{2,1,0:T(8,128)(2,1)}), bf16[16,40,128]{2,1,0:T(8,128)(2,1)S(1)}, u32[]{:S(2)}, u32[]{:S(2)}) async-start(bf16[16,40,128]{2,1,0:T(8,128)(2,1)} %source.1.refs_2_), calls=%async_computation.1 | async-start | bytes 327680 | tf_op jit(solution)/shard_map/all_to_all | solution.py:413
  37.3 1.6 %collective-permute-start.2 = (bf16[3,8,256]{2,1,0:T(8,128)(2,1)}, bf16[3,8,256]{2,1,0:T(8,128)(2,1)S(1)}, u32[]{:S(2)}, u32[]{:S(2)}) collective-permute-start(bf16[3,8,256]{2,1,0:T(8,128)(2,1)} %get-tuple-element.14), channel_id=1, source_target_pairs={{0,32},{32,64},{64,96},{96,128},{128,160},{160,192},{192,224},{224... | collective-permute-start | bytes 36872 | tf_op jit(solution)/shard_map/ppermute | solution.py:416
  38.9 0.0 collective-permute-start.3
  38.9 1.0 %collective-permute-done.2.refs_2_.before = bf16[3,8,256]{2,1,0:T(8,128)(2,1)S(1)} collective-permute-done((bf16[3,8,256]{2,1,0:T(8,128)(2,1)}, bf16[3,8,256]{2,1,0:T(8,128)(2,1)S(1)}, u32[]{:S(2)}, u32[]{:S(2)}) %collective-permute-start.2) | collective-permute-done | bytes 12320 | tf_op jit(solution)/shard_map/ppermute | solution.py:416
  40.0 3.8 %collective-permute-done.3.refs_3_.after = bf16[3,8,256]{2,1,0:T(8,128)(2,1)S(1)} collective-permute-done((bf16[3,8,256]{2,1,0:T(8,128)(2,1)}, bf16[3,8,256]{2,1,0:T(8,128)(2,1)S(1)}, u32[]{:S(2)}, u32[]{:S(2)}) %collective-permute-start.3) | collective-permute-done | bytes 12320 | tf_op jit(solution)/shard_map/ppermute | solution.py:417
  43.7 3.5 %all-to-all-done.1 = bf16[16,40,128]{2,1,0:T(8,128)(2,1)S(1)} async-done(((bf16[16,40,128]{2,1,0:T(8,128)(2,1)}), bf16[16,40,128]{2,1,0:T(8,128)(2,1)S(1)}, u32[]{:S(2)}, u32[]{:S(2)}) %all-to-all-start.1) | async-done | bytes 163872 | tf_op jit(solution)/shard_map/all_to_all | solution.py:413
  47.2 1.0 %transform.1 = bf16[512,128]{1,0:T(8,128)(2,1)} custom-call(bf16[512,640]{1,0:T(8,128)(2,1)S(1)} %copy-done.2, bf16[640,128]{1,0:T(8,128)(2,1)S(1)} %bitcast.7, bf16[3,8,256]{2,1,0:T(8,128)(2,1)S(1)} %collective-permute-done.2.refs_2_.before, bf16[3,8,256]{2,1,0:T(8,128)(2,1)S(1)} %collective-permute-done.3.refs_3_.after), custom_call_target="tpu_custom_call" | custom-call | flops 83886080 | bytes 843776 | tf_op jit(solution)/shard_map/transform/pallas_call | solution.py:25
  48.2 3.4 %all-to-all-start.2 = ((bf16[16,32,128]{2,1,0:T(8,128)(2,1)}), bf16[16,32,128]{2,1,0:T(8,128)(2,1)S(1)}, u32[]{:S(2)}, u32[]{:S(2)}) async-start(bf16[16,32,128]{2,1,0:T(8,128)(2,1)} %bitcast.5), calls=%async_computation.2 | async-start | bytes 262144 | tf_op jit(solution)/shard_map/all_to_all | solution.py:450
  51.7 0.0 copy-start.1
  51.7 4.2 %predictor.1 = f32[3,32,8,256]{3,2,1,0:T(8,128)} custom-call(bf16[32,8,128]{2,1,0:T(8,128)(2,1)} %copy-done.3, f32[3,32,8,256]{3,2,1,0:T(8,128)} %refs_1_.1, bf16[3,8,256]{2,1,0:T(8,128)(2,1)} %copy-done.6, bf16[3,8,256]{2,1,0:T(8,128)(2,1)} %copy-done.7, bf16[3,32,256]{2,1,0:T(8,128)(2,1)} %copy-done.4, bf16[3,32,256]{2,1,0:T(8,128)(2,1)} %copy-done.5), custom_call_target="tpu_custom_call" | custom-call | flops 1610612736 | bytes 974848 | tf_op jit(solution)/shard_map/predictor/pallas_call | solution.py:25
  55.9 4.0 %all-to-all-done.2.spread = bf16[16,32,128]{2,1,0:T(8,128)(2,1)S(1)} async-done(((bf16[16,32,128]{2,1,0:T(8,128)(2,1)}), bf16[16,32,128]{2,1,0:T(8,128)(2,1)S(1)}, u32[]{:S(2)}, u32[]{:S(2)}) %all-to-all-start.2) | async-done | bytes 131104 | tf_op jit(solution)/shard_map/all_to_all | solution.py:450
  59.9 1.3 %solve.1 = f32[256,256]{1,0:T(8,128)} custom-call(bf16[16,32,128]{2,1,0:T(8,128)(2,1)S(1)} %all-to-all-done.2.spread, bf16[16,256,256]{2,1,0:T(8,128)(2,1)S(1)} %copy-done.1), custom_call_target="tpu_custom_call" | custom-call | flops 33554432 | bytes 2228224 | tf_op jit(solution)/shard_map/solve/pallas_call | solution.py:25
  (13 shorter events, 0.0 us)
Async XLA Ops:
  0.6 26.5 %copy-start = (f32[3,32,8,256]{3,2,1,0:T(8,128)S(1)}, f32[3,32,8,256]{3,2,1,0:T(8,128)}, u32[]{:S(2)}) copy-start(f32[3,32,8,256]{3,2,1,0:T(8,128)} %refs_1_.1) | copy-start | bytes 2359300
  3.1 44.1 %copy-start.2 = (bf16[512,640]{1,0:T(8,128)(2,1)S(1)}, bf16[512,640]{1,0:T(8,128)(2,1)}, u32[]{:S(2)}) copy-start(bf16[512,640]{1,0:T(8,128)(2,1)} %constant.2.clone.table) | copy-start | bytes 1966084
  3.1 22.8 %all-to-all-start = ((bf16[32,8,128]{2,1,0:T(8,128)(2,1)}), bf16[32,8,128]{2,1,0:T(8,128)(2,1)S(1)}, u32[]{:S(2)}, u32[]{:S(2)}) async-start(bf16[32,8,128]{2,1,0:T(8,128)(2,1)} %get-tuple-element.9), calls=%async_computation | async-start | bytes 131072 | tf_op jit(solution)/shard_map/all_to_all | solution.py:384
  17.0 9.7 %collective-permute-start = (bf16[3,32,256]{2,1,0:T(8,128)(2,1)}, bf16[3,32,256]{2,1,0:T(8,128)(2,1)S(1)}, u32[]{:S(2)}, u32[]{:S(2)}) collective-permute-start(bf16[3,32,256]{2,1,0:T(8,128)(2,1)} %get-tuple-element.12), channel_id=1, source_target_pairs={{0,1},{1,2},{2,3},{3,4},{4,5},{5,6},{6,7},{7,8},{8,9},{9,10},{10,1... | collective-permute-start | bytes 147464 | tf_op jit(solution)/shard_map/ppermute | solution.py:386
  20.1 6.9 %collective-permute-start.1 = (bf16[3,32,256]{2,1,0:T(8,128)(2,1)}, bf16[3,32,256]{2,1,0:T(8,128)(2,1)S(1)}, u32[]{:S(2)}, u32[]{:S(2)}) collective-permute-start(bf16[3,32,256]{2,1,0:T(8,128)(2,1)} %get-tuple-element.13), channel_id=1, source_target_pairs={{0,31},{1,0},{2,1},{3,2},{4,3},{5,4},{6,5},{7,6},{8,7},{9,8},{10,9... | collective-permute-start | bytes 147464 | tf_op jit(solution)/shard_map/ppermute | solution.py:387
  26.0 22.3 %copy-start.3 = (bf16[32,8,128]{2,1,0:T(8,128)(2,1)}, bf16[32,8,128]{2,1,0:T(8,128)(2,1)S(1)}, u32[]{:S(2)}) copy-start(bf16[32,8,128]{2,1,0:T(8,128)(2,1)S(1)} %all-to-all-done.arrived.refs_0_) | copy-start | bytes 196612
  26.7 25.0 %copy-start.4 = (bf16[3,32,256]{2,1,0:T(8,128)(2,1)}, bf16[3,32,256]{2,1,0:T(8,128)(2,1)S(1)}, u32[]{:S(2)}) copy-start(bf16[3,32,256]{2,1,0:T(8,128)(2,1)S(1)} %collective-permute-done.x_before.refs_4_) | copy-start | bytes 147460
  27.1 24.6 %copy-start.5 = (bf16[3,32,256]{2,1,0:T(8,128)(2,1)}, bf16[3,32,256]{2,1,0:T(8,128)(2,1)S(1)}, u32[]{:S(2)}) copy-start(bf16[3,32,256]{2,1,0:T(8,128)(2,1)S(1)} %collective-permute-done.1.x_after.refs_5_) | copy-start | bytes 147460
  28.0 19.2 %all-to-all-start.1 = ((bf16[16,40,128]{2,1,0:T(8,128)(2,1)}), bf16[16,40,128]{2,1,0:T(8,128)(2,1)S(1)}, u32[]{:S(2)}, u32[]{:S(2)}) async-start(bf16[16,40,128]{2,1,0:T(8,128)(2,1)} %source.1.refs_2_), calls=%async_computation.1 | async-start | bytes 327680 | tf_op jit(solution)/shard_map/all_to_all | solution.py:413
  37.3 2.7 %collective-permute-start.2 = (bf16[3,8,256]{2,1,0:T(8,128)(2,1)}, bf16[3,8,256]{2,1,0:T(8,128)(2,1)S(1)}, u32[]{:S(2)}, u32[]{:S(2)}) collective-permute-start(bf16[3,8,256]{2,1,0:T(8,128)(2,1)} %get-tuple-element.14), channel_id=1, source_target_pairs={{0,32},{32,64},{64,96},{96,128},{128,160},{160,192},{192,224},{224... | collective-permute-start | bytes 36872 | tf_op jit(solution)/shard_map/ppermute | solution.py:416
  38.9 4.8 %collective-permute-start.3 = (bf16[3,8,256]{2,1,0:T(8,128)(2,1)}, bf16[3,8,256]{2,1,0:T(8,128)(2,1)S(1)}, u32[]{:S(2)}, u32[]{:S(2)}) collective-permute-start(bf16[3,8,256]{2,1,0:T(8,128)(2,1)} %get-tuple-element.15), channel_id=1, source_target_pairs={{0,480},{32,0},{64,32},{96,64},{128,96},{160,128},{192,160},{224,1... | collective-permute-start | bytes 36872 | tf_op jit(solution)/shard_map/ppermute | solution.py:417
  40.0 11.7 %copy-start.6 = (bf16[3,8,256]{2,1,0:T(8,128)(2,1)}, bf16[3,8,256]{2,1,0:T(8,128)(2,1)S(1)}, u32[]{:S(2)}) copy-start(bf16[3,8,256]{2,1,0:T(8,128)(2,1)S(1)} %collective-permute-done.2.refs_2_.before) | copy-start | bytes 36868
  43.7 8.0 %copy-start.7 = (bf16[3,8,256]{2,1,0:T(8,128)(2,1)}, bf16[3,8,256]{2,1,0:T(8,128)(2,1)S(1)}, u32[]{:S(2)}) copy-start(bf16[3,8,256]{2,1,0:T(8,128)(2,1)S(1)} %collective-permute-done.3.refs_3_.after) | copy-start | bytes 36868
  48.2 11.6 %all-to-all-start.2 = ((bf16[16,32,128]{2,1,0:T(8,128)(2,1)}), bf16[16,32,128]{2,1,0:T(8,128)(2,1)S(1)}, u32[]{:S(2)}, u32[]{:S(2)}) async-start(bf16[16,32,128]{2,1,0:T(8,128)(2,1)} %bitcast.5), calls=%async_computation.2 | async-start | bytes 262144 | tf_op jit(solution)/shard_map/all_to_all | solution.py:450
  51.7 8.2 %copy-start.1 = (bf16[16,256,256]{2,1,0:T(8,128)(2,1)S(1)}, bf16[16,256,256]{2,1,0:T(8,128)(2,1)}, u32[]{:S(2)}) copy-start(bf16[16,256,256]{2,1,0:T(8,128)(2,1)} %inverse.1) | copy-start | bytes 6291460

commit v6 on v5

--- a/solution.py
+++ b/solution.py
@@ -50,8 +50,10 @@
 
 def pack_body(*refs):
     hbm, held = refs[:8], refs[13:21]
-    out, first_x, last_x, first_theta, last_theta = refs[8:13]
-    listed, slips, payload, staged, sems = refs[21:]
+    results = refs[8:13]
+    listed, slips, payload, staged, sems = refs[21:26]
+    packed, *layers = made = refs[26:31]
+    sent = refs[31]
     copies = [
         pltpu.make_async_copy(source, target, sems.at[i])
         for i, (source, target) in enumerate(zip(hbm, held))
@@ -89,22 +91,38 @@
     used = slot < count
     place = jnp.minimum(start + slot, lines * LANES - 1)
     bubble = take_rows(listed, place >> 7, place & 127)
-    row, column = bubble >> 7, bubble & 127
-    for k in range(4):
-        value = take_rows(payload.at[k], row, column)
-        staged[:, k, :] = jnp.where(used, value, 0.0)
-    cell = take_rows(payload.at[4], row, column).astype(jnp.int32)
-    cell = jnp.where(used, cell, 0)
-    staged[:, 4, :] = (cell >> 8).astype(jnp.float32)
-    staged[:, 5, :] = (cell & 255).astype(jnp.float32)
-    staged[:, 6, :] = jnp.zeros(shape, jnp.float32)
-    staged[:, 7, :] = jnp.zeros(shape, jnp.float32)
-    out[...] = staged[...].astype(jnp.bfloat16)
     copies[7].wait()
-    first_x[...] = block[:, :, 0, :].astype(jnp.bfloat16)
-    last_x[...] = block[:, :, ROWS - 1, :].astype(jnp.bfloat16)
-    first_theta[...] = block[:, 0].astype(jnp.bfloat16)
-    last_theta[...] = block[:, block.shape[1] - 1].astype(jnp.bfloat16)
+    layers[0][...] = block[:, :, 0, :].astype(jnp.bfloat16)
+    layers[1][...] = block[:, :, ROWS - 1, :].astype(jnp.bfloat16)
+    layers[2][...] = block[:, 0].astype(jnp.bfloat16)
+    layers[3][...] = block[:, block.shape[1] - 1].astype(jnp.bfloat16)
+    leaving = [
+        pltpu.make_async_copy(made[i], results[i], sent.at[i - 1]) for i in range(1, len(made))
+    ]
+    for copy in leaving:
+        copy.start()
+    blank = jnp.zeros((ROWS, LANES), jnp.float32)
+    for first in range(0, peers, ROWS):
+        span = slice(first, first + ROWS)
+        row, column = bubble[span] >> 7, bubble[span] & 127
+        for k in range(4):
+            value = take_rows(payload.at[k], row, column)
+            staged[span, k, :] = jnp.where(used[span], value, 0.0)
+        cell = take_rows(payload.at[4], row, column).astype(jnp.int32)
+        cell = jnp.where(used[span], cell, 0)
+        staged[span, 4, :] = (cell >> 8).astype(jnp.float32)
+        staged[span, 5, :] = (cell & 255).astype(jnp.float32)
+        staged[span, 6, :] = blank
+        staged[span, 7, :] = blank
+        packed[span] = staged[span].astype(jnp.bfloat16)
+        eight = pl.ds(first, ROWS)
+        copy = pltpu.make_async_copy(
+            packed.at[eight], results[0].at[eight], sent.at[len(leaving)]
+        )
+        copy.start()
+        leaving.append(copy)
+    for copy in leaving:
+        copy.wait()
 
 
 def radial_neighbours(v):
@@ -371,6 +389,7 @@
         ),
         bubbles_in,
         specs=[ANY] * 8,
+        out_specs=(ANY,) * 5,
         limit=60,
         scratch=tuple(pltpu.VMEM(x.shape, x.dtype) for x in bubbles_in)
         + (
@@ -379,6 +398,12 @@
             pltpu.VMEM((5,) + square, f32),
             pltpu.VMEM((peers, ROWS, LANES), f32),
             pltpu.SemaphoreType.DMA((8,)),
+            pltpu.VMEM((peers, ROWS, LANES), bf16),
+            pltpu.VMEM((3, th, width), bf16),
+            pltpu.VMEM((3, th, width), bf16),
+            pltpu.VMEM((3, ax, width), bf16),
+            pltpu.VMEM((3, ax, width), bf16),
+            pltpu.SemaphoreType.DMA((4 + peers // ROWS,)),
         ),
     )
     arrived = lax.all_to_all(packed, "ax", split_axis=0, concat_axis=0, tiled=True)

time: 61.6 us -> 61.9 us (level)
  no operation moved by 1% of the time
where the time goes in v6:
time: 61.9 us; the launch traced here: 61.5 us
  starting transfers between devices  36.7 us (59%)
  waiting for transfers between devices  13 us (21%)
  Pallas kernels  10.9 us (18%)
  between operations  0.79 us (1%)
    all_to_all x1, starting transfers between devices, on_device(): lax.all_to_all(packed, 'ax', split_axis=0, concat_axis=0, tiled=True)  13.9 us
    pallas_call x6, Pallas kernels, call(): pl.pallas_call(body, name=name, out_shape=out_shape, in_specs=[VMEM] * le...  10.9 us
    all_to_all x1, starting transfers between devices, on_device(): lax.all_to_all(source, 'az', split_axis=0, concat_axis=0, tiled=True)  9.21 us
    ppermute x1, starting transfers between devices, on_device(): x_after = lax.ppermute(first_x, 'ax', ring('ax', -1))  5.46 us
    all_to_all x1, waiting for transfers between devices, on_device(): lax.all_to_all(coefficients.reshape(groups, th, LANES), 'az', split_axis=...  3.97 us
    ppermute x1, waiting for transfers between devices, on_device(): theta_after = lax.ppermute(first_layer, 'az', ring('az', -1))  3.78 us
    all_to_all x1, waiting for transfers between devices, on_device(): lax.all_to_all(source, 'az', split_axis=0, concat_axis=0, tiled=True)  3.5 us
    all_to_all x1, starting transfers between devices, on_device(): lax.all_to_all(coefficients.reshape(groups, th, LANES), 'az', split_axis=...  3.42 us
  transfers between devices with their start and end apart: 7, of which 6 were waited for; matrix products, arithmetic and copies ran while one was open for 0% of the time, Pallas kernels for 8%

profile of v6, /device:TPU:1, one launch (start us, length us, event | category | flops | bytes accessed | tf_op | source)
XLA Modules:
  0.0 61.5 jit_solution(12653783203157910669)
XLA Ops:
  0.6 0.0 copy-start
  0.6 2.7 %pack_bubbles.1 = (bf16[32,8,128]{2,1,0:T(8,128)(2,1)}, bf16[3,32,256]{2,1,0:T(8,128)(2,1)}, bf16[3,32,256]{2,1,0:T(8,128)(2,1)}, bf16[3,8,256]{2,1,0:T(8,128)(2,1)}, bf16[3,8,256]{2,1,0:T(8,128)(2,1)}) custom-call(f32[3,2048]{1,0:T(4,128)} %refs_0_.1, f32[16,128]{1,0:T(8,128)} %bitcast.9, f32[16,128]{1,0:T(8,128)} %bitcast.10, s32[16,128]{1,0:T(8,128)} %bitcast.11, ...), custom_call_target="tpu_custom_call" | custom-call | bytes 852096 | tf_op jit(solution)/shard_map/pack_bubbles/pallas_call | solution.py:25
  3.4 0.0 copy-start.2
  3.4 13.9 %all-to-all-start = ((bf16[32,8,128]{2,1,0:T(8,128)(2,1)}), bf16[32,8,128]{2,1,0:T(8,128)(2,1)S(1)}, u32[]{:S(2)}, u32[]{:S(2)}) async-start(bf16[32,8,128]{2,1,0:T(8,128)(2,1)} %get-tuple-element.9), calls=%async_computation | async-start | bytes 131072 | tf_op jit(solution)/shard_map/all_to_all | solution.py:409
  17.3 3.1 %collective-permute-start = (bf16[3,32,256]{2,1,0:T(8,128)(2,1)}, bf16[3,32,256]{2,1,0:T(8,128)(2,1)S(1)}, u32[]{:S(2)}, u32[]{:S(2)}) collective-permute-start(bf16[3,32,256]{2,1,0:T(8,128)(2,1)} %get-tuple-element.12), channel_id=1, source_target_pairs={{0,1},{1,2},{2,3},{3,4},{4,5},{5,6},{6,7},{7,8},{8,9},{9,10},{10,1... | collective-permute-start | bytes 147464 | tf_op jit(solution)/shard_map/ppermute | solution.py:411
  20.4 5.5 %collective-permute-start.1 = (bf16[3,32,256]{2,1,0:T(8,128)(2,1)}, bf16[3,32,256]{2,1,0:T(8,128)(2,1)S(1)}, u32[]{:S(2)}, u32[]{:S(2)}) collective-permute-start(bf16[3,32,256]{2,1,0:T(8,128)(2,1)} %get-tuple-element.13), channel_id=1, source_target_pairs={{0,31},{1,0},{2,1},{3,2},{4,3},{5,4},{6,5},{7,6},{8,7},{9,8},{10,9... | collective-permute-start | bytes 147464 | tf_op jit(solution)/shard_map/ppermute | solution.py:412
  25.9 0.3 all-to-all-done.arrived.refs_0_
  26.2 0.7 %density.1 = f32[256,256]{1,0:T(8,128)S(1)} custom-call(bf16[32,8,128]{2,1,0:T(8,128)(2,1)S(1)} %all-to-all-done.arrived.refs_0_), custom_call_target="tpu_custom_call" | custom-call | flops 536870912 | bytes 65536 | tf_op jit(solution)/shard_map/density/pallas_call | solution.py:25
  27.0 0.0 collective-permute-done.x_before.refs_4_
  27.0 0.0 copy-start.4
  27.0 0.4 collective-permute-done.1.x_after.refs_5_
  27.3 0.9 %source.1.refs_2_ = bf16[16,40,128]{2,1,0:T(8,128)(2,1)} custom-call(f32[256,256]{1,0:T(8,128)S(1)} %density.1, f32[3,32,8,256]{3,2,1,0:T(8,128)S(1)} %copy-done, bf16[3,32,256]{2,1,0:T(8,128)(2,1)S(1)} %collective-permute-done.x_before.refs_4_, bf16[3,32,256]{2,1,0:T(8,128)(2,1)S(1)} %collective-permute-done.1.x_after.refs_5_), custom_call_target="tpu_custom_call" | custom-call | flops 1966080 | bytes 1146880 | tf_op jit(solution)/shard_map/source/pallas_call | solution.py:25
  28.3 9.2 %all-to-all-start.1 = ((bf16[16,40,128]{2,1,0:T(8,128)(2,1)}), bf16[16,40,128]{2,1,0:T(8,128)(2,1)S(1)}, u32[]{:S(2)}, u32[]{:S(2)}) async-start(bf16[16,40,128]{2,1,0:T(8,128)(2,1)} %source.1.refs_2_), calls=%async_computation.1 | async-start | bytes 327680 | tf_op jit(solution)/shard_map/all_to_all | solution.py:438
  37.5 1.6 %collective-permute-start.2 = (bf16[3,8,256]{2,1,0:T(8,128)(2,1)}, bf16[3,8,256]{2,1,0:T(8,128)(2,1)S(1)}, u32[]{:S(2)}, u32[]{:S(2)}) collective-permute-start(bf16[3,8,256]{2,1,0:T(8,128)(2,1)} %get-tuple-element.14), channel_id=1, source_target_pairs={{0,32},{32,64},{64,96},{96,128},{128,160},{160,192},{192,224},{224... | collective-permute-start | bytes 36872 | tf_op jit(solution)/shard_map/ppermute | solution.py:441
  39.2 0.0 collective-permute-start.3
  39.2 1.0 %collective-permute-done.2.refs_2_.before = bf16[3,8,256]{2,1,0:T(8,128)(2,1)S(1)} collective-permute-done((bf16[3,8,256]{2,1,0:T(8,128)(2,1)}, bf16[3,8,256]{2,1,0:T(8,128)(2,1)S(1)}, u32[]{:S(2)}, u32[]{:S(2)}) %collective-permute-start.2) | collective-permute-done | bytes 12320 | tf_op jit(solution)/shard_map/ppermute | solution.py:441
  40.2 3.8 %collective-permute-done.3.refs_3_.after = bf16[3,8,256]{2,1,0:T(8,128)(2,1)S(1)} collective-permute-done((bf16[3,8,256]{2,1,0:T(8,128)(2,1)}, bf16[3,8,256]{2,1,0:T(8,128)(2,1)S(1)}, u32[]{:S(2)}, u32[]{:S(2)}) %collective-permute-start.3) | collective-permute-done | bytes 12320 | tf_op jit(solution)/shard_map/ppermute | solution.py:442
  44.0 3.5 %all-to-all-done.1 = bf16[16,40,128]{2,1,0:T(8,128)(2,1)S(1)} async-done(((bf16[16,40,128]{2,1,0:T(8,128)(2,1)}), bf16[16,40,128]{2,1,0:T(8,128)(2,1)S(1)}, u32[]{:S(2)}, u32[]{:S(2)}) %all-to-all-start.1) | async-done | bytes 163872 | tf_op jit(solution)/shard_map/all_to_all | solution.py:438
  47.5 1.0 %transform.1 = bf16[512,128]{1,0:T(8,128)(2,1)} custom-call(bf16[512,640]{1,0:T(8,128)(2,1)S(1)} %copy-done.2, bf16[640,128]{1,0:T(8,128)(2,1)S(1)} %bitcast.7, bf16[3,8,256]{2,1,0:T(8,128)(2,1)S(1)} %collective-permute-done.2.refs_2_.before, bf16[3,8,256]{2,1,0:T(8,128)(2,1)S(1)} %collective-permute-done.3.refs_3_.after), custom_call_target="tpu_custom_call" | custom-call | flops 83886080 | bytes 843776 | tf_op jit(solution)/shard_map/transform/pallas_call | solution.py:25
  48.5 3.4 %all-to-all-start.2 = ((bf16[16,32,128]{2,1,0:T(8,128)(2,1)}), bf16[16,32,128]{2,1,0:T(8,128)(2,1)S(1)}, u32[]{:S(2)}, u32[]{:S(2)}) async-start(bf16[16,32,128]{2,1,0:T(8,128)(2,1)} %bitcast.5), calls=%async_computation.2 | async-start | bytes 262144 | tf_op jit(solution)/shard_map/all_to_all | solution.py:475
  52.0 0.0 copy-start.1
  52.0 4.2 %predictor.1 = f32[3,32,8,256]{3,2,1,0:T(8,128)} custom-call(bf16[32,8,128]{2,1,0:T(8,128)(2,1)} %copy-done.3, f32[3,32,8,256]{3,2,1,0:T(8,128)} %refs_1_.1, bf16[3,8,256]{2,1,0:T(8,128)(2,1)} %copy-done.6, bf16[3,8,256]{2,1,0:T(8,128)(2,1)} %copy-done.7, bf16[3,32,256]{2,1,0:T(8,128)(2,1)} %copy-done.4, bf16[3,32,256]{2,1,0:T(8,128)(2,1)} %copy-done.5), custom_call_target="tpu_custom_call" | custom-call | flops 1610612736 | bytes 974848 | tf_op jit(solution)/shard_map/predictor/pallas_call | solution.py:25
  56.2 4.0 %all-to-all-done.2.spread = bf16[16,32,128]{2,1,0:T(8,128)(2,1)S(1)} async-done(((bf16[16,32,128]{2,1,0:T(8,128)(2,1)}), bf16[16,32,128]{2,1,0:T(8,128)(2,1)S(1)}, u32[]{:S(2)}, u32[]{:S(2)}) %all-to-all-start.2) | async-done | bytes 131104 | tf_op jit(solution)/shard_map/all_to_all | solution.py:475
  60.1 1.3 %solve.1 = f32[256,256]{1,0:T(8,128)} custom-call(bf16[16,32,128]{2,1,0:T(8,128)(2,1)S(1)} %all-to-all-done.2.spread, bf16[16,256,256]{2,1,0:T(8,128)(2,1)S(1)} %copy-done.1), custom_call_target="tpu_custom_call" | custom-call | flops 33554432 | bytes 2228224 | tf_op jit(solution)/shard_map/solve/pallas_call | solution.py:25
  (13 shorter events, 0.0 us)
Async XLA Ops:
  0.6 26.7 %copy-start = (f32[3,32,8,256]{3,2,1,0:T(8,128)S(1)}, f32[3,32,8,256]{3,2,1,0:T(8,128)}, u32[]{:S(2)}) copy-start(f32[3,32,8,256]{3,2,1,0:T(8,128)} %refs_1_.1) | copy-start | bytes 2359300
  3.4 44.1 %copy-start.2 = (bf16[512,640]{1,0:T(8,128)(2,1)S(1)}, bf16[512,640]{1,0:T(8,128)(2,1)}, u32[]{:S(2)}) copy-start(bf16[512,640]{1,0:T(8,128)(2,1)} %constant.2.clone.table) | copy-start | bytes 1966084
  3.4 22.8 %all-to-all-start = ((bf16[32,8,128]{2,1,0:T(8,128)(2,1)}), bf16[32,8,128]{2,1,0:T(8,128)(2,1)S(1)}, u32[]{:S(2)}, u32[]{:S(2)}) async-start(bf16[32,8,128]{2,1,0:T(8,128)(2,1)} %get-tuple-element.9), calls=%async_computation | async-start | bytes 131072 | tf_op jit(solution)/shard_map/all_to_all | solution.py:409
  17.3 9.7 %collective-permute-start = (bf16[3,32,256]{2,1,0:T(8,128)(2,1)}, bf16[3,32,256]{2,1,0:T(8,128)(2,1)S(1)}, u32[]{:S(2)}, u32[]{:S(2)}) collective-permute-start(bf16[3,32,256]{2,1,0:T(8,128)(2,1)} %get-tuple-element.12), channel_id=1, source_target_pairs={{0,1},{1,2},{2,3},{3,4},{4,5},{5,6},{6,7},{7,8},{8,9},{9,10},{10,1... | collective-permute-start | bytes 147464 | tf_op jit(solution)/shard_map/ppermute | solution.py:411
  20.4 6.9 %collective-permute-start.1 = (bf16[3,32,256]{2,1,0:T(8,128)(2,1)}, bf16[3,32,256]{2,1,0:T(8,128)(2,1)S(1)}, u32[]{:S(2)}, u32[]{:S(2)}) collective-permute-start(bf16[3,32,256]{2,1,0:T(8,128)(2,1)} %get-tuple-element.13), channel_id=1, source_target_pairs={{0,31},{1,0},{2,1},{3,2},{4,3},{5,4},{6,5},{7,6},{8,7},{9,8},{10,9... | collective-permute-start | bytes 147464 | tf_op jit(solution)/shard_map/ppermute | solution.py:412
  26.2 22.3 %copy-start.3 = (bf16[32,8,128]{2,1,0:T(8,128)(2,1)}, bf16[32,8,128]{2,1,0:T(8,128)(2,1)S(1)}, u32[]{:S(2)}) copy-start(bf16[32,8,128]{2,1,0:T(8,128)(2,1)S(1)} %all-to-all-done.arrived.refs_0_) | copy-start | bytes 196612
  27.0 24.9 %copy-start.4 = (bf16[3,32,256]{2,1,0:T(8,128)(2,1)}, bf16[3,32,256]{2,1,0:T(8,128)(2,1)S(1)}, u32[]{:S(2)}) copy-start(bf16[3,32,256]{2,1,0:T(8,128)(2,1)S(1)} %collective-permute-done.x_before.refs_4_) | copy-start | bytes 147460
  27.3 24.6 %copy-start.5 = (bf16[3,32,256]{2,1,0:T(8,128)(2,1)}, bf16[3,32,256]{2,1,0:T(8,128)(2,1)S(1)}, u32[]{:S(2)}) copy-start(bf16[3,32,256]{2,1,0:T(8,128)(2,1)S(1)} %collective-permute-done.1.x_after.refs_5_) | copy-start | bytes 147460
  28.3 19.2 %all-to-all-start.1 = ((bf16[16,40,128]{2,1,0:T(8,128)(2,1)}), bf16[16,40,128]{2,1,0:T(8,128)(2,1)S(1)}, u32[]{:S(2)}, u32[]{:S(2)}) async-start(bf16[16,40,128]{2,1,0:T(8,128)(2,1)} %source.1.refs_2_), calls=%async_computation.1 | async-start | bytes 327680 | tf_op jit(solution)/shard_map/all_to_all | solution.py:438
  37.5 2.7 %collective-permute-start.2 = (bf16[3,8,256]{2,1,0:T(8,128)(2,1)}, bf16[3,8,256]{2,1,0:T(8,128)(2,1)S(1)}, u32[]{:S(2)}, u32[]{:S(2)}) collective-permute-start(bf16[3,8,256]{2,1,0:T(8,128)(2,1)} %get-tuple-element.14), channel_id=1, source_target_pairs={{0,32},{32,64},{64,96},{96,128},{128,160},{160,192},{192,224},{224... | collective-permute-start | bytes 36872 | tf_op jit(solution)/shard_map/ppermute | solution.py:441
  39.2 4.8 %collective-permute-start.3 = (bf16[3,8,256]{2,1,0:T(8,128)(2,1)}, bf16[3,8,256]{2,1,0:T(8,128)(2,1)S(1)}, u32[]{:S(2)}, u32[]{:S(2)}) collective-permute-start(bf16[3,8,256]{2,1,0:T(8,128)(2,1)} %get-tuple-element.15), channel_id=1, source_target_pairs={{0,480},{32,0},{64,32},{96,64},{128,96},{160,128},{192,160},{224,1... | collective-permute-start | bytes 36872 | tf_op jit(solution)/shard_map/ppermute | solution.py:442
  40.2 11.7 %copy-start.6 = (bf16[3,8,256]{2,1,0:T(8,128)(2,1)}, bf16[3,8,256]{2,1,0:T(8,128)(2,1)S(1)}, u32[]{:S(2)}) copy-start(bf16[3,8,256]{2,1,0:T(8,128)(2,1)S(1)} %collective-permute-done.2.refs_2_.before) | copy-start | bytes 36868
  44.0 8.0 %copy-start.7 = (bf16[3,8,256]{2,1,0:T(8,128)(2,1)}, bf16[3,8,256]{2,1,0:T(8,128)(2,1)S(1)}, u32[]{:S(2)}) copy-start(bf16[3,8,256]{2,1,0:T(8,128)(2,1)S(1)} %collective-permute-done.3.refs_3_.after) | copy-start | bytes 36868
  48.5 11.6 %all-to-all-start.2 = ((bf16[16,32,128]{2,1,0:T(8,128)(2,1)}), bf16[16,32,128]{2,1,0:T(8,128)(2,1)S(1)}, u32[]{:S(2)}, u32[]{:S(2)}) async-start(bf16[16,32,128]{2,1,0:T(8,128)(2,1)} %bitcast.5), calls=%async_computation.2 | async-start | bytes 262144 | tf_op jit(solution)/shard_map/all_to_all | solution.py:475
  52.0 8.2 %copy-start.1 = (bf16[16,256,256]{2,1,0:T(8,128)(2,1)S(1)}, bf16[16,256,256]{2,1,0:T(8,128)(2,1)}, u32[]{:S(2)}) copy-start(bf16[16,256,256]{2,1,0:T(8,128)(2,1)} %inverse.1) | copy-start | bytes 6291460
